TPU v7x, 128 devices: a whole 4x4x4 slice. The times are simulated.
128 devices in a mesh: dp: 8 (over x, core), depth: 2 (over y_lo), height: 8 (over z, y_hi).
Axes of the slice: x: 4, y: 4 (y_hi: 2, y_lo: 2; y = y_hi * 2 + y_lo), z: 4, core: 2. Of those that a mesh axis runs over, the one named last changes fastest.
Arguments:
- act_one: bfloat16 [8, 32, 8, 128, 128], P('dp', None, 'depth', 'height'), may hold values from -6 to 6
- pre_two: bfloat16 [8, 64, 8, 128, 128], P('dp', None, 'depth', 'height'), may hold values from -6 to 6
- cot_three: bfloat16 [8, 128, 4, 4096], P('dp', None, 'depth', 'height'), may hold values from -24 to 24
- weight_two: float32 [64, 864], replicated, may hold values from -6 to 6
- weight_three: float32 [128, 1728], replicated, may hold values from -6 to 6
- moment_two: float32 [55296], P(('dp', 'depth', 'height')), may hold values from -1.2 to 1.2
- moment_three: float32 [221184], P(('dp', 'depth', 'height')), may hold values from -1.2 to 1.2
Outputs:
- grad_input: bfloat16 [8, 32, 8, 128, 128], P('dp', None, 'depth', 'height')
- new_weight_two: float32 [64, 864], replicated
- new_weight_three: float32 [128, 1728], replicated
- new_moment_two: float32 [55296], P(('dp', 'depth', 'height'))
- new_moment_three: float32 [221184], P(('dp', 'depth', 'height'))
All inputs are finite; a program needn't handle non-finite values.
Results may differ from a plain program's by a relative error of at most 0.007.
Values may be sent and summed in bfloat16 or wider, within the bound.
No kernel may reach another device: no remote copies, remote signals or barrier semaphores. Data moves between devices by JAX's collectives and lax.ppermute only.
A program may use at most 128 MiB of HBM per device.

v0:
```python
import jax
import jax.numpy as jnp
from jax import lax
from jax.experimental import pallas as pl
from jax.experimental.pallas import tpu as pltpu
from jax.sharding import PartitionSpec as P

SLOPE = 0.3
LEARN = 4.0
TRUST = 0.05
MOMENTUM = 0.9
EPSILON = 1e-06
AXES = ("dp", "depth", "height")
F32 = jnp.float32
BF16 = jnp.bfloat16


def call(body, outs, scratch=(), flops=0, moved=0):
    return pl.pallas_call(
        body,
        out_shape=[jax.ShapeDtypeStruct(shape, dtype) for shape, dtype in outs],
        scratch_shapes=list(scratch),
        compiler_params=pltpu.CompilerParams(vmem_limit_bytes=48 * 1024 * 1024),
        cost_estimate=pl.CostEstimate(flops=flops, bytes_accessed=moved, transcendentals=0),
    )


def dot_nt(a, b):
    return lax.dot_general(a, b, (((1,), (1,)), ((), ())), preferred_element_type=F32)


def dot_nn(a, b):
    return lax.dot_general(a, b, (((1,), (0,)), ((), ())), preferred_element_type=F32)


def shifted(x, amount):
    size = x.shape[-1]
    amount = amount % size
    if amount == 0:
        return x
    return jnp.concatenate([x[..., amount:], x[..., :amount]], axis=-1)


def arrange(cot_ref, pre_ref, cot_out, pre_out, up_out, down_out, side_out, diag_up_out, diag_down_out):
    last = lax.axis_index("depth") == 0
    for d in range(2):
        cot = cot_ref[:, d, :]
        cot_out[d] = cot
        for out in (up_out, diag_up_out):
            out[128 * d : 128 * d + 128] = cot[:, :128]
        for out in (down_out, diag_down_out):
            out[128 * d : 128 * d + 128] = cot[:, 384:]
    for d in range(4):
        rows = jnp.swapaxes(pre_ref[:, d].astype(F32), 0, 1).astype(BF16)
        pre_out[d] = rows
        up_out[256 + 64 * d : 320 + 64 * d] = rows[0]
        down_out[256 + 64 * d : 320 + 64 * d] = rows[15]
        if d in (0, 3):
            @pl.when(last == (d == 3))
            def _():
                side_out[...] = rows
                diag_up_out[256:] = rows[0]
                diag_down_out[256:] = rows[15]


def prepare(pre_ref, act_ref, w2_ref, w3_ref, pooled_out, act_out, w2_out, w3_out, norm_out, t2, t3):
    row = lax.broadcasted_iota(jnp.int32, (256, 128), 0)
    col = lax.broadcasted_iota(jnp.int32, (256, 128), 1)
    pool = jnp.where(row // 2 == col, 0.125, 0.0).astype(BF16)
    for d in range(2):
        for t in range(4):
            halves = []
            for half in range(2):
                total = None
                for i in range(2):
                    for j in range(2):
                        x = pre_ref[2 * d + i, 4 * t + 2 * half + j].astype(F32)
                        x = jnp.where(x > 0, x, SLOPE * x)
                        total = x if total is None else total + x
                halves.append(total)
            total = jnp.concatenate(halves, axis=1)
            high = total.astype(BF16)
            low = (total - high.astype(F32)).astype(BF16)
            mean = dot_nn(high, pool) + dot_nn(low, pool)
            pooled_out[64 * d : 64 * d + 64, 128 * t : 128 * t + 128] = mean.astype(BF16)
    lane = lax.broadcasted_iota(jnp.int32, (16, 32, 128), 2)
    for d in range(4):
        rows = jnp.swapaxes(act_ref[:, d].astype(F32), 0, 1)
        before = jnp.where(lane < 127, shifted(rows, 1), 0.0)
        after = jnp.where(lane > 0, shifted(rows, -1), 0.0)
        for ow, value in enumerate((before, rows, after)):
            start = 96 * d + 32 * ow
            act_out[:, start : start + 32, :] = value.astype(BF16)
    w2 = w2_ref[...]
    w3 = w3_ref[...]
    norm_out[0] = jnp.sqrt(jnp.sum(w2 * w2))
    norm_out[1] = jnp.sqrt(jnp.sum(w3 * w3))
    t2[...] = jnp.transpose(w2)
    t3[...] = jnp.transpose(w3)
    for kd in range(3):
        for oh in range(3):
            for ow in range(3):
                k = kd * 9 + (2 - oh) * 3 + (2 - ow)
                block = t3[pl.ds(k, 64, stride=27), :].astype(BF16)
                tap = oh * 3 + ow
                w3_out[64 * kd : 64 * kd + 64, 128 * tap : 128 * tap + 128] = block
    zero = jnp.zeros((32, 64), F32)
    for kd in range(3):
        for ow in range(3):
            taps = []
            for oh in range(3):
                k = kd * 9 + (2 - oh) * 3 + (2 - ow)
                taps.append(t2[pl.ds(k, 32, stride=27), :])
            for r in range(2):
                blocks = taps + [zero] if r == 0 else [zero] + taps
                start = 64 * kd + 32 * r
                w2_out[start : start + 32, 256 * ow : 256 * ow + 256] = jnp.concatenate(blocks, axis=1).astype(BF16)


def coarse(scale, own_ref, side_ref, up_ref, down_ref, dup_ref, ddown_ref, w3_ref, pooled_ref,
           back_out, grad_out, x_buf, s_buf, t3):
    dep = lax.axis_index("depth")
    hgt = lax.axis_index("height")
    x_buf[0] = jnp.zeros((128, 768), BF16)
    x_buf[5] = jnp.zeros((128, 768), BF16)
    own = 1 + 2 * dep
    other = 3 - 2 * dep
    for d in range(2):
        x_buf[own + d, :, 128:640] = own_ref[d]
        x_buf[own + d, :, :128] = up_ref[128 * d : 128 * d + 128]
        x_buf[own + d, :, 640:] = down_ref[128 * d : 128 * d + 128]
        x_buf[other + d, :, 128:640] = side_ref[d]
        x_buf[other + d, :, :128] = dup_ref[128 * d : 128 * d + 128]
        x_buf[other + d, :, 640:] = ddown_ref[128 * d : 128 * d + 128]
    column = lax.broadcasted_iota(jnp.int32, (128, 768), 1) % 64
    back = [None, None, None]
    for z in range(5):
        x = x_buf[dep + z]
        for ow in range(3):
            if ow == 0:
                moved = jnp.where(column > 0, shifted(x, -1), jnp.zeros_like(x))
            elif ow == 1:
                moved = x
            else:
                moved = jnp.where(column < 63, shifted(x, 1), jnp.zeros_like(x))
            for oh in range(3):
                tap = oh * 3 + ow
                s_buf[z, 128 * tap : 128 * tap + 128, :] = shifted(moved, (oh - 1) * 64)
        outs = [i for i in range(3) if 0 <= z - i <= 2]
        low = 2 - z + outs[0]
        y = dot_nn(w3_ref[64 * low : 64 * (low + len(outs)), :], s_buf[z])
        for n, i in enumerate(outs):
            part = y[64 * n : 64 * n + 64]
            back[i] = part if back[i] is None else back[i] + part
    lane = lax.broadcasted_iota(jnp.int32, (64, 768), 1)
    keep = ((lane >= 128) | (hgt > 0)) & ((lane < 640) | (hgt < 7))
    for i in range(3):
        back_out[i + 1 - dep] = jnp.where(keep, scale * back[i], 0.0).astype(BF16)
    back_out[3 * dep] = jnp.zeros((64, 768), BF16)
    parts = [None, None, None]
    for z in range(4):
        s = s_buf[dep + z, :, 128:640]
        ds = [d for d in range(2) if 0 <= z - d <= 2]
        r = dot_nt(pooled_ref[64 * ds[0] : 64 * (ds[-1] + 1), :], s)
        for n, d in enumerate(ds):
            part = r[64 * n : 64 * n + 64]
            od = z - d
            parts[od] = part if parts[od] is None else parts[od] + part
    for od in range(3):
        for oh in range(3):
            for ow in range(3):
                k = (2 - od) * 9 + (2 - oh) * 3 + (2 - ow)
                tap = oh * 3 + ow
                t3[pl.ds(k, 64, stride=27), :] = parts[od][:, 128 * tap : 128 * tap + 128]
    grad_out[...] = jnp.transpose(t3[...]).astype(BF16)


def fine(back_ref, pre_ref, side_ref, up_ref, down_ref, dup_ref, ddown_ref, act_ref,
         z_out, grad_out, upper, t2):
    dep = lax.axis_index("depth")
    row = lax.broadcasted_iota(jnp.int32, (128, 256), 0)
    col = lax.broadcasted_iota(jnp.int32, (128, 256), 1)
    spread = jnp.where(row == col // 2, 0.125, 0.0).astype(BF16)
    for t in range(6):
        x = back_ref[:, :, 128 * t : 128 * t + 128].reshape(256, 128)
        y = dot_nn(x, spread).reshape(4, 64, 256)
        if t > 0:
            upper[:, 2 * t - 1] = y[:, :, :128]
        if t < 5:
            upper[:, 2 * t] = y[:, :, 128:]

    def cot(up, pre):
        return jnp.where(pre.astype(F32) > 0, up, SLOPE * up).astype(BF16)

    for f in range(1, 5):
        slot = (f + 1) // 2
        for h in range(18):
            parent = (h + 1) // 2
            if h == 0:
                pre = up_ref[256 + 64 * (f - 1) : 320 + 64 * (f - 1)]
            elif h == 17:
                pre = down_ref[256 + 64 * (f - 1) : 320 + 64 * (f - 1)]
            else:
                pre = pre_ref[f - 1, h - 1]
            z_out[f, h] = cot(upper[slot, parent], pre)
    edge = 5 * (1 - dep)
    slot = 3 * (1 - dep)
    z_out[5 * dep] = jnp.zeros((18, 64, 128), BF16)
    for h in range(18):
        parent = (h + 1) // 2
        if h == 0:
            pre = dup_ref[256:]
        elif h == 17:
            pre = ddown_ref[256:]
        else:
            pre = side_ref[h - 1]
        z_out[edge, h] = cot(upper[slot, parent], pre)
    parts = [None, None, None]
    for z in range(6):
        first, final = max(0, z - 2), min(3, z)
        total = None
        for h in range(4):
            lhs = jnp.concatenate([act_ref[h + 4 * i, 96 * first : 96 * (final + 1), :] for i in range(4)], axis=1)
            rhs = jnp.concatenate(
                [z_out[z, h + 4 * i : h + 4 * i + 3].reshape(192, 128) for i in range(4)], axis=1
            )
            r = dot_nt(lhs, rhs)
            total = r if total is None else total + r
        for d in range(first, final + 1):
            part = total[96 * (d - first) : 96 * (d - first + 1)]
            parts[z - d] = part if parts[z - d] is None else parts[z - d] + part
    for od in range(3):
        for oh in range(3):
            for ow in range(3):
                k = (2 - od) * 9 + (2 - oh) * 3 + (2 - ow)
                t2[pl.ds(k, 32, stride=27), :] = parts[od][32 * ow : 32 * ow + 32, 64 * oh : 64 * oh + 64]
    grad_out[...] = jnp.transpose(t2[...]).astype(BF16)


def into(scale, z_ref, w2_ref, out_ref, rows):
    lane = lax.broadcasted_iota(jnp.int32, (256, 128), 1)
    for jp in range(4):
        acc = [None] * 4
        for z in range(6):
            blocks = []
            for j in (2 * jp, 2 * jp + 1):
                x = z_ref[z, 2 * j : 2 * j + 4].reshape(256, 128)
                left = jnp.where(lane > 0, shifted(x, -1), jnp.zeros_like(x))
                right = jnp.where(lane < 127, shifted(x, 1), jnp.zeros_like(x))
                blocks.append(jnp.concatenate([left, x, right], axis=0))
            rhs = jnp.concatenate(blocks, axis=1)
            first, final = max(0, z - 2), min(3, z)
            low = 2 - z + first
            y = dot_nn(w2_ref[64 * low : 64 * (low + final - first + 1), :], rhs)
            for d in range(first, final + 1):
                part = y[64 * (d - first) : 64 * (d - first + 1)]
                acc[d] = part if acc[d] is None else acc[d] + part
        for d in range(4):
            for j in range(2):
                for r in range(2):
                    rows[d, 4 * jp + 2 * j + r] = acc[d][32 * r : 32 * r + 32, 128 * j : 128 * j + 128]
    for d in range(4):
        out_ref[:, d] = (scale * jnp.swapaxes(rows[d], 0, 1)).astype(BF16)


def local(act_one, pre_two, cot_three, weight_two, weight_three, moment_two, moment_three):
    scale_two = (act_one.shape[1] * 27) ** (-0.5)
    scale_three = (pre_two.shape[1] * 27) ** (-0.5)
    volumes = lax.axis_size("dp")
    devices = lax.axis_size(AXES)
    pre, act, cot = pre_two[0], act_one[0], cot_three[0]

    cot_rows, pre_rows, send_up, send_down, send_side, send_dup, send_ddown = call(
        arrange,
        [((2, 128, 512), BF16), ((4, 16, 64, 128), BF16), ((512, 128), BF16), ((512, 128), BF16),
         ((16, 64, 128), BF16), ((320, 128), BF16), ((320, 128), BF16)],
        moved=4_000_000,
    )(cot, pre)
    pair = ("depth", "height")
    tall = lax.axis_size("height")
    swap = [(0, 1), (1, 0)]
    lower = [(h, h - 1) for h in range(1, tall)]
    raise_ = [(h, h + 1) for h in range(tall - 1)]
    cross_lower = [(d * tall + h, (1 - d) * tall + h - 1) for d in range(2) for h in range(1, tall)]
    cross_raise = [(d * tall + h, (1 - d) * tall + h + 1) for d in range(2) for h in range(tall - 1)]
    cot_side = lax.ppermute(cot_rows, "depth", swap)
    from_down = lax.ppermute(send_up, "height", lower)
    from_up = lax.ppermute(send_down, "height", raise_)
    from_ddown = lax.ppermute(send_dup, pair, cross_lower)
    from_dup = lax.ppermute(send_ddown, pair, cross_raise)
    pre_side = lax.ppermute(send_side, "depth", swap)

    pooled, acts, wide_two, wide_three, norms = pl.pallas_call(
        prepare,
        out_shape=[
            jax.ShapeDtypeStruct((128, 512), BF16),
            jax.ShapeDtypeStruct((16, 384, 128), BF16),
            jax.ShapeDtypeStruct((192, 768), BF16),
            jax.ShapeDtypeStruct((192, 1152), BF16),
            jax.ShapeDtypeStruct((2,), F32),
        ],
        out_specs=[pl.BlockSpec(memory_space=pltpu.VMEM)] * 4 + [pl.BlockSpec(memory_space=pltpu.SMEM)],
        scratch_shapes=[pltpu.VMEM((864, 64), F32), pltpu.VMEM((1728, 128), F32)],
        compiler_params=pltpu.CompilerParams(vmem_limit_bytes=48 * 1024 * 1024),
        cost_estimate=pl.CostEstimate(flops=100_000_000, bytes_accessed=8_000_000, transcendentals=0),
    )(pre_rows, act, weight_two, weight_three)

    back, part_three = call(
        lambda *refs: coarse(scale_three, *refs),
        [((4, 64, 768), BF16), ((128, 1728), BF16)],
        [pltpu.VMEM((6, 128, 768), BF16), pltpu.VMEM((5, 1152, 768), BF16), pltpu.VMEM((1728, 128), F32)],
        flops=2_000_000_000, moved=4_000_000,
    )(cot_rows, cot_side, from_up, from_down, from_dup, from_ddown, wide_three, pooled)

    cot_two, part_two = call(
        fine,
        [((6, 18, 64, 128), BF16), ((64, 864), BF16)],
        [pltpu.VMEM((4, 10, 64, 128), F32), pltpu.VMEM((864, 64), F32)],
        flops=2_000_000_000, moved=6_000_000,
    )(back, pre_rows, pre_side, from_up, from_down, from_dup, from_ddown, acts)

    grad_input, = call(
        lambda *refs: into(scale_two, *refs),
        [((32, 4, 16, 128), BF16)],
        [pltpu.VMEM((4, 16, 32, 128), F32)],
        flops=4_000_000_000, moved=6_000_000,
    )(cot_two, wide_two)

    shard_two = moment_two.shape[0]
    shard_three = moment_three.shape[0]
    parts = jnp.concatenate([part_two.reshape(devices, shard_two), part_three], axis=1)
    parts = lax.all_to_all(parts, AXES, 0, 0, tiled=True)
    own = jnp.sum(parts.astype(F32), axis=0)
    own_two = own[:shard_two] * (scale_two / volumes)
    own_three = own[shard_two:] * (scale_three / volumes)
    send = jnp.concatenate([own_two, own_three, moment_two, moment_three]).astype(BF16)
    send = jnp.broadcast_to(send[None], (devices, send.shape[0]))
    full = lax.all_to_all(send, AXES, 0, 0, tiled=True).astype(F32)
    shard = shard_two + shard_three
    grad_two = full[:, :shard_two]
    grad_three = full[:, shard_two:shard]
    all_two = full[:, shard : shard + shard_two]
    all_three = full[:, shard + shard_two :]
    trust_two = TRUST * norms[0] / (jnp.sqrt(jnp.sum(grad_two * grad_two)) + EPSILON)
    trust_three = TRUST * norms[1] / (jnp.sqrt(jnp.sum(grad_three * grad_three)) + EPSILON)
    new_moment_two = MOMENTUM * moment_two + LEARN * trust_two * own_two
    new_moment_three = MOMENTUM * moment_three + LEARN * trust_three * own_three
    full_two = MOMENTUM * all_two + LEARN * trust_two * grad_two
    full_three = MOMENTUM * all_three + LEARN * trust_three * grad_three
    new_weight_two = weight_two - full_two.reshape(weight_two.shape)
    new_weight_three = weight_three - full_three.reshape(weight_three.shape)
    return (grad_input[None], new_weight_two, new_weight_three, new_moment_two, new_moment_three)


def solution(mesh):
    in_specs = (
        P("dp", None, "depth", "height", None),
        P("dp", None, "depth", "height", None),
        P("dp", None, "depth", "height"),
        P(),
        P(),
        P(AXES),
        P(AXES),
    )
    out_specs = (
        P("dp", None, "depth", "height", None),
        P(),
        P(),
        P(AXES),
        P(AXES),
    )
    return jax.shard_map(local, mesh=mesh, in_specs=in_specs, out_specs=out_specs, check_vma=False)
```

profile of v0, /device:TPU:1, one launch (start us, length us, event | category | flops | bytes accessed | tf_op | source)
XLA Modules:
  0.0 123.4 jit_solution(9848729865419554154)
XLA Ops:
  0.6 1.2 copy-done
  1.9 0.9 copy-done.3
  2.8 1.9 %shard_map.110 = (bf16[2,128,512]{2,1,0:T(8,128)(2,1)S(1)}, bf16[4,16,64,128]{3,2,1,0:T(8,128)(2,1)S(1)}, bf16[512,128]{1,0:T(8,128)(2,1)}, bf16[512,128]{1,0:T(...) custom-call(bf16[128,2,512]{2,1,0:T(2,128)(2,1)S(1)} %bitcast.13, ...), custom_call_target="tpu_custom_call" | custom-call | bytes 4000000 | tf_op jit(solution)/shard_map/pallas_call | solution.py:273
  4.7 2.1 %collective-permute-start = (bf16[2,128,512]{2,1,0:T(8,128)(2,1)S(1)}, bf16[2,128,512]{2,1,0:T(8,128)(2,1)}, u32[]{:S(2)}, u32[]{:S(2)}) collective-permute-start(bf16[2,128,512]{2,1,0:T(8,128)(2,1)S(1)} %get-tuple-element.21.refs_0_), channel_id=1, source_target_pairs={{0,8},{8,0},{1,9},{9,1},{2,10},{10,2},{3,11},{11,3},{4,12},{12,4},... | collective-permute-start | bytes 786440 | tf_op jit(solution)/shard_map/ppermute | solution.py:286
  6.9 3.8 %collective-permute-start.3 = (bf16[320,128]{1,0:T(8,128)(2,1)S(1)}, bf16[320,128]{1,0:T(8,128)(2,1)S(1)}, u32[]{:S(2)}, u32[]{:S(2)}) collective-permute-start(bf16[320,128]{1,0:T(8,128)(2,1)S(1)} %get-tuple-element.24), channel_id=1, source_target_pairs={{0,9},{1,10},{2,11},{3,12},{4,13},{5,14},{6,15},{8,1},{9,2},{10,3}... | collective-permute-start | bytes 245768 | tf_op jit(solution)/shard_map/ppermute | solution.py:290
  10.7 4.1 %collective-permute-start.1 = (bf16[512,128]{1,0:T(8,128)(2,1)}, bf16[512,128]{1,0:T(8,128)(2,1)}, u32[]{:S(2)}, u32[]{:S(2)}) collective-permute-start(bf16[512,128]{1,0:T(8,128)(2,1)} %get-tuple-element.22), channel_id=1, source_target_pairs={{0,1},{1,2},{2,3},{3,4},{4,5},{5,6},{6,7},{8,9},{9,10},{10,11},{11... | collective-permute-start | bytes 393224 | tf_op jit(solution)/shard_map/ppermute | solution.py:288
  14.8 1.3 %collective-permute-start.2 = (bf16[512,128]{1,0:T(8,128)(2,1)}, bf16[512,128]{1,0:T(8,128)(2,1)}, u32[]{:S(2)}, u32[]{:S(2)}) collective-permute-start(bf16[512,128]{1,0:T(8,128)(2,1)} %get-tuple-element.23), channel_id=1, source_target_pairs={{1,0},{2,1},{3,2},{4,3},{5,4},{6,5},{7,6},{9,8},{10,9},{11,10},{12... | collective-permute-start | bytes 393224 | tf_op jit(solution)/shard_map/ppermute | solution.py:287
  16.1 1.3 %collective-permute-start.4 = (bf16[320,128]{1,0:T(8,128)(2,1)}, bf16[320,128]{1,0:T(8,128)(2,1)}, u32[]{:S(2)}, u32[]{:S(2)}) collective-permute-start(bf16[320,128]{1,0:T(8,128)(2,1)} %get-tuple-element.25), channel_id=1, source_target_pairs={{1,8},{2,9},{3,10},{4,11},{5,12},{6,13},{7,14},{9,0},{10,1},{11,2}... | collective-permute-start | bytes 245768 | tf_op jit(solution)/shard_map/ppermute | solution.py:289
  17.4 1.2 %collective-permute-start.5 = (bf16[16,64,128]{2,1,0:T(8,128)(2,1)S(1)}, bf16[16,64,128]{2,1,0:T(8,128)(2,1)}, u32[]{:S(2)}, u32[]{:S(2)}) collective-permute-start(bf16[16,64,128]{2,1,0:T(8,128)(2,1)S(1)} %get-tuple-element.30), channel_id=1, source_target_pairs={{0,8},{8,0},{1,9},{9,1},{2,10},{10,2},{3,11},{11,3},{4,12},{12,4},... | collective-permute-start | bytes 786440 | tf_op jit(solution)/shard_map/ppermute | solution.py:291
  18.6 1.5 %copy.19.w3_ref = f32[128,1728]{1,0:T(8,128)S(1)} copy(f32[128,1728]{0,1:T(8,128)} %param.11) | data formatting | bytes 1769472 | tf_op args[4]
  20.1 1.9 %shard_map.111 = (bf16[128,512]{1,0:T(8,128)(2,1)S(1)}, bf16[16,384,128]{2,1,0:T(8,128)(2,1)S(1)}, bf16[192,768]{1,0:T(8,128)(2,1)S(1)}, bf16[192,1152]{1,0:T(8,128)(2,1)S(1)}, f32[2]{0:T(128)S(1)}) custom-call(bf16[4,16,64,128]{3,2,1,0:T(8,128)(2,1)S(1)} %get-tuple-element.26.pre_ref, bf16[32,4,16,128]{3,2,1,0:T(8,128)(2,1)S(1)} %bitcast.12, ...), custom_call_target="tpu_custom_call" | custom-call | flops 100000000 | bytes 8000000 | tf_op jit(solution)/shard_map/pallas_call | solution.py:293
  22.0 3.0 %collective-permute-done.4.refs_5_.ddown_ref = bf16[320,128]{1,0:T(8,128)(2,1)} collective-permute-done((bf16[320,128]{1,0:T(8,128)(2,1)}, bf16[320,128]{1,0:T(8,128)(2,1)}, u32[]{:S(2)}, u32[]{:S(2)}) %collective-permute-start.4) | collective-permute-done | bytes 81952 | tf_op jit(solution)/shard_map/ppermute | solution.py:289
  25.0 5.3 %shard_map.112 = (bf16[4,64,768]{2,1,0:T(8,128)(2,1)S(1)}, bf16[128,1728]{1,0:T(8,128)(2,1)S(1)}) custom-call(bf16[2,128,512]{2,1,0:T(8,128)(2,1)S(1)} %get-tuple-element.21.refs_0_, bf16[2,128,512]{2,1,0:T(8,128)(2,1)} %collective-permute-done.refs_1_, bf16[512,128]{1,0:T(8,128)(2,1)} %collective-permute-done.1.refs_2_.up_ref, ...), custom_call_target="tpu_custom_call" | custom-call | flops 2000000000 | bytes 4000000 | tf_op jit(solution)/shard_map/pallas_call | solution.py:308
  30.4 3.7 %shard_map.113 = (bf16[6,18,64,128]{3,2,1,0:T(8,128)(2,1)S(1)}, bf16[64,864]{1,0:T(8,128)(2,1)S(1)}) custom-call(bf16[4,64,768]{2,1,0:T(8,128)(2,1)S(1)} %get-tuple-element.29.back_ref, bf16[4,16,64,128]{3,2,1,0:T(8,128)(2,1)S(1)} %get-tuple-element.26.pre_ref, bf16[16,64,128]{2,1,0:T(8,128)(2,1)} %collective-permute-done.5.side_ref, ...), custom_call_target="tpu_custom_call" | custom-call | flops 2000000000 | bytes 6000000 | tf_op jit(solution)/shard_map/pallas_call | solution.py:315
  34.0 1.2 copy-done.6
  36.1 1.0 reduce.1
  37.1 1.4 %reshape.63 = bf16[128,2,1080]{2,1,0:T(2,128)(2,1)} reshape(bf16[128,2160]{1,0:T(8,128)(2,1)S(1)} %reduce.1) | data formatting | bytes 1105920
  38.5 12.6 %all-to-all-start = ((bf16[128,2,1080]{2,1,0:T(2,128)(2,1)}), bf16[128,2,1080]{2,1,0:T(2,128)(2,1)S(1)}, u32[]{:S(2)}, u32[]{:S(2)}) async-start(bf16[128,2,1080]{2,1,0:T(2,128)(2,1)} %reshape.63), calls=%async_computation | async-start | bytes 1179648 | tf_op jit(solution)/shard_map/all_to_all | solution.py:332
  51.2 14.4 %all-to-all-done = bf16[128,2,1080]{2,1,0:T(2,128)(2,1)S(1)} async-done(((bf16[128,2,1080]{2,1,0:T(2,128)(2,1)}), bf16[128,2,1080]{2,1,0:T(2,128)(2,1)S(1)}, u32[]{:S(2)}, u32[]{:S(2)}) %all-to-all-start) | async-done | bytes 552992 | tf_op jit(solution)/shard_map/all_to_all | solution.py:332
  66.3 1.2 convert_reduce_fusion
  67.7 1.1 broadcast_in_dim.10
  68.8 9.0 %reduce.2 = bf16[128,4320]{1,0:T(8,128)(2,1)} reduce(bf16[128,1,4320]{2,1,0:T(2,128)(2,1)S(1)} %broadcast_in_dim.10, bf16[]{:T(256)} %broadcast.6), dimensions={1}, to_apply=%broadcast_in_dim.10.reduce_sub_computation | reduce | bytes 2211842 | tf_op jit(solution)/shard_map/broadcast_in_dim | solution.py:337
  77.8 2.6 %reshape.65 = bf16[128,2,2160]{2,1,0:T(2,128)(2,1)} reshape(bf16[128,4320]{1,0:T(8,128)(2,1)} %reduce.2) | data formatting | bytes 2211840
  80.4 5.0 %all-to-all-start.1 = ((bf16[128,2,2160]{2,1,0:T(2,128)(2,1)}), bf16[128,2,2160]{2,1,0:T(2,128)(2,1)}, u32[]{:S(2)}, u32[]{:S(2)}) async-start(bf16[128,2,2160]{2,1,0:T(2,128)(2,1)} %reshape.65), calls=%async_computation.1 | async-start | bytes 2228224 | tf_op jit(solution)/shard_map/all_to_all | solution.py:338
  87.3 3.0 %shard_map.114 = bf16[32,4,16,128]{3,2,1,0:T(8,128)(2,1)} custom-call(bf16[6,18,64,128]{3,2,1,0:T(8,128)(2,1)S(1)} %copy-done.7, bf16[192,768]{1,0:T(8,128)(2,1)S(1)} %get-tuple-element.33.refs_1_), custom_call_target="tpu_custom_call" | custom-call | flops 4000000000 | bytes 6000000 | tf_op jit(solution)/shard_map/pallas_call | solution.py:322
  90.3 14.8 %all-to-all-done.1 = bf16[128,2,2160]{2,1,0:T(2,128)(2,1)} async-done(((bf16[128,2,2160]{2,1,0:T(2,128)(2,1)}), bf16[128,2,2160]{2,1,0:T(2,128)(2,1)}, u32[]{:S(2)}, u32[]{:S(2)}) %all-to-all-start.1) | async-done | bytes 1105952 | tf_op jit(solution)/shard_map/all_to_all | solution.py:338
  105.1 7.0 %reshape.66 = bf16[128,1,4320]{2,1,0:T(2,128)(2,1)S(1)} reshape(bf16[128,2,2160]{2,1,0:T(2,128)(2,1)} %all-to-all-done.1) | data formatting | bytes 2211840
  112.1 3.6 %copy.21 = bf16[128,1,4320]{0,2,1:T(8,128)(2,1)} copy(bf16[128,1,4320]{2,1,0:T(2,128)(2,1)S(1)} %reshape.66) | data formatting | bytes 2211840 | tf_op jit(solution)/shard_map/all_to_all | solution.py:338
  115.7 1.4 %bitcast_convert_fusion = f32[128,4320]{0,1:T(8,128)S(1)} fusion(bf16[128,1,4320]{0,2,1:T(8,128)(2,1)} %copy.21), kind=kLoop, calls=%fused_computation.1 | loop fusion | flops 552960 | bytes 3317760 | tf_op jit(solution)/shard_map/convert_element_type | solution.py:338
  117.1 0.8 multiply_reduce_fusion
  121.3 1.0 fusion.1
  122.6 0.7 sub.6
  (40 shorter events, 4.5 us)
Async XLA Ops:
  0.6 1.2 copy-start
  1.9 0.9 copy-start.3
  4.7 15.4 %copy-start.1 = (f32[64,864]{1,0:T(8,128)S(1)}, f32[64,864]{1,0:T(8,128)}, u32[]{:S(2)}) copy-start(f32[64,864]{1,0:T(8,128)} %w2_ref.1) | copy-start | bytes 663556
  4.7 15.4 %copy-start.2 = (bf16[1,32,4,16,128]{4,3,2,1,0:T(8,128)(2,1)S(1)}, bf16[1,32,4,16,128]{4,3,2,1,0:T(8,128)(2,1)}, u32[]{:S(2)}) copy-start(bf16[1,32,4,16,128]{4,3,2,1,0:T(8,128)(2,1)} %param.7) | copy-start | bytes 1572868
  4.7 20.3 %collective-permute-start = (bf16[2,128,512]{2,1,0:T(8,128)(2,1)S(1)}, bf16[2,128,512]{2,1,0:T(8,128)(2,1)}, u32[]{:S(2)}, u32[]{:S(2)}) collective-permute-start(bf16[2,128,512]{2,1,0:T(8,128)(2,1)S(1)} %get-tuple-element.21.refs_0_), channel_id=1, source_target_pairs={{0,8},{8,0},{1,9},{9,1},{2,10},{10,2},{3,11},{11,3},{4,12},{12,4},... | collective-permute-start | bytes 786440 | tf_op jit(solution)/shard_map/ppermute | solution.py:286
  6.9 10.5 %collective-permute-start.3 = (bf16[320,128]{1,0:T(8,128)(2,1)S(1)}, bf16[320,128]{1,0:T(8,128)(2,1)S(1)}, u32[]{:S(2)}, u32[]{:S(2)}) collective-permute-start(bf16[320,128]{1,0:T(8,128)(2,1)S(1)} %get-tuple-element.24), channel_id=1, source_target_pairs={{0,9},{1,10},{2,11},{3,12},{4,13},{5,14},{6,15},{8,1},{9,2},{10,3}... | collective-permute-start | bytes 245768 | tf_op jit(solution)/shard_map/ppermute | solution.py:290
  10.7 14.3 %collective-permute-start.1 = (bf16[512,128]{1,0:T(8,128)(2,1)}, bf16[512,128]{1,0:T(8,128)(2,1)}, u32[]{:S(2)}, u32[]{:S(2)}) collective-permute-start(bf16[512,128]{1,0:T(8,128)(2,1)} %get-tuple-element.22), channel_id=1, source_target_pairs={{0,1},{1,2},{2,3},{3,4},{4,5},{5,6},{6,7},{8,9},{9,10},{10,11},{11... | collective-permute-start | bytes 393224 | tf_op jit(solution)/shard_map/ppermute | solution.py:288
  14.8 10.2 %collective-permute-start.2 = (bf16[512,128]{1,0:T(8,128)(2,1)}, bf16[512,128]{1,0:T(8,128)(2,1)}, u32[]{:S(2)}, u32[]{:S(2)}) collective-permute-start(bf16[512,128]{1,0:T(8,128)(2,1)} %get-tuple-element.23), channel_id=1, source_target_pairs={{1,0},{2,1},{3,2},{4,3},{5,4},{6,5},{7,6},{9,8},{10,9},{11,10},{12... | collective-permute-start | bytes 393224 | tf_op jit(solution)/shard_map/ppermute | solution.py:287
  16.1 9.0 %collective-permute-start.4 = (bf16[320,128]{1,0:T(8,128)(2,1)}, bf16[320,128]{1,0:T(8,128)(2,1)}, u32[]{:S(2)}, u32[]{:S(2)}) collective-permute-start(bf16[320,128]{1,0:T(8,128)(2,1)} %get-tuple-element.25), channel_id=1, source_target_pairs={{1,8},{2,9},{3,10},{4,11},{5,12},{6,13},{7,14},{9,0},{10,1},{11,2}... | collective-permute-start | bytes 245768 | tf_op jit(solution)/shard_map/ppermute | solution.py:289
  17.4 2.7 %copy-start.4 = (bf16[320,128]{1,0:T(8,128)(2,1)}, bf16[320,128]{1,0:T(8,128)(2,1)S(1)}, u32[]{:S(2)}) copy-start(bf16[320,128]{1,0:T(8,128)(2,1)S(1)} %collective-permute-done.3.refs_4_.dup_ref) | copy-start | bytes 245764
  17.4 13.0 %collective-permute-start.5 = (bf16[16,64,128]{2,1,0:T(8,128)(2,1)S(1)}, bf16[16,64,128]{2,1,0:T(8,128)(2,1)}, u32[]{:S(2)}, u32[]{:S(2)}) collective-permute-start(bf16[16,64,128]{2,1,0:T(8,128)(2,1)S(1)} %get-tuple-element.30), channel_id=1, source_target_pairs={{0,8},{8,0},{1,9},{9,1},{2,10},{10,2},{3,11},{11,3},{4,12},{12,4},... | collective-permute-start | bytes 786440 | tf_op jit(solution)/shard_map/ppermute | solution.py:291
  20.1 4.9 %copy-start.5 = (bf16[320,128]{1,0:T(8,128)(2,1)S(1)}, bf16[320,128]{1,0:T(8,128)(2,1)}, u32[]{:S(2)}) copy-start(bf16[320,128]{1,0:T(8,128)(2,1)} %copy-done.4) | copy-start | bytes 245764
  34.0 1.2 copy-start.6
  37.1 14.1 %copy-start.9 = (f32[1728]{0:T(1024)S(1)}, f32[1728]{0:T(1024)}, u32[]{:S(2)}) copy-start(f32[1728]{0:T(1024)} %param.13) | copy-start | bytes 20740
  37.1 14.1 %copy-start.10 = (f32[432]{0:T(512)S(1)}, f32[432]{0:T(512)}, u32[]{:S(2)}) copy-start(f32[432]{0:T(512)} %param.12) | copy-start | bytes 5188
  38.5 27.1 %all-to-all-start = ((bf16[128,2,1080]{2,1,0:T(2,128)(2,1)}), bf16[128,2,1080]{2,1,0:T(2,128)(2,1)S(1)}, u32[]{:S(2)}, u32[]{:S(2)}) async-start(bf16[128,2,1080]{2,1,0:T(2,128)(2,1)} %reshape.63), calls=%async_computation | async-start | bytes 1179648 | tf_op jit(solution)/shard_map/all_to_all | solution.py:332
  80.4 6.9 %copy-start.7 = (bf16[6,18,64,128]{3,2,1,0:T(8,128)(2,1)S(1)}, bf16[6,18,64,128]{3,2,1,0:T(8,128)(2,1)}, u32[]{:S(2)}) copy-start(bf16[6,18,64,128]{3,2,1,0:T(8,128)(2,1)} %copy-done.6) | copy-start | bytes 5308420
  80.4 24.6 %all-to-all-start.1 = ((bf16[128,2,2160]{2,1,0:T(2,128)(2,1)}), bf16[128,2,2160]{2,1,0:T(2,128)(2,1)}, u32[]{:S(2)}, u32[]{:S(2)}) async-start(bf16[128,2,2160]{2,1,0:T(2,128)(2,1)} %reshape.65), calls=%async_computation.1 | async-start | bytes 2228224 | tf_op jit(solution)/shard_map/all_to_all | solution.py:338
  117.1 4.2 %copy-start.8 = (f32[128,1728]{0,1:T(8,128)S(1)}, f32[128,1728]{0,1:T(8,128)}, u32[]{:S(2)}) copy-start(f32[128,1728]{0,1:T(8,128)} %param.11) | copy-start | bytes 2654212
where the time goes:
time: 124 us; the launch traced here: 123 us
  waiting for transfers between devices  32.2 us (26%)
  starting transfers between devices  31.4 us (25%)
  local copies, waits for them, and re-layouts  22.9 us (18%)
  other arithmetic  17.4 us (14%)
  Pallas kernels  15.8 us (13%)
  between operations  3.69 us (3%)
    unnamed x27, local copies, waits for them, and re-layouts  16.6 us
    all_to_all x1, waiting for transfers between devices, local(): full = lax.all_to_all(send, AXES, 0, 0, tiled=True).astype(F32)  14.8 us
    all_to_all x1, waiting for transfers between devices, local(): parts = lax.all_to_all(parts, AXES, 0, 0, tiled=True)  14.4 us
    all_to_all x1, starting transfers between devices, local(): parts = lax.all_to_all(parts, AXES, 0, 0, tiled=True)  12.6 us
    broadcast_in_dim x1, other arithmetic, local(): send = jnp.broadcast_to(send[None], (devices, send.shape[0]))  9 us
    pallas_call x1, Pallas kernels, local(): call(lambda *refs: coarse(scale_three, *refs), [((4, 64, 768), BF16), ((1...  5.31 us
    all_to_all x1, starting transfers between devices, local(): full = lax.all_to_all(send, AXES, 0, 0, tiled=True).astype(F32)  4.96 us
    ppermute x1, starting transfers between devices, local(): from_up = lax.ppermute(send_down, 'height', raise_)  4.1 us
  transfers between devices with their start and end apart: 8, of which 3 were waited for; matrix products, arithmetic and copies ran while one was open for 2% of the time, Pallas kernels for 8%

commit v1 on v0

--- a/solution.py
+++ b/solution.py
@@ -63,7 +63,7 @@
                 diag_down_out[256:] = rows[15]
 
 
-def prepare(pre_ref, act_ref, w2_ref, w3_ref, pooled_out, act_out, w2_out, w3_out, norm_out, t2, t3):
+def prepare(pre_ref, act_ref, w2_ref, w3_ref, pooled_out, act_out, w2_out, w3_out, t2, t3):
     row = lax.broadcasted_iota(jnp.int32, (256, 128), 0)
     col = lax.broadcasted_iota(jnp.int32, (256, 128), 1)
     pool = jnp.where(row // 2 == col, 0.125, 0.0).astype(BF16)
@@ -91,12 +91,8 @@
         for ow, value in enumerate((before, rows, after)):
             start = 96 * d + 32 * ow
             act_out[:, start : start + 32, :] = value.astype(BF16)
-    w2 = w2_ref[...]
-    w3 = w3_ref[...]
-    norm_out[0] = jnp.sqrt(jnp.sum(w2 * w2))
-    norm_out[1] = jnp.sqrt(jnp.sum(w3 * w3))
-    t2[...] = jnp.transpose(w2)
-    t3[...] = jnp.transpose(w3)
+    t2[...] = jnp.transpose(w2_ref[...])
+    t3[...] = jnp.transpose(w3_ref[...])
     for kd in range(3):
         for oh in range(3):
             for ow in range(3):
@@ -172,11 +168,13 @@
                 k = (2 - od) * 9 + (2 - oh) * 3 + (2 - ow)
                 tap = oh * 3 + ow
                 t3[pl.ds(k, 64, stride=27), :] = parts[od][:, 128 * tap : 128 * tap + 128]
-    grad_out[...] = jnp.transpose(t3[...]).astype(BF16)
-
-
-def fine(back_ref, pre_ref, side_ref, up_ref, down_ref, dup_ref, ddown_ref, act_ref,
-         z_out, grad_out, upper, t2):
+    t3[1728:] = jnp.zeros((64, 128), F32)
+    for b in range(14):
+        grad_out[b] = jnp.transpose(t3[128 * b : 128 * b + 128, :])
+
+
+def fine(back_ref, pre_ref, side_ref, up_ref, down_ref, dup_ref, ddown_ref, act_ref, three_ref,
+         z_out, parts_out, upper, t2, stage):
     dep = lax.axis_index("depth")
     row = lax.broadcasted_iota(jnp.int32, (128, 256), 0)
     col = lax.broadcasted_iota(jnp.int32, (128, 256), 1)
@@ -234,7 +232,19 @@
             for ow in range(3):
                 k = (2 - od) * 9 + (2 - oh) * 3 + (2 - ow)
                 t2[pl.ds(k, 32, stride=27), :] = parts[od][32 * ow : 32 * ow + 32, 64 * oh : 64 * oh + 64]
-    grad_out[...] = jnp.transpose(t2[...]).astype(BF16)
+    t2[864:] = jnp.zeros((80, 64), F32)
+    tail = lax.broadcasted_iota(jnp.int32, (64, 128), 1) < 48
+    for half in range(2):
+        for b in range(4):
+            start = 432 * half + 128 * b
+            block = jnp.transpose(t2[start : start + 128, :])
+            if b == 3:
+                block = jnp.where(tail, block, 0.0)
+            stage[pl.ds(half, 64, stride=2), b, :] = block
+    for b in range(14):
+        stage[:, 4 + b, :] = three_ref[b]
+    stage[:, 18:, :] = jnp.zeros((128, 6, 128), F32)
+    parts_out[...] = stage[...].astype(BF16)
 
 
 def into(scale, z_ref, w2_ref, out_ref, rows):
@@ -263,11 +273,56 @@
         out_ref[:, d] = (scale * jnp.swapaxes(rows[d], 0, 1)).astype(BF16)
 
 
+def reduce(scale_two, scale_three, parts_ref, m2_ref, m3_ref, send_out, own_out, rows):
+    total = jnp.sum(parts_ref[...].astype(F32), axis=0)
+    row = lax.broadcasted_iota(jnp.int32, (24, 128), 0)
+    total = total * jnp.where(row < 4, scale_two, scale_three)
+    own_out[...] = total
+    rows[...] = jnp.zeros((40, 128), F32)
+    rows[:18] = total[:18]
+    for b in range(3):
+        rows[18 + b, :] = m2_ref[pl.ds(128 * b, 128)]
+    rows[21, :48] = m2_ref[pl.ds(384, 48)]
+    for b in range(13):
+        rows[22 + b, :] = m3_ref[pl.ds(128 * b, 128)]
+    rows[35, :64] = m3_ref[pl.ds(1664, 64)]
+    send_out[...] = jnp.broadcast_to(rows[...].astype(BF16)[None], (128, 40, 128))
+
+
+def update(full_ref, own_ref, w2_ref, w3_ref, m2_ref, m3_ref, w2_out, w3_out, m2_out, m3_out, stage):
+    w2 = w2_ref[...]
+    w3 = w3_ref[...]
+    grad = full_ref[:, :18, :].astype(F32)
+    square = jnp.sum(grad * grad, axis=0)
+    row = lax.broadcasted_iota(jnp.int32, (18, 128), 0)
+    norm_two = jnp.sqrt(jnp.sum(jnp.where(row < 4, square, 0.0), keepdims=True))
+    norm_three = jnp.sqrt(jnp.sum(jnp.where(row < 4, 0.0, square), keepdims=True))
+    rate_two = LEARN * (TRUST * jnp.sqrt(jnp.sum(w2 * w2, keepdims=True)) / (norm_two + EPSILON))
+    rate_three = LEARN * (TRUST * jnp.sqrt(jnp.sum(w3 * w3, keepdims=True)) / (norm_three + EPSILON))
+    rate = jnp.where(row < 4, rate_two, rate_three)
+    stage[...] = MOMENTUM * full_ref[:, 18:36, :].astype(F32) + rate[None] * grad
+    for b in range(13):
+        cols = slice(128 * b, 128 * b + 128)
+        w3_out[:, cols] = w3[:, cols] - stage[:, 4 + b, :]
+    w3_out[:, 1664:] = w3[:, 1664:] - stage[:, 17, :64]
+    halves = []
+    for half in range(2):
+        blocks = [stage[pl.ds(half, 64, stride=2), b, :] for b in range(4)]
+        halves.append(jnp.concatenate(blocks, axis=1)[:, :432])
+    w2_out[...] = w2 - jnp.concatenate(halves, axis=1)
+    own = rate * own_ref[:18]
+    for b in range(3):
+        m2_out[pl.ds(128 * b, 128)] = MOMENTUM * m2_ref[pl.ds(128 * b, 128)] + own[b]
+    m2_out[pl.ds(384, 48)] = MOMENTUM * m2_ref[pl.ds(384, 48)] + own[3, :48]
+    for b in range(13):
+        m3_out[pl.ds(128 * b, 128)] = MOMENTUM * m3_ref[pl.ds(128 * b, 128)] + own[4 + b]
+    m3_out[pl.ds(1664, 64)] = MOMENTUM * m3_ref[pl.ds(1664, 64)] + own[17, :64]
+
+
 def local(act_one, pre_two, cot_three, weight_two, weight_three, moment_two, moment_three):
     scale_two = (act_one.shape[1] * 27) ** (-0.5)
     scale_three = (pre_two.shape[1] * 27) ** (-0.5)
     volumes = lax.axis_size("dp")
-    devices = lax.axis_size(AXES)
     pre, act, cot = pre_two[0], act_one[0], cot_three[0]
 
     cot_rows, pre_rows, send_up, send_down, send_side, send_dup, send_ddown = call(
@@ -290,34 +345,26 @@
     from_dup = lax.ppermute(send_ddown, pair, cross_raise)
     pre_side = lax.ppermute(send_side, "depth", swap)
 
-    pooled, acts, wide_two, wide_three, norms = pl.pallas_call(
+    pooled, acts, wide_two, wide_three = call(
         prepare,
-        out_shape=[
-            jax.ShapeDtypeStruct((128, 512), BF16),
-            jax.ShapeDtypeStruct((16, 384, 128), BF16),
-            jax.ShapeDtypeStruct((192, 768), BF16),
-            jax.ShapeDtypeStruct((192, 1152), BF16),
-            jax.ShapeDtypeStruct((2,), F32),
-        ],
-        out_specs=[pl.BlockSpec(memory_space=pltpu.VMEM)] * 4 + [pl.BlockSpec(memory_space=pltpu.SMEM)],
-        scratch_shapes=[pltpu.VMEM((864, 64), F32), pltpu.VMEM((1728, 128), F32)],
-        compiler_params=pltpu.CompilerParams(vmem_limit_bytes=48 * 1024 * 1024),
-        cost_estimate=pl.CostEstimate(flops=100_000_000, bytes_accessed=8_000_000, transcendentals=0),
+        [((128, 512), BF16), ((16, 384, 128), BF16), ((192, 768), BF16), ((192, 1152), BF16)],
+        [pltpu.VMEM((864, 64), F32), pltpu.VMEM((1728, 128), F32)],
+        flops=100_000_000, moved=8_000_000,
     )(pre_rows, act, weight_two, weight_three)
 
     back, part_three = call(
         lambda *refs: coarse(scale_three, *refs),
-        [((4, 64, 768), BF16), ((128, 1728), BF16)],
-        [pltpu.VMEM((6, 128, 768), BF16), pltpu.VMEM((5, 1152, 768), BF16), pltpu.VMEM((1728, 128), F32)],
+        [((4, 64, 768), BF16), ((14, 128, 128), F32)],
+        [pltpu.VMEM((6, 128, 768), BF16), pltpu.VMEM((5, 1152, 768), BF16), pltpu.VMEM((1792, 128), F32)],
         flops=2_000_000_000, moved=4_000_000,
     )(cot_rows, cot_side, from_up, from_down, from_dup, from_ddown, wide_three, pooled)
 
-    cot_two, part_two = call(
+    cot_two, parts = call(
         fine,
-        [((6, 18, 64, 128), BF16), ((64, 864), BF16)],
-        [pltpu.VMEM((4, 10, 64, 128), F32), pltpu.VMEM((864, 64), F32)],
+        [((6, 18, 64, 128), BF16), ((128, 24, 128), BF16)],
+        [pltpu.VMEM((4, 10, 64, 128), F32), pltpu.VMEM((944, 64), F32), pltpu.VMEM((128, 24, 128), F32)],
         flops=2_000_000_000, moved=6_000_000,
-    )(back, pre_rows, pre_side, from_up, from_down, from_dup, from_ddown, acts)
+    )(back, pre_rows, pre_side, from_up, from_down, from_dup, from_ddown, acts, part_three)
 
     grad_input, = call(
         lambda *refs: into(scale_two, *refs),
@@ -326,29 +373,20 @@
         flops=4_000_000_000, moved=6_000_000,
     )(cot_two, wide_two)
 
-    shard_two = moment_two.shape[0]
-    shard_three = moment_three.shape[0]
-    parts = jnp.concatenate([part_two.reshape(devices, shard_two), part_three], axis=1)
     parts = lax.all_to_all(parts, AXES, 0, 0, tiled=True)
-    own = jnp.sum(parts.astype(F32), axis=0)
-    own_two = own[:shard_two] * (scale_two / volumes)
-    own_three = own[shard_two:] * (scale_three / volumes)
-    send = jnp.concatenate([own_two, own_three, moment_two, moment_three]).astype(BF16)
-    send = jnp.broadcast_to(send[None], (devices, send.shape[0]))
-    full = lax.all_to_all(send, AXES, 0, 0, tiled=True).astype(F32)
-    shard = shard_two + shard_three
-    grad_two = full[:, :shard_two]
-    grad_three = full[:, shard_two:shard]
-    all_two = full[:, shard : shard + shard_two]
-    all_three = full[:, shard + shard_two :]
-    trust_two = TRUST * norms[0] / (jnp.sqrt(jnp.sum(grad_two * grad_two)) + EPSILON)
-    trust_three = TRUST * norms[1] / (jnp.sqrt(jnp.sum(grad_three * grad_three)) + EPSILON)
-    new_moment_two = MOMENTUM * moment_two + LEARN * trust_two * own_two
-    new_moment_three = MOMENTUM * moment_three + LEARN * trust_three * own_three
-    full_two = MOMENTUM * all_two + LEARN * trust_two * grad_two
-    full_three = MOMENTUM * all_three + LEARN * trust_three * grad_three
-    new_weight_two = weight_two - full_two.reshape(weight_two.shape)
-    new_weight_three = weight_three - full_three.reshape(weight_three.shape)
+    send, own = call(
+        lambda *refs: reduce(scale_two / volumes, scale_three / volumes, *refs),
+        [((128, 40, 128), BF16), ((24, 128), F32)],
+        [pltpu.VMEM((40, 128), F32)],
+        moved=2_000_000,
+    )(parts, moment_two, moment_three)
+    full = lax.all_to_all(send, AXES, 0, 0, tiled=True)
+    new_weight_two, new_weight_three, new_moment_two, new_moment_three = call(
+        update,
+        [(weight_two.shape, F32), (weight_three.shape, F32), (moment_two.shape, F32), (moment_three.shape, F32)],
+        [pltpu.VMEM((128, 18, 128), F32)],
+        moved=4_000_000,
+    )(full, own, weight_two, weight_three, moment_two, moment_three)
     return (grad_input[None], new_weight_two, new_weight_three, new_moment_two, new_moment_three)
 
 

time: 124 us -> 95.2 us (0.77)
  blocking collectives: 0 us -> 28.1 us
  other arithmetic: 17.4 us -> 0 us
  local copies, waits for them, and re-layouts: 22.9 us -> 6.33 us
  starting transfers between devices: 31.4 us -> 17.7 us
  waiting for transfers between devices: 32.2 us -> 22.2 us
  Pallas kernels: 15.8 us -> 19.7 us
  between operations: 3.69 us -> 0.78 us
    all_to_all x0 -> x1, blocking collectives: none -> 28.1 us  [local(): parts = lax.all_to_all(parts, AXES, 0, 0, tiled=True)]
    all_to_all x2 -> x1, starting transfers between devices: 17.6 us -> 4.45 us  [local(): full = lax.all_to_all(send, AXES, 0, 0, tiled=True)]
    all_to_all x2 -> x1, waiting for transfers between devices: 29.2 us -> 17.6 us  [local(): full = lax.all_to_all(send, AXES, 0, 0, tiled=True)]
    unnamed x27 -> x16, local copies, waits for them, and re-layouts: 16.6 us -> 6.33 us
    broadcast_in_dim x1 -> x0, other arithmetic: 9 us -> none  [local(): send = jnp.broadcast_to(send[None], (devices, send.shape[0]))]
    all_to_all x2 -> x0, local copies, waits for them, and re-layouts: 4.13 us -> none  [the longest x1 3.62 us: local(): full = lax.all_to_all(send, AXES, 0, 0, tiled=True).astype(F32)]
    pallas_call x2 -> x4, Pallas kernels: 5.54 us -> 9.33 us  [the longest x1 4.3 us: local(): call(fine, [((6, 18, 64, 128), BF16), ((128, 24, 128), BF16)], [pltpu.VME...]
    reduce_sum x3 -> x0, other arithmetic: 2.67 us -> none  [the longest x1 1.19 us: local(): own = jnp.sum(parts.astype(F32), axis=0)]
  transfers between devices with their start and end apart: 8 -> 7, of which waited for: 3 -> 2; matrix products, arithmetic and copies ran while one was open for 2% -> 2% of each run, Pallas kernels for 8% -> 10%
where the time goes in v1:
time: 95.2 us; the launch traced here: 94.8 us
  blocking collectives  28.1 us (30%)
  waiting for transfers between devices  22.2 us (23%)
  Pallas kernels  19.7 us (21%)
  starting transfers between devices  17.7 us (19%)
  local copies, waits for them, and re-layouts  6.33 us (7%)
    all_to_all x1, blocking collectives, local(): parts = lax.all_to_all(parts, AXES, 0, 0, tiled=True)  28.1 us
    all_to_all x1, waiting for transfers between devices, local(): full = lax.all_to_all(send, AXES, 0, 0, tiled=True)  17.6 us
    unnamed x16, local copies, waits for them, and re-layouts  6.33 us
    pallas_call x1, Pallas kernels, local(): call(lambda *refs: coarse(scale_three, *refs), [((4, 64, 768), BF16), ((1...  5.39 us
    ppermute x1, waiting for transfers between devices, local(): from_ddown = lax.ppermute(send_dup, pair, cross_lower)  4.56 us
    all_to_all x1, starting transfers between devices, local(): full = lax.all_to_all(send, AXES, 0, 0, tiled=True)  4.45 us
    pallas_call x1, Pallas kernels, local(): call(fine, [((6, 18, 64, 128), BF16), ((128, 24, 128), BF16)], [pltpu.VME...  4.3 us
    ppermute x1, starting transfers between devices, local(): from_dup = lax.ppermute(send_ddown, pair, cross_raise)  3.8 us
  transfers between devices with their start and end apart: 7, of which 2 were waited for; matrix products, arithmetic and copies ran while one was open for 2% of the time, Pallas kernels for 10%

profile of v1, /device:TPU:1, one launch (start us, length us, event | category | flops | bytes accessed | tf_op | source)
XLA Modules:
  0.0 94.8 jit_solution(12811305235010288526)
XLA Ops:
  0.6 0.0 copy-start
  0.6 1.2 %copy-done = bf16[1,64,4,16,128]{4,3,2,1,0:T(8,128)(2,1)S(1)} copy-done((bf16[1,64,4,16,128]{4,3,2,1,0:T(8,128)(2,1)S(1)}, bf16[1,64,4,16,128]{4,3,2,1,0:T(8,128)(2,1)}, u32[]{:S(2)}) %copy-start) | copy-done | bytes 1048600
  1.9 0.9 %copy-done.3 = bf16[1,128,2,512]{3,2,1,0:T(2,128)(2,1)S(1)} copy-done((bf16[1,128,2,512]{3,2,1,0:T(2,128)(2,1)S(1)}, bf16[1,128,2,512]{3,2,1,0:T(2,128)(2,1)}, u32[]{:S(2)}) %copy-start.3) | copy-done | bytes 262168
  2.8 2.0 %shard_map.110 = (bf16[2,128,512]{2,1,0:T(8,128)(2,1)}, bf16[4,16,64,128]{3,2,1,0:T(8,128)(2,1)S(1)}, bf16[512,128]{1,0:T(8,128)(2,1)}, bf16[512,128]{1,0:T(8,12...) custom-call(bf16[128,2,512]{2,1,0:T(2,128)(2,1)S(1)} %bitcast.6, ...), custom_call_target="tpu_custom_call" | custom-call | bytes 4000000 | tf_op jit(solution)/shard_map/pallas_call | solution.py:328
  4.8 2.1 %collective-permute-start = (bf16[2,128,512]{2,1,0:T(8,128)(2,1)}, bf16[2,128,512]{2,1,0:T(8,128)(2,1)}, u32[]{:S(2)}, u32[]{:S(2)}) collective-permute-start(bf16[2,128,512]{2,1,0:T(8,128)(2,1)} %get-tuple-element.26.refs_0_), channel_id=1, source_target_pairs={{0,8},{8,0},{1,9},{9,1},{2,10},{10,2},{3,11},{11,3},{4,12},{12,4},... | collective-permute-start | bytes 786440 | tf_op jit(solution)/shard_map/ppermute | solution.py:341
  7.0 3.8 %collective-permute-start.3 = (bf16[320,128]{1,0:T(8,128)(2,1)S(1)}, bf16[320,128]{1,0:T(8,128)(2,1)S(1)}, u32[]{:S(2)}, u32[]{:S(2)}) collective-permute-start(bf16[320,128]{1,0:T(8,128)(2,1)S(1)} %get-tuple-element.29), channel_id=1, source_target_pairs={{0,9},{1,10},{2,11},{3,12},{4,13},{5,14},{6,15},{8,1},{9,2},{10,3}... | collective-permute-start | bytes 245768 | tf_op jit(solution)/shard_map/ppermute | solution.py:345
  10.8 3.3 %collective-permute-start.1 = (bf16[512,128]{1,0:T(8,128)(2,1)}, bf16[512,128]{1,0:T(8,128)(2,1)S(1)}, u32[]{:S(2)}, u32[]{:S(2)}) collective-permute-start(bf16[512,128]{1,0:T(8,128)(2,1)} %get-tuple-element.27), channel_id=1, source_target_pairs={{0,1},{1,2},{2,3},{3,4},{4,5},{5,6},{6,7},{8,9},{9,10},{10,11},{11... | collective-permute-start | bytes 393224 | tf_op jit(solution)/shard_map/ppermute | solution.py:343
  14.1 1.3 %collective-permute-start.2 = (bf16[512,128]{1,0:T(8,128)(2,1)}, bf16[512,128]{1,0:T(8,128)(2,1)}, u32[]{:S(2)}, u32[]{:S(2)}) collective-permute-start(bf16[512,128]{1,0:T(8,128)(2,1)} %get-tuple-element.28), channel_id=1, source_target_pairs={{1,0},{2,1},{3,2},{4,3},{5,4},{6,5},{7,6},{9,8},{10,9},{11,10},{12... | collective-permute-start | bytes 393224 | tf_op jit(solution)/shard_map/ppermute | solution.py:342
  15.4 1.3 %collective-permute-start.4 = (bf16[320,128]{1,0:T(8,128)(2,1)}, bf16[320,128]{1,0:T(8,128)(2,1)}, u32[]{:S(2)}, u32[]{:S(2)}) collective-permute-start(bf16[320,128]{1,0:T(8,128)(2,1)} %get-tuple-element.30), channel_id=1, source_target_pairs={{1,8},{2,9},{3,10},{4,11},{5,12},{6,13},{7,14},{9,0},{10,1},{11,2}... | collective-permute-start | bytes 245768 | tf_op jit(solution)/shard_map/ppermute | solution.py:344
  16.7 0.0 collective-permute-done.3.refs_4_.dup_ref
  16.7 1.4 %collective-permute-start.5 = (bf16[16,64,128]{2,1,0:T(8,128)(2,1)S(1)}, bf16[16,64,128]{2,1,0:T(8,128)(2,1)}, u32[]{:S(2)}, u32[]{:S(2)}) collective-permute-start(bf16[16,64,128]{2,1,0:T(8,128)(2,1)S(1)} %get-tuple-element.35), channel_id=1, source_target_pairs={{0,8},{8,0},{1,9},{9,1},{2,10},{10,2},{3,11},{11,3},{4,12},{12,4},... | collective-permute-start | bytes 786440 | tf_op jit(solution)/shard_map/ppermute | solution.py:346
  18.1 1.5 %copy.12.w3_ref = f32[128,1728]{1,0:T(8,128)S(1)} copy(f32[128,1728]{0,1:T(8,128)} %param.11) | data formatting | bytes 1769472 | tf_op args[4]
  19.6 1.3 %shard_map.111 = (bf16[128,512]{1,0:T(8,128)(2,1)S(1)}, bf16[16,384,128]{2,1,0:T(8,128)(2,1)S(1)}, bf16[192,768]{1,0:T(8,128)(2,1)S(1)}, bf16[192,1152]{1,0:T(8,128)(2,1)S(1)}) custom-call(bf16[4,16,64,128]{3,2,1,0:T(8,128)(2,1)S(1)} %get-tuple-element.31.pre_ref, bf16[32,4,16,128]{3,2,1,0:T(8,128)(2,1)S(1)} %bitcast.5, f32[64,864]{1,0:T(8,128)S(1)} %copy-done.1, ...), custom_call_target="tpu_custom_call" | custom-call | flops 100000000 | bytes 8000000 | tf_op jit(solution)/shard_map/pallas_call | solution.py:348
  20.9 4.6 %collective-permute-done.4.refs_5_.ddown_ref = bf16[320,128]{1,0:T(8,128)(2,1)} collective-permute-done((bf16[320,128]{1,0:T(8,128)(2,1)}, bf16[320,128]{1,0:T(8,128)(2,1)}, u32[]{:S(2)}, u32[]{:S(2)}) %collective-permute-start.4) | collective-permute-done | bytes 81952 | tf_op jit(solution)/shard_map/ppermute | solution.py:344
  25.4 0.0 collective-permute-done.1.refs_2_.up_ref
  25.4 0.0 collective-permute-done.2.refs_3_.down_ref
  25.4 0.0 collective-permute-done.refs_1_
  25.5 5.4 %shard_map.112 = (bf16[4,64,768]{2,1,0:T(8,128)(2,1)S(1)}, f32[14,128,128]{2,1,0:T(8,128)S(1)}) custom-call(bf16[2,128,512]{2,1,0:T(8,128)(2,1)} %get-tuple-element.26.refs_0_, bf16[2,128,512]{2,1,0:T(8,128)(2,1)} %collective-permute-done.refs_1_, bf16[512,128]{1,0:T(8,128)(2,1)S(1)} %collective-permute-done.1.refs_2_.up_ref, ...), custom_call_target="tpu_custom_call" | custom-call | flops 2000000000 | bytes 4000000 | tf_op jit(solution)/shard_map/pallas_call | solution.py:355
  30.9 0.0 collective-permute-done.5.side_ref
  30.9 4.3 %shard_map.113 = (bf16[6,18,64,128]{3,2,1,0:T(8,128)(2,1)}, bf16[128,24,128]{2,1,0:T(8,128)(2,1)S(1)}) custom-call(bf16[4,64,768]{2,1,0:T(8,128)(2,1)S(1)} %get-tuple-element.34.back_ref, bf16[4,16,64,128]{3,2,1,0:T(8,128)(2,1)S(1)} %get-tuple-element.31.pre_ref, bf16[16,64,128]{2,1,0:T(8,128)(2,1)} %collective-permute-done.5.side_ref, ...), custom_call_target="tpu_custom_call" | custom-call | flops 2000000000 | bytes 6000000 | tf_op jit(solution)/shard_map/pallas_call | solution.py:362
  35.2 0.0 copy-start.4
  35.2 0.0 copy-start.5
  35.2 28.1 %all_to_all.10.refs_0_ = bf16[128,24,128]{2,1,0:T(8,128)(2,1)S(1)} all-to-all(bf16[128,24,128]{2,1,0:T(8,128)(2,1)S(1)} %get-tuple-element.40), channel_id=1, replica_groups=mesh['dp'=8,'depth'=2,'height'=8] {'dp','depth','height'}, dimensions={0} | all-to-all | bytes 1572864 | tf_op jit(solution)/shard_map/all_to_all | solution.py:376
  63.3 0.0 copy-done.5
  63.3 1.3 %shard_map.115 = (bf16[128,40,128]{2,1,0:T(8,128)(2,1)}, f32[24,128]{1,0:T(8,128)S(1)}) custom-call(bf16[128,24,128]{2,1,0:T(8,128)(2,1)S(1)} %all_to_all.10.refs_0_, f32[432]{0:T(512)S(1)} %copy-done.5, f32[1728]{0:T(1024)S(1)} %copy-done.4), custom_call_target="tpu_custom_call" | custom-call | bytes 2000000 | tf_op jit(solution)/shard_map/pallas_call | solution.py:377
  64.6 4.5 %all-to-all-start.1 = ((bf16[128,40,128]{2,1,0:T(8,128)(2,1)}), bf16[128,40,128]{2,1,0:T(8,128)(2,1)S(1)}, u32[]{:S(2)}, u32[]{:S(2)}) async-start(bf16[128,40,128]{2,1,0:T(8,128)(2,1)} %get-tuple-element.41), calls=%async_computation.1 | async-start | bytes 2621440 | tf_op jit(solution)/shard_map/all_to_all | solution.py:383
  69.0 0.0 copy-start.6
  69.0 1.5 %copy-done.6 = bf16[6,18,64,128]{3,2,1,0:T(8,128)(2,1)S(1)} copy-done((bf16[6,18,64,128]{3,2,1,0:T(8,128)(2,1)S(1)}, bf16[6,18,64,128]{3,2,1,0:T(8,128)(2,1)}, u32[]{:S(2)}) %copy-start.6) | copy-done | bytes 1769496
  70.5 3.0 %shard_map.114 = bf16[32,4,16,128]{3,2,1,0:T(8,128)(2,1)} custom-call(bf16[6,18,64,128]{3,2,1,0:T(8,128)(2,1)S(1)} %copy-done.6, bf16[192,768]{1,0:T(8,128)(2,1)S(1)} %get-tuple-element.39.refs_1_), custom_call_target="tpu_custom_call" | custom-call | flops 4000000000 | bytes 6000000 | tf_op jit(solution)/shard_map/pallas_call | solution.py:369
  73.5 17.6 %all-to-all-done.1.full_ref = bf16[128,40,128]{2,1,0:T(8,128)(2,1)S(1)} async-done(((bf16[128,40,128]{2,1,0:T(8,128)(2,1)}), bf16[128,40,128]{2,1,0:T(8,128)(2,1)S(1)}, u32[]{:S(2)}, u32[]{:S(2)}) %all-to-all-start.1) | async-done | bytes 1310752 | tf_op jit(solution)/shard_map/all_to_all | solution.py:383
  91.1 2.4 %shard_map.116 = (f32[64,864]{1,0:T(8,128)}, f32[128,1728]{1,0:T(8,128)S(1)}, f32[432]{0:T(512)}, f32[1728]{0:T(1024)}) custom-call(bf16[128,40,128]{2,1,0:T(8,128)(2,1)S(1)} %all-to-all-done.1.full_ref, f32[24,128]{1,0:T(8,128)S(1)} %get-tuple-element.42.own_ref, f32[64,864]{1,0:T(8,128)S(1)} %copy-done.1, f32[128,1728]{1,0:T(8,128)S(1)} %copy.12.w3_ref, ...), custom_call_target="tpu_custom_call" | custom-call | bytes 4000000 | tf_op jit(solution)/shard_map/pallas_call | solution.py:384
  93.5 1.2 %copy.14 = f32[128,1728]{0,1:T(8,128)} copy(f32[128,1728]{1,0:T(8,128)S(1)} %get-tuple-element.49) | data formatting | bytes 1769472
  (6 shorter events, 0.0 us)
Async XLA Ops:
  0.6 1.2 %copy-start = (bf16[1,64,4,16,128]{4,3,2,1,0:T(8,128)(2,1)S(1)}, bf16[1,64,4,16,128]{4,3,2,1,0:T(8,128)(2,1)}, u32[]{:S(2)}) copy-start(bf16[1,64,4,16,128]{4,3,2,1,0:T(8,128)(2,1)} %param.8) | copy-start | bytes 3145732
  1.9 0.9 %copy-start.3 = (bf16[1,128,2,512]{3,2,1,0:T(2,128)(2,1)S(1)}, bf16[1,128,2,512]{3,2,1,0:T(2,128)(2,1)}, u32[]{:S(2)}) copy-start(bf16[1,128,2,512]{3,2,1,0:T(2,128)(2,1)} %param.9) | copy-start | bytes 786436
  2.8 16.7 %copy-start.1 = (f32[64,864]{1,0:T(8,128)S(1)}, f32[64,864]{1,0:T(8,128)}, u32[]{:S(2)}) copy-start(f32[64,864]{1,0:T(8,128)} %w2_ref.3) | copy-start | bytes 663556
  2.8 16.8 %copy-start.2 = (bf16[1,32,4,16,128]{4,3,2,1,0:T(8,128)(2,1)S(1)}, bf16[1,32,4,16,128]{4,3,2,1,0:T(8,128)(2,1)}, u32[]{:S(2)}) copy-start(bf16[1,32,4,16,128]{4,3,2,1,0:T(8,128)(2,1)} %param.7) | copy-start | bytes 1572868
  4.8 20.6 %collective-permute-start = (bf16[2,128,512]{2,1,0:T(8,128)(2,1)}, bf16[2,128,512]{2,1,0:T(8,128)(2,1)}, u32[]{:S(2)}, u32[]{:S(2)}) collective-permute-start(bf16[2,128,512]{2,1,0:T(8,128)(2,1)} %get-tuple-element.26.refs_0_), channel_id=1, source_target_pairs={{0,8},{8,0},{1,9},{9,1},{2,10},{10,2},{3,11},{11,3},{4,12},{12,4},... | collective-permute-start | bytes 786440 | tf_op jit(solution)/shard_map/ppermute | solution.py:341
  7.0 9.7 %collective-permute-start.3 = (bf16[320,128]{1,0:T(8,128)(2,1)S(1)}, bf16[320,128]{1,0:T(8,128)(2,1)S(1)}, u32[]{:S(2)}, u32[]{:S(2)}) collective-permute-start(bf16[320,128]{1,0:T(8,128)(2,1)S(1)} %get-tuple-element.29), channel_id=1, source_target_pairs={{0,9},{1,10},{2,11},{3,12},{4,13},{5,14},{6,15},{8,1},{9,2},{10,3}... | collective-permute-start | bytes 245768 | tf_op jit(solution)/shard_map/ppermute | solution.py:345
  10.8 14.7 %collective-permute-start.1 = (bf16[512,128]{1,0:T(8,128)(2,1)}, bf16[512,128]{1,0:T(8,128)(2,1)S(1)}, u32[]{:S(2)}, u32[]{:S(2)}) collective-permute-start(bf16[512,128]{1,0:T(8,128)(2,1)} %get-tuple-element.27), channel_id=1, source_target_pairs={{0,1},{1,2},{2,3},{3,4},{4,5},{5,6},{6,7},{8,9},{9,10},{10,11},{11... | collective-permute-start | bytes 393224 | tf_op jit(solution)/shard_map/ppermute | solution.py:343
  14.1 11.4 %collective-permute-start.2 = (bf16[512,128]{1,0:T(8,128)(2,1)}, bf16[512,128]{1,0:T(8,128)(2,1)}, u32[]{:S(2)}, u32[]{:S(2)}) collective-permute-start(bf16[512,128]{1,0:T(8,128)(2,1)} %get-tuple-element.28), channel_id=1, source_target_pairs={{1,0},{2,1},{3,2},{4,3},{5,4},{6,5},{7,6},{9,8},{10,9},{11,10},{12... | collective-permute-start | bytes 393224 | tf_op jit(solution)/shard_map/ppermute | solution.py:342
  15.4 10.0 %collective-permute-start.4 = (bf16[320,128]{1,0:T(8,128)(2,1)}, bf16[320,128]{1,0:T(8,128)(2,1)}, u32[]{:S(2)}, u32[]{:S(2)}) collective-permute-start(bf16[320,128]{1,0:T(8,128)(2,1)} %get-tuple-element.30), channel_id=1, source_target_pairs={{1,8},{2,9},{3,10},{4,11},{5,12},{6,13},{7,14},{9,0},{10,1},{11,2}... | collective-permute-start | bytes 245768 | tf_op jit(solution)/shard_map/ppermute | solution.py:344
  16.7 14.2 %collective-permute-start.5 = (bf16[16,64,128]{2,1,0:T(8,128)(2,1)S(1)}, bf16[16,64,128]{2,1,0:T(8,128)(2,1)}, u32[]{:S(2)}, u32[]{:S(2)}) collective-permute-start(bf16[16,64,128]{2,1,0:T(8,128)(2,1)S(1)} %get-tuple-element.35), channel_id=1, source_target_pairs={{0,8},{8,0},{1,9},{9,1},{2,10},{10,2},{3,11},{11,3},{4,12},{12,4},... | collective-permute-start | bytes 786440 | tf_op jit(solution)/shard_map/ppermute | solution.py:346
  35.2 28.1 %copy-start.4 = (f32[1728]{0:T(1024)S(1)}, f32[1728]{0:T(1024)}, u32[]{:S(2)}) copy-start(f32[1728]{0:T(1024)} %m3_ref.1) | copy-start | bytes 20740
  35.2 28.1 %copy-start.5 = (f32[432]{0:T(512)S(1)}, f32[432]{0:T(512)}, u32[]{:S(2)}) copy-start(f32[432]{0:T(512)} %m2_ref.1) | copy-start | bytes 5188
  64.6 26.5 %all-to-all-start.1 = ((bf16[128,40,128]{2,1,0:T(8,128)(2,1)}), bf16[128,40,128]{2,1,0:T(8,128)(2,1)S(1)}, u32[]{:S(2)}, u32[]{:S(2)}) async-start(bf16[128,40,128]{2,1,0:T(8,128)(2,1)} %get-tuple-element.41), calls=%async_computation.1 | async-start | bytes 2621440 | tf_op jit(solution)/shard_map/all_to_all | solution.py:383
  69.0 1.5 %copy-start.6 = (bf16[6,18,64,128]{3,2,1,0:T(8,128)(2,1)S(1)}, bf16[6,18,64,128]{3,2,1,0:T(8,128)(2,1)}, u32[]{:S(2)}) copy-start(bf16[6,18,64,128]{3,2,1,0:T(8,128)(2,1)} %get-tuple-element.38.refs_0_) | copy-start | bytes 5308420

commit v2 on v1

v2 whole, which is shorter than its diff:
```python
import jax
import jax.numpy as jnp
from jax import lax
from jax.experimental import pallas as pl
from jax.experimental.pallas import tpu as pltpu
from jax.sharding import PartitionSpec as P

SLOPE = 0.3
LEARN = 4.0
TRUST = 0.05
MOMENTUM = 0.9
EPSILON = 1e-06
AXES = ("dp", "depth", "height")
F32 = jnp.float32
BF16 = jnp.bfloat16


def call(body, outs, scratch=(), flops=0, moved=0):
    return pl.pallas_call(
        body,
        out_shape=[jax.ShapeDtypeStruct(shape, dtype) for shape, dtype in outs],
        scratch_shapes=list(scratch),
        compiler_params=pltpu.CompilerParams(vmem_limit_bytes=48 * 1024 * 1024),
        cost_estimate=pl.CostEstimate(flops=flops, bytes_accessed=moved, transcendentals=0),
    )


def dot_nt(a, b):
    return lax.dot_general(a, b, (((1,), (1,)), ((), ())), preferred_element_type=F32)


def dot_nn(a, b):
    return lax.dot_general(a, b, (((1,), (0,)), ((), ())), preferred_element_type=F32)


def shifted(x, amount):
    size = x.shape[-1]
    amount = amount % size
    if amount == 0:
        return x
    return jnp.concatenate([x[..., amount:], x[..., :amount]], axis=-1)


def arrange(cot_ref, pre_ref, act_ref, cot_out, pre_out, side_out, a_out, b_out, diag_a_out, diag_b_out):
    dep = lax.axis_index("depth")
    odd = lax.rem(lax.axis_index("height"), 2) == 1
    cots = [cot_ref[:, d, :] for d in range(2)]
    for d in range(2):
        cot_out[d] = cots[d]
        top, bottom = cots[d][:, :128], cots[d][:, 384:]
        a_out[128 * d : 128 * d + 128] = jnp.where(odd, top, bottom)
        b_out[128 * d : 128 * d + 128] = jnp.where(odd, bottom, top)
    near = jnp.where(dep == 0, cots[1], cots[0])
    diag_a_out[...] = jnp.where(odd, near[:, :128], near[:, 384:])
    diag_b_out[...] = jnp.where(odd, near[:, 384:], near[:, :128])
    for t in range(4):
        side_out[128 * t : 128 * t + 128] = near[:, 128 * t : 128 * t + 128]
    layer = jnp.swapaxes(act_ref[:, 3 * (1 - dep)].astype(F32), 0, 1).astype(BF16)
    side_out[512:] = layer.reshape(512, 128)
    for d in range(4):
        rows = jnp.swapaxes(pre_ref[:, d].astype(F32), 0, 1).astype(BF16)
        pre_out[d] = rows
        place = slice(256 + 64 * d, 320 + 64 * d)
        a_out[place] = jnp.where(odd, rows[0], rows[15])
        b_out[place] = jnp.where(odd, rows[15], rows[0])


def shifts(rows):
    lane = lax.broadcasted_iota(jnp.int32, rows.shape, rows.ndim - 1)
    before = jnp.where(lane < 127, shifted(rows, 1), 0.0)
    after = jnp.where(lane > 0, shifted(rows, -1), 0.0)
    return before, rows, after


def prepare(pre_ref, act_ref, w2_ref, w3_ref, pooled_out, act_out, w2_out, w3_out, t2, t3):
    row = lax.broadcasted_iota(jnp.int32, (256, 128), 0)
    col = lax.broadcasted_iota(jnp.int32, (256, 128), 1)
    pool = jnp.where(row // 2 == col, 0.125, 0.0).astype(BF16)
    for d in range(2):
        for t in range(4):
            halves = []
            for half in range(2):
                total = None
                for i in range(2):
                    for j in range(2):
                        x = pre_ref[2 * d + i, 4 * t + 2 * half + j].astype(F32)
                        x = jnp.where(x > 0, x, SLOPE * x)
                        total = x if total is None else total + x
                halves.append(total)
            total = jnp.concatenate(halves, axis=1)
            high = total.astype(BF16)
            low = (total - high.astype(F32)).astype(BF16)
            mean = dot_nn(high, pool) + dot_nn(low, pool)
            pooled_out[64 * d : 64 * d + 64, 128 * t : 128 * t + 128] = mean.astype(BF16)
    for d in range(4):
        rows = jnp.swapaxes(act_ref[:, d].astype(F32), 0, 1)
        for ow, value in enumerate(shifts(rows)):
            start = 96 * d + 32 * ow
            act_out[:, start : start + 32, :] = value.astype(BF16)
    t2[...] = jnp.transpose(w2_ref[...])
    t3[...] = jnp.transpose(w3_ref[...])
    for kd in range(3):
        for oh in range(3):
            for ow in range(3):
                k = kd * 9 + (2 - oh) * 3 + (2 - ow)
                block = t3[pl.ds(k, 64, stride=27), :].astype(BF16)
                tap = oh * 3 + ow
                w3_out[64 * kd : 64 * kd + 64, 128 * tap : 128 * tap + 128] = block
    zero = jnp.zeros((32, 64), F32)
    for kd in range(3):
        for ow in range(3):
            taps = []
            for oh in range(3):
                k = kd * 9 + (2 - oh) * 3 + (2 - ow)
                taps.append(t2[pl.ds(k, 32, stride=27), :])
            for r in range(2):
                blocks = taps + [zero] if r == 0 else [zero] + taps
                start = 64 * kd + 32 * r
                w2_out[start : start + 32, 256 * ow : 256 * ow + 256] = jnp.concatenate(blocks, axis=1).astype(BF16)


def coarse(scale, own_ref, side_ref, a_ref, b_ref, da_ref, db_ref, w3_ref, pooled_ref,
           back_out, grad_out, s_buf, back, parts, t3):
    dep = lax.axis_index("depth")
    hgt = lax.axis_index("height")
    odd = lax.rem(hgt, 2) == 1

    def slice_of(rows, a, b):
        return jnp.concatenate([jnp.where(odd, a, b)] + rows + [jnp.where(odd, b, a)], axis=1)

    column = lax.broadcasted_iota(jnp.int32, (128, 768), 1) % 64

    def taps(n, x):
        for ow in range(3):
            if ow == 0:
                moved = jnp.where(column > 0, shifted(x, -1), jnp.zeros_like(x))
            elif ow == 1:
                moved = x
            else:
                moved = jnp.where(column < 63, shifted(x, 1), jnp.zeros_like(x))
            for oh in range(3):
                tap = oh * 3 + ow
                s_buf[n, 128 * tap : 128 * tap + 128, :] = shifted(moved, (oh - 1) * 64)

    for z in range(2):
        rows = slice(128 * z, 128 * z + 128)
        taps(z, slice_of([own_ref[z]], a_ref[rows], b_ref[rows]))
    taps(2, slice_of([side_ref[128 * t : 128 * t + 128] for t in range(4)], da_ref[...], db_ref[...]))
    y0 = dot_nn(w3_ref[64:192, :], s_buf[0])
    y1 = dot_nn(w3_ref[0:128, :], s_buf[1])
    back[0] = y0[:64] + y1[:64]
    back[1] = y0[64:] + y1[64:]
    kd = pl.multiple_of(128 * dep, 128)
    back[1 - dep] += dot_nn(w3_ref[pl.ds(kd, 64), :], s_buf[2])
    lane = lax.broadcasted_iota(jnp.int32, (64, 768), 1)
    keep = ((lane >= 128) | (hgt > 0)) & ((lane < 640) | (hgt < 7))
    for d in range(2):
        back_out[d] = jnp.where(keep, scale * back[d], 0.0).astype(BF16)
    r0 = dot_nt(pooled_ref[...], s_buf[0, :, 128:640])
    r1 = dot_nt(pooled_ref[...], s_buf[1, :, 128:640])
    parts[0] = r0[64:]
    parts[1] = r0[:64] + r1[64:]
    parts[2] = r1[:64]
    d = pl.multiple_of(64 * (1 - dep), 64)
    parts[2 * (1 - dep)] += dot_nt(pooled_ref[pl.ds(d, 64), :], s_buf[2, :, 128:640])
    for od in range(3):
        for oh in range(3):
            for ow in range(3):
                k = (2 - od) * 9 + (2 - oh) * 3 + (2 - ow)
                tap = oh * 3 + ow
                t3[pl.ds(k, 64, stride=27), :] = parts[od, :, 128 * tap : 128 * tap + 128]
    t3[1728:] = jnp.zeros((64, 128), F32)
    for b in range(14):
        grad_out[b] = jnp.transpose(t3[128 * b : 128 * b + 128, :])


def fine(back_ref, pre_ref, a_ref, b_ref, act_ref, side_ref, three_ref,
         z_out, parts_out, upper, near, parts, t2, stage):
    dep = lax.axis_index("depth")
    odd = lax.rem(lax.axis_index("height"), 2) == 1
    row = lax.broadcasted_iota(jnp.int32, (128, 256), 0)
    col = lax.broadcasted_iota(jnp.int32, (128, 256), 1)
    spread = jnp.where(row == col // 2, 0.125, 0.0).astype(BF16)
    for t in range(6):
        x = back_ref[:, :, 128 * t : 128 * t + 128].reshape(128, 128)
        y = dot_nn(x, spread).reshape(2, 64, 256)
        if t > 0:
            upper[:, 2 * t - 1] = y[:, :, :128]
        if t < 5:
            upper[:, 2 * t] = y[:, :, 128:]
    for f in range(4):
        place = slice(256 + 64 * f, 320 + 64 * f)
        for h in range(18):
            if h == 0:
                pre = jnp.where(odd, a_ref[place], b_ref[place])
            elif h == 17:
                pre = jnp.where(odd, b_ref[place], a_ref[place])
            else:
                pre = pre_ref[f, h - 1]
            up = upper[f // 2, (h + 1) // 2]
            z_out[f, h] = jnp.where(pre.astype(F32) > 0, up, SLOPE * up).astype(BF16)
    layer = side_ref[512:].astype(F32).reshape(16, 32, 128)
    for ow, value in enumerate(shifts(layer)):
        near[:, 32 * ow : 32 * ow + 32, :] = value.astype(BF16)

    def correlate(z, lhs):
        total = None
        for h in range(4):
            left = jnp.concatenate([lhs(h + 4 * i) for i in range(4)], axis=1)
            right = jnp.concatenate(
                [z_out[z, h + 4 * i : h + 4 * i + 3].reshape(192, 128) for i in range(4)], axis=1
            )
            r = dot_nt(left, right)
            total = r if total is None else total + r
        return total

    sums = [None, None, None]
    for z in range(4):
        first, final = max(0, z - 1), min(3, z + 1)
        total = correlate(z, lambda h: act_ref[h, 96 * first : 96 * (final + 1), :])
        for d in range(first, final + 1):
            part = total[96 * (d - first) : 96 * (d - first + 1)]
            od = z - d + 1
            sums[od] = part if sums[od] is None else sums[od] + part
    for od in range(3):
        parts[od] = sums[od]
    parts[2 * dep] += correlate(3 * (1 - dep), lambda h: near[h])
    for od in range(3):
        for oh in range(3):
            for ow in range(3):
                k = (2 - od) * 9 + (2 - oh) * 3 + (2 - ow)
                t2[pl.ds(k, 32, stride=27), :] = parts[od, 32 * ow : 32 * ow + 32, 64 * oh : 64 * oh + 64]
    t2[864:] = jnp.zeros((80, 64), F32)
    tail = lax.broadcasted_iota(jnp.int32, (64, 128), 1) < 48
    for half in range(2):
        for b in range(4):
            start = 432 * half + 128 * b
            block = jnp.transpose(t2[start : start + 128, :])
            if b == 3:
                block = jnp.where(tail, block, 0.0)
            stage[pl.ds(half, 64, stride=2), b, :] = block
    for b in range(14):
        stage[:, 4 + b, :] = three_ref[b]
    stage[:, 18:, :] = jnp.zeros((128, 6, 128), F32)
    parts_out[...] = stage[...].astype(BF16)


def into(z_ref, w2_ref, rows, ship):
    dep = lax.axis_index("depth")
    lane = lax.broadcasted_iota(jnp.int32, (256, 128), 1)
    for jp in range(4):
        acc = [None] * 6
        for z in range(4):
            blocks = []
            for j in (2 * jp, 2 * jp + 1):
                x = z_ref[z, 2 * j : 2 * j + 4].reshape(256, 128)
                left = jnp.where(lane > 0, shifted(x, -1), jnp.zeros_like(x))
                right = jnp.where(lane < 127, shifted(x, 1), jnp.zeros_like(x))
                blocks.append(jnp.concatenate([left, x, right], axis=0))
            y = dot_nn(w2_ref[...], jnp.concatenate(blocks, axis=1))
            for kd in range(3):
                d = z + kd
                part = y[64 * kd : 64 * kd + 64]
                acc[d] = part if acc[d] is None else acc[d] + part
        for j in range(2):
            for r in range(2):
                h = 4 * jp + 2 * j + r
                block = (slice(32 * r, 32 * r + 32), slice(128 * j, 128 * j + 128))
                ship[h] = jnp.where(dep == 0, acc[5][block], acc[0][block])
                for d in range(4):
                    rows[d, h] = acc[d + 1][block]


def finish(scale, rows_ref, ship_ref, out_ref):
    dep = lax.axis_index("depth")
    for d in range(4):
        rows = rows_ref[d]
        if d in (0, 3):
            rows = rows + jnp.where(dep == (0 if d == 3 else 1), ship_ref[...], 0.0)
        out_ref[:, d] = (scale * jnp.swapaxes(rows, 0, 1)).astype(BF16)


def reduce(scale_two, scale_three, parts_ref, m2_ref, m3_ref, send_out, own_out, rows):
    total = jnp.sum(parts_ref[...].astype(F32), axis=0)
    row = lax.broadcasted_iota(jnp.int32, (24, 128), 0)
    total = total * jnp.where(row < 4, scale_two, scale_three)
    own_out[...] = total
    rows[...] = jnp.zeros((40, 128), F32)
    rows[:18] = total[:18]
    for b in range(3):
        rows[18 + b, :] = m2_ref[pl.ds(128 * b, 128)]
    rows[21, :48] = m2_ref[pl.ds(384, 48)]
    for b in range(13):
        rows[22 + b, :] = m3_ref[pl.ds(128 * b, 128)]
    rows[35, :64] = m3_ref[pl.ds(1664, 64)]
    send_out[...] = jnp.broadcast_to(rows[...].astype(BF16)[None], (128, 40, 128))


def update(full_ref, own_ref, w2_ref, w3_ref, m2_ref, m3_ref, w2_out, w3_out, m2_out, m3_out, stage):
    w2 = w2_ref[...]
    w3 = w3_ref[...]
    grad = full_ref[:, :18, :].astype(F32)
    square = jnp.sum(grad * grad, axis=0)
    row = lax.broadcasted_iota(jnp.int32, (18, 128), 0)
    norm_two = jnp.sqrt(jnp.sum(jnp.where(row < 4, square, 0.0), keepdims=True))
    norm_three = jnp.sqrt(jnp.sum(jnp.where(row < 4, 0.0, square), keepdims=True))
    rate_two = LEARN * (TRUST * jnp.sqrt(jnp.sum(w2 * w2, keepdims=True)) / (norm_two + EPSILON))
    rate_three = LEARN * (TRUST * jnp.sqrt(jnp.sum(w3 * w3, keepdims=True)) / (norm_three + EPSILON))
    rate = jnp.where(row < 4, rate_two, rate_three)
    stage[...] = MOMENTUM * full_ref[:, 18:36, :].astype(F32) + rate[None] * grad
    for b in range(13):
        cols = slice(128 * b, 128 * b + 128)
        w3_out[:, cols] = w3[:, cols] - stage[:, 4 + b, :]
    w3_out[:, 1664:] = w3[:, 1664:] - stage[:, 17, :64]
    halves = []
    for half in range(2):
        blocks = [stage[pl.ds(half, 64, stride=2), b, :] for b in range(4)]
        halves.append(jnp.concatenate(blocks, axis=1)[:, :432])
    w2_out[...] = w2 - jnp.concatenate(halves, axis=1)
    own = rate * own_ref[:18]
    for b in range(3):
        m2_out[pl.ds(128 * b, 128)] = MOMENTUM * m2_ref[pl.ds(128 * b, 128)] + own[b]
    m2_out[pl.ds(384, 48)] = MOMENTUM * m2_ref[pl.ds(384, 48)] + own[3, :48]
    for b in range(13):
        m3_out[pl.ds(128 * b, 128)] = MOMENTUM * m3_ref[pl.ds(128 * b, 128)] + own[4 + b]
    m3_out[pl.ds(1664, 64)] = MOMENTUM * m3_ref[pl.ds(1664, 64)] + own[17, :64]


def local(act_one, pre_two, cot_three, weight_two, weight_three, moment_two, moment_three):
    scale_two = (act_one.shape[1] * 27) ** (-0.5)
    scale_three = (pre_two.shape[1] * 27) ** (-0.5)
    volumes = lax.axis_size("dp")
    pre, act, cot = pre_two[0], act_one[0], cot_three[0]

    cot_rows, pre_rows, send_side, send_a, send_b, send_da, send_db = call(
        arrange,
        [((2, 128, 512), BF16), ((4, 16, 64, 128), BF16), ((1024, 128), BF16), ((512, 128), BF16),
         ((512, 128), BF16), ((128, 128), BF16), ((128, 128), BF16)],
        moved=4_000_000,
    )(cot, pre, act)
    tall = lax.axis_size("height")
    swap = [(0, 1), (1, 0)]
    pairs_a = [(h, h ^ 1) for h in range(tall)]
    pairs_b = [(h, ((h + 1) ^ 1) - 1) for h in range(1, tall - 1)]
    cross_a, cross_b = (
        [(d * tall + i, (1 - d) * tall + j) for d in range(2) for i, j in pairs] for pairs in (pairs_a, pairs_b)
    )
    side = lax.ppermute(send_side, "depth", swap)
    got_a = lax.ppermute(send_a, "height", pairs_a)
    got_b = lax.ppermute(send_b, "height", pairs_b)
    got_da = lax.ppermute(send_da, ("depth", "height"), cross_a)
    got_db = lax.ppermute(send_db, ("depth", "height"), cross_b)

    pooled, acts, wide_two, wide_three = call(
        prepare,
        [((128, 512), BF16), ((16, 384, 128), BF16), ((192, 768), BF16), ((192, 1152), BF16)],
        [pltpu.VMEM((864, 64), F32), pltpu.VMEM((1728, 128), F32)],
        flops=100_000_000, moved=8_000_000,
    )(pre_rows, act, weight_two, weight_three)

    back, part_three = call(
        lambda *refs: coarse(scale_three, *refs),
        [((2, 64, 768), BF16), ((14, 128, 128), F32)],
        [pltpu.VMEM((3, 1152, 768), BF16), pltpu.VMEM((2, 64, 768), F32), pltpu.VMEM((3, 64, 1152), F32),
         pltpu.VMEM((1792, 128), F32)],
        flops=2_000_000_000, moved=4_000_000,
    )(cot_rows, side, got_a, got_b, got_da, got_db, wide_three, pooled)

    cot_two, parts = call(
        fine,
        [((4, 18, 64, 128), BF16), ((128, 24, 128), BF16)],
        [pltpu.VMEM((2, 10, 64, 128), F32), pltpu.VMEM((16, 96, 128), BF16), pltpu.VMEM((3, 96, 192), F32),
         pltpu.VMEM((944, 64), F32), pltpu.VMEM((128, 24, 128), F32)],
        flops=2_000_000_000, moved=6_000_000,
    )(back, pre_rows, got_a, got_b, acts, side, part_three)

    into_rows, ship = call(
        into,
        [((4, 16, 32, 128), F32), ((16, 32, 128), F32)],
        flops=4_000_000_000, moved=6_000_000,
    )(cot_two, wide_two)
    ship = lax.ppermute(ship, "depth", swap)
    grad_input, = call(
        lambda *refs: finish(scale_two, *refs),
        [((32, 4, 16, 128), BF16)],
        moved=2_000_000,
    )(into_rows, ship)

    parts = lax.all_to_all(parts, AXES, 0, 0, tiled=True)
    send, own = call(
        lambda *refs: reduce(scale_two / volumes, scale_three / volumes, *refs),
        [((128, 40, 128), BF16), ((24, 128), F32)],
        [pltpu.VMEM((40, 128), F32)],
        moved=2_000_000,
    )(parts, moment_two, moment_three)
    full = lax.all_to_all(send, AXES, 0, 0, tiled=True)
    new_weight_two, new_weight_three, new_moment_two, new_moment_three = call(
        update,
        [(weight_two.shape, F32), (weight_three.shape, F32), (moment_two.shape, F32), (moment_three.shape, F32)],
        [pltpu.VMEM((128, 18, 128), F32)],
        moved=4_000_000,
    )(full, own, weight_two, weight_three, moment_two, moment_three)
    return (grad_input[None], new_weight_two, new_weight_three, new_moment_two, new_moment_three)


def solution(mesh):
    in_specs = (
        P("dp", None, "depth", "height", None),
        P("dp", None, "depth", "height", None),
        P("dp", None, "depth", "height"),
        P(),
        P(),
        P(AXES),
        P(AXES),
    )
    out_specs = (
        P("dp", None, "depth", "height", None),
        P(),
        P(),
        P(AXES),
        P(AXES),
    )
    return jax.shard_map(local, mesh=mesh, in_specs=in_specs, out_specs=out_specs, check_vma=False)
```

time: 95.2 us -> 89.8 us (0.943)
  waiting for transfers between devices: 22.2 us -> 16.9 us
  Pallas kernels: 19.7 us -> 17.3 us
  local copies, waits for them, and re-layouts: 6.33 us -> 7.88 us
  blocking collectives: 28.1 us -> 29.5 us
    all_to_all x1, waiting for transfers between devices: 17.6 us -> 0.01 us  [local(): full = lax.all_to_all(send, AXES, 0, 0, tiled=True)]
    ppermute x6, waiting for transfers between devices: 4.57 us -> 16.9 us  [the longest x1 16.9 us: local(): ship = lax.ppermute(ship, 'depth', swap)]
    pallas_call x4 -> x5, Pallas kernels: 14.7 us -> 12.2 us  [the longest x1 3.7 us: local(): call(lambda *refs: coarse(scale_three, *refs), [((2, 64, 768), BF16), ((1...]
    unnamed x16 -> x24, local copies, waits for them, and re-layouts: 6.33 us -> 7.88 us
    all_to_all x1, blocking collectives: 28.1 us -> 29.5 us  [local(): parts = lax.all_to_all(parts, AXES, 0, 0, tiled=True)]
  transfers between devices with their start and end apart: 7 -> 7, of which waited for: 2 -> 1; matrix products, arithmetic and copies ran while one was open for 2% -> 2% of each run, Pallas kernels for 10% -> 4%
where the time goes in v2:
time: 89.8 us; the launch traced here: 89.3 us
  blocking collectives  29.5 us (33%)
  Pallas kernels  17.3 us (19%)
  starting transfers between devices  16.9 us (19%)
  waiting for transfers between devices  16.9 us (19%)
  local copies, waits for them, and re-layouts  7.88 us (9%)
    all_to_all x1, blocking collectives, local(): parts = lax.all_to_all(parts, AXES, 0, 0, tiled=True)  29.5 us
    ppermute x1, waiting for transfers between devices, local(): ship = lax.ppermute(ship, 'depth', swap)  16.9 us
    unnamed x24, local copies, waits for them, and re-layouts  7.88 us
    all_to_all x1, starting transfers between devices, local(): full = lax.all_to_all(send, AXES, 0, 0, tiled=True)  4.45 us
    ppermute x1, starting transfers between devices, local(): got_da = lax.ppermute(send_da, ('depth', 'height'), cross_a)  4.28 us
    pallas_call x1, Pallas kernels, local(): call(lambda *refs: coarse(scale_three, *refs), [((2, 64, 768), BF16), ((1...  3.7 us
    pallas_call x1, Pallas kernels, local(): call(fine, [((4, 18, 64, 128), BF16), ((128, 24, 128), BF16)], [pltpu.VME...  3.69 us
    ppermute x1, starting transfers between devices, local(): got_a = lax.ppermute(send_a, 'height', pairs_a)  2.62 us
  transfers between devices with their start and end apart: 7, of which 1 were waited for; matrix products, arithmetic and copies ran while one was open for 2% of the time, Pallas kernels for 4%

profile of v2, /device:TPU:1, one launch (start us, length us, event | category | flops | bytes accessed | tf_op | source)
XLA Modules:
  0.0 89.3 jit_solution(11414109932963738764)
XLA Ops:
  0.6 0.0 copy-start
  0.6 1.0 %copy-done = bf16[1,32,4,16,128]{4,3,2,1,0:T(8,128)(2,1)S(1)} copy-done((bf16[1,32,4,16,128]{4,3,2,1,0:T(8,128)(2,1)S(1)}, bf16[1,32,4,16,128]{4,3,2,1,0:T(8,128)(2,1)}, u32[]{:S(2)}) %copy-start) | copy-done | bytes 524312
  1.7 1.2 %copy-done.2 = bf16[1,64,4,16,128]{4,3,2,1,0:T(8,128)(2,1)S(1)} copy-done((bf16[1,64,4,16,128]{4,3,2,1,0:T(8,128)(2,1)S(1)}, bf16[1,64,4,16,128]{4,3,2,1,0:T(8,128)(2,1)}, u32[]{:S(2)}) %copy-start.2) | copy-done | bytes 1048600
  2.9 0.9 %copy-done.4 = bf16[1,128,2,512]{3,2,1,0:T(2,128)(2,1)S(1)} copy-done((bf16[1,128,2,512]{3,2,1,0:T(2,128)(2,1)S(1)}, bf16[1,128,2,512]{3,2,1,0:T(2,128)(2,1)}, u32[]{:S(2)}) %copy-start.4) | copy-done | bytes 262168
  3.9 2.3 %shard_map.110 = (bf16[2,128,512]{2,1,0:T(8,128)(2,1)S(1)}, bf16[4,16,64,128]{3,2,1,0:T(8,128)(2,1)S(1)}, bf16[1024,128]{1,0:T(8,128)(2,1)}, bf16[512,128]{1,0:T...) custom-call(bf16[128,2,512]{2,1,0:T(2,128)(2,1)S(1)} %bitcast.7, ...), custom_call_target="tpu_custom_call" | custom-call | bytes 4000000 | tf_op jit(solution)/shard_map/pallas_call | solution.py:335
  6.1 0.0 copy-start.7
  6.2 0.7 copy-done.7
  6.9 2.1 %collective-permute-start = (bf16[1024,128]{1,0:T(8,128)(2,1)}, bf16[1024,128]{1,0:T(8,128)(2,1)S(1)}, u32[]{:S(2)}, u32[]{:S(2)}) collective-permute-start(bf16[1024,128]{1,0:T(8,128)(2,1)} %get-tuple-element.29), channel_id=1, source_target_pairs={{0,8},{8,0},{1,9},{9,1},{2,10},{10,2},{3,11},{11,3},{4,12},{12,4},... | collective-permute-start | bytes 786440 | tf_op jit(solution)/shard_map/ppermute | solution.py:348
  9.0 2.6 %collective-permute-start.1 = (bf16[512,128]{1,0:T(8,128)(2,1)}, bf16[512,128]{1,0:T(8,128)(2,1)S(1)}, u32[]{:S(2)}, u32[]{:S(2)}) collective-permute-start(bf16[512,128]{1,0:T(8,128)(2,1)} %get-tuple-element.30), channel_id=1, source_target_pairs={{0,1},{1,0},{2,3},{3,2},{4,5},{5,4},{6,7},{7,6},{8,9},{9,8},{10,11... | collective-permute-start | bytes 393224 | tf_op jit(solution)/shard_map/ppermute | solution.py:349
  11.6 1.3 %collective-permute-start.2 = (bf16[512,128]{1,0:T(8,128)(2,1)}, bf16[512,128]{1,0:T(8,128)(2,1)}, u32[]{:S(2)}, u32[]{:S(2)}) collective-permute-start(bf16[512,128]{1,0:T(8,128)(2,1)} %get-tuple-element.31), channel_id=1, source_target_pairs={{1,2},{2,1},{3,4},{4,3},{5,6},{6,5},{9,10},{10,9},{11,12},{12,11},... | collective-permute-start | bytes 393224 | tf_op jit(solution)/shard_map/ppermute | solution.py:350
  12.9 4.3 %collective-permute-start.3 = (bf16[128,128]{1,0:T(8,128)(2,1)S(1)}, bf16[128,128]{1,0:T(8,128)(2,1)S(1)}, u32[]{:S(2)}, u32[]{:S(2)}) collective-permute-start(bf16[128,128]{1,0:T(8,128)(2,1)S(1)} %get-tuple-element.32), channel_id=1, source_target_pairs={{0,9},{1,8},{2,11},{3,10},{4,13},{5,12},{6,15},{7,14},{8,1},{9,0},... | collective-permute-start | bytes 98312 | tf_op jit(solution)/shard_map/ppermute | solution.py:351
  17.2 0.7 collective-permute-start.4
  17.8 1.5 %copy.12.w3_ref = f32[128,1728]{1,0:T(8,128)S(1)} copy(f32[128,1728]{0,1:T(8,128)} %param.11) | data formatting | bytes 1769472 | tf_op args[4]
  19.3 0.0 copy-start.8
  19.4 1.3 %shard_map.111 = (bf16[128,512]{1,0:T(8,128)(2,1)S(1)}, bf16[16,384,128]{2,1,0:T(8,128)(2,1)S(1)}, bf16[192,768]{1,0:T(8,128)(2,1)S(1)}, bf16[192,1152]{1,0:T(8,128)(2,1)S(1)}) custom-call(bf16[4,16,64,128]{3,2,1,0:T(8,128)(2,1)S(1)} %get-tuple-element.34.pre_ref, bf16[32,4,16,128]{3,2,1,0:T(8,128)(2,1)S(1)} %bitcast.5, f32[64,864]{1,0:T(8,128)S(1)} %copy-done.3, ...), custom_call_target="tpu_custom_call" | custom-call | flops 100000000 | bytes 8000000 | tf_op jit(solution)/shard_map/pallas_call | solution.py:354
  20.7 0.0 collective-permute-done.3.refs_4_
  20.7 0.0 collective-permute-done.4.refs_5_
  20.7 0.0 collective-permute-done.refs_1_.side_ref
  20.7 3.7 %shard_map.112 = (bf16[2,64,768]{2,1,0:T(8,128)(2,1)S(1)}, f32[14,128,128]{2,1,0:T(8,128)S(1)}) custom-call(bf16[2,128,512]{2,1,0:T(8,128)(2,1)S(1)} %copy-done.8, bf16[1024,128]{1,0:T(8,128)(2,1)S(1)} %collective-permute-done.refs_1_.side_ref, bf16[512,128]{1,0:T(8,128)(2,1)S(1)} %collective-permute-done.1.refs_2_.a_ref, ...), custom_call_target="tpu_custom_call" | custom-call | flops 2000000000 | bytes 4000000 | tf_op jit(solution)/shard_map/pallas_call | solution.py:361
  24.4 3.7 %shard_map.113 = (bf16[4,18,64,128]{3,2,1,0:T(8,128)(2,1)S(1)}, bf16[128,24,128]{2,1,0:T(8,128)(2,1)S(1)}) custom-call(bf16[2,64,768]{2,1,0:T(8,128)(2,1)S(1)} %get-tuple-element.37.back_ref, bf16[4,16,64,128]{3,2,1,0:T(8,128)(2,1)S(1)} %get-tuple-element.34.pre_ref, bf16[512,128]{1,0:T(8,128)(2,1)S(1)} %collective-permute-done.1.refs_2_.a_ref, ...), custom_call_target="tpu_custom_call" | custom-call | flops 2000000000 | bytes 6000000 | tf_op jit(solution)/shard_map/pallas_call | solution.py:369
  28.1 0.0 copy-start.5
  28.2 0.0 copy-start.6
  28.2 29.5 %all_to_all.10.refs_0_ = bf16[128,24,128]{2,1,0:T(8,128)(2,1)S(1)} all-to-all(bf16[128,24,128]{2,1,0:T(8,128)(2,1)S(1)} %get-tuple-element.44), channel_id=1, replica_groups=mesh['dp'=8,'depth'=2,'height'=8] {'dp','depth','height'}, dimensions={0} | all-to-all | bytes 1572864 | tf_op jit(solution)/shard_map/all_to_all | solution.py:389
  57.6 1.3 %shard_map.116 = (bf16[128,40,128]{2,1,0:T(8,128)(2,1)}, f32[24,128]{1,0:T(8,128)S(1)}) custom-call(bf16[128,24,128]{2,1,0:T(8,128)(2,1)S(1)} %all_to_all.10.refs_0_, f32[432]{0:T(512)S(1)} %copy-done.6, f32[1728]{0:T(1024)S(1)} %copy-done.5), custom_call_target="tpu_custom_call" | custom-call | bytes 2000000 | tf_op jit(solution)/shard_map/pallas_call | solution.py:390
  58.9 4.5 %all-to-all-start.1 = ((bf16[128,40,128]{2,1,0:T(8,128)(2,1)}), bf16[128,40,128]{2,1,0:T(8,128)(2,1)S(1)}, u32[]{:S(2)}, u32[]{:S(2)}) async-start(bf16[128,40,128]{2,1,0:T(8,128)(2,1)} %get-tuple-element.45), calls=%async_computation.1 | async-start | bytes 2621440 | tf_op jit(solution)/shard_map/all_to_all | solution.py:396
  63.4 1.3 %copy-done.10 = bf16[4,18,64,128]{3,2,1,0:T(8,128)(2,1)S(1)} copy-done((bf16[4,18,64,128]{3,2,1,0:T(8,128)(2,1)S(1)}, bf16[4,18,64,128]{3,2,1,0:T(8,128)(2,1)}, u32[]{:S(2)}) %copy-start.10) | copy-done | bytes 1179672
  64.7 1.5 %shard_map.114 = (f32[4,16,32,128]{3,2,1,0:T(8,128)S(1)}, f32[16,32,128]{2,1,0:T(8,128)S(1)}) custom-call(bf16[4,18,64,128]{3,2,1,0:T(8,128)(2,1)S(1)} %copy-done.10, bf16[192,768]{1,0:T(8,128)(2,1)S(1)} %get-tuple-element.41.w2_ref), custom_call_target="tpu_custom_call" | custom-call | flops 4000000000 | bytes 6000000 | tf_op jit(solution)/shard_map/pallas_call | solution.py:377
  66.2 1.5 %collective-permute-start.5 = (f32[16,32,128]{2,1,0:T(8,128)S(1)}, f32[16,32,128]{2,1,0:T(8,128)S(1)}, u32[]{:S(2)}, u32[]{:S(2)}) collective-permute-start(f32[16,32,128]{2,1,0:T(8,128)S(1)} %get-tuple-element.43), channel_id=1, source_target_pairs={{0,8},{8,0},{1,9},{9,1},{2,10},{10,2},{3,11},{11,3},{4,12},{12,4},... | collective-permute-start | bytes 786440 | tf_op jit(solution)/shard_map/ppermute | solution.py:382
  67.6 16.9 %collective-permute-done.5.refs_1_ = f32[16,32,128]{2,1,0:T(8,128)S(1)} collective-permute-done((f32[16,32,128]{2,1,0:T(8,128)S(1)}, f32[16,32,128]{2,1,0:T(8,128)S(1)}, u32[]{:S(2)}, u32[]{:S(2)}) %collective-permute-start.5) | collective-permute-done | bytes 262176 | tf_op jit(solution)/shard_map/ppermute | solution.py:382
  84.5 1.1 %shard_map.115 = bf16[32,4,16,128]{3,2,1,0:T(8,128)(2,1)} custom-call(f32[4,16,32,128]{3,2,1,0:T(8,128)S(1)} %get-tuple-element.42.refs_0_, f32[16,32,128]{2,1,0:T(8,128)S(1)} %collective-permute-done.5.refs_1_), custom_call_target="tpu_custom_call" | custom-call | bytes 2000000 | tf_op jit(solution)/shard_map/pallas_call | solution.py:383
  85.6 2.4 %shard_map.117 = (f32[64,864]{1,0:T(8,128)}, f32[128,1728]{1,0:T(8,128)S(1)}, f32[432]{0:T(512)}, f32[1728]{0:T(1024)}) custom-call(bf16[128,40,128]{2,1,0:T(8,128)(2,1)S(1)} %all-to-all-done.1.full_ref, f32[24,128]{1,0:T(8,128)S(1)} %get-tuple-element.46.own_ref, f32[64,864]{1,0:T(8,128)S(1)} %copy-done.3, f32[128,1728]{1,0:T(8,128)S(1)} %copy.12.w3_ref, ...), custom_call_target="tpu_custom_call" | custom-call | bytes 4000000 | tf_op jit(solution)/shard_map/pallas_call | solution.py:397
  88.0 1.2 %copy.14 = f32[128,1728]{0,1:T(8,128)} copy(f32[128,1728]{1,0:T(8,128)S(1)} %get-tuple-element.53) | data formatting | bytes 1769472
  (15 shorter events, 0.0 us)
Async XLA Ops:
  0.6 1.0 %copy-start = (bf16[1,32,4,16,128]{4,3,2,1,0:T(8,128)(2,1)S(1)}, bf16[1,32,4,16,128]{4,3,2,1,0:T(8,128)(2,1)}, u32[]{:S(2)}) copy-start(bf16[1,32,4,16,128]{4,3,2,1,0:T(8,128)(2,1)} %param.7) | copy-start | bytes 1572868
  1.7 1.2 %copy-start.2 = (bf16[1,64,4,16,128]{4,3,2,1,0:T(8,128)(2,1)S(1)}, bf16[1,64,4,16,128]{4,3,2,1,0:T(8,128)(2,1)}, u32[]{:S(2)}) copy-start(bf16[1,64,4,16,128]{4,3,2,1,0:T(8,128)(2,1)} %param.8) | copy-start | bytes 3145732
  2.9 0.9 %copy-start.4 = (bf16[1,128,2,512]{3,2,1,0:T(2,128)(2,1)S(1)}, bf16[1,128,2,512]{3,2,1,0:T(2,128)(2,1)}, u32[]{:S(2)}) copy-start(bf16[1,128,2,512]{3,2,1,0:T(2,128)(2,1)} %param.9) | copy-start | bytes 786436
  6.1 0.7 copy-start.7
  6.8 12.5 %copy-start.1 = (bf16[1,32,4,16,128]{4,3,2,1,0:T(8,128)(2,1)S(1)}, bf16[1,32,4,16,128]{4,3,2,1,0:T(8,128)(2,1)}, u32[]{:S(2)}) copy-start(bf16[1,32,4,16,128]{4,3,2,1,0:T(8,128)(2,1)} %param.7) | copy-start | bytes 1572868
  6.9 12.5 %copy-start.3 = (f32[64,864]{1,0:T(8,128)S(1)}, f32[64,864]{1,0:T(8,128)}, u32[]{:S(2)}) copy-start(f32[64,864]{1,0:T(8,128)} %w2_ref.3) | copy-start | bytes 663556
  6.9 13.9 %collective-permute-start = (bf16[1024,128]{1,0:T(8,128)(2,1)}, bf16[1024,128]{1,0:T(8,128)(2,1)S(1)}, u32[]{:S(2)}, u32[]{:S(2)}) collective-permute-start(bf16[1024,128]{1,0:T(8,128)(2,1)} %get-tuple-element.29), channel_id=1, source_target_pairs={{0,8},{8,0},{1,9},{9,1},{2,10},{10,2},{3,11},{11,3},{4,12},{12,4},... | collective-permute-start | bytes 786440 | tf_op jit(solution)/shard_map/ppermute | solution.py:348
  9.0 11.7 %collective-permute-start.1 = (bf16[512,128]{1,0:T(8,128)(2,1)}, bf16[512,128]{1,0:T(8,128)(2,1)S(1)}, u32[]{:S(2)}, u32[]{:S(2)}) collective-permute-start(bf16[512,128]{1,0:T(8,128)(2,1)} %get-tuple-element.30), channel_id=1, source_target_pairs={{0,1},{1,0},{2,3},{3,2},{4,5},{5,4},{6,7},{7,6},{8,9},{9,8},{10,11... | collective-permute-start | bytes 393224 | tf_op jit(solution)/shard_map/ppermute | solution.py:349
  11.6 9.1 %collective-permute-start.2 = (bf16[512,128]{1,0:T(8,128)(2,1)}, bf16[512,128]{1,0:T(8,128)(2,1)}, u32[]{:S(2)}, u32[]{:S(2)}) collective-permute-start(bf16[512,128]{1,0:T(8,128)(2,1)} %get-tuple-element.31), channel_id=1, source_target_pairs={{1,2},{2,1},{3,4},{4,3},{5,6},{6,5},{9,10},{10,9},{11,12},{12,11},... | collective-permute-start | bytes 393224 | tf_op jit(solution)/shard_map/ppermute | solution.py:350
  12.9 7.8 %collective-permute-start.3 = (bf16[128,128]{1,0:T(8,128)(2,1)S(1)}, bf16[128,128]{1,0:T(8,128)(2,1)S(1)}, u32[]{:S(2)}, u32[]{:S(2)}) collective-permute-start(bf16[128,128]{1,0:T(8,128)(2,1)S(1)} %get-tuple-element.32), channel_id=1, source_target_pairs={{0,9},{1,8},{2,11},{3,10},{4,13},{5,12},{6,15},{7,14},{8,1},{9,0},... | collective-permute-start | bytes 98312 | tf_op jit(solution)/shard_map/ppermute | solution.py:351
  17.2 3.5 %collective-permute-start.4 = (bf16[128,128]{1,0:T(8,128)(2,1)S(1)}, bf16[128,128]{1,0:T(8,128)(2,1)S(1)}, u32[]{:S(2)}, u32[]{:S(2)}) collective-permute-start(bf16[128,128]{1,0:T(8,128)(2,1)S(1)} %get-tuple-element.33), channel_id=1, source_target_pairs={{1,10},{2,9},{3,12},{4,11},{5,14},{6,13},{9,2},{10,1},{11,4},{12,3... | collective-permute-start | bytes 98312 | tf_op jit(solution)/shard_map/ppermute | solution.py:352
  19.3 1.4 %copy-start.8 = (bf16[2,128,512]{2,1,0:T(8,128)(2,1)S(1)}, bf16[2,128,512]{2,1,0:T(8,128)(2,1)}, u32[]{:S(2)}) copy-start(bf16[2,128,512]{2,1,0:T(8,128)(2,1)} %copy-done.7) | copy-start | bytes 786436
  28.1 30.8 %copy-start.9 = (bf16[4,18,64,128]{3,2,1,0:T(8,128)(2,1)}, bf16[4,18,64,128]{3,2,1,0:T(8,128)(2,1)S(1)}, u32[]{:S(2)}) copy-start(bf16[4,18,64,128]{3,2,1,0:T(8,128)(2,1)S(1)} %get-tuple-element.40.z_ref) | copy-start | bytes 3538948
  28.1 29.5 %copy-start.5 = (f32[1728]{0:T(1024)S(1)}, f32[1728]{0:T(1024)}, u32[]{:S(2)}) copy-start(f32[1728]{0:T(1024)} %m3_ref.1) | copy-start | bytes 20740
  28.2 29.5 %copy-start.6 = (f32[432]{0:T(512)S(1)}, f32[432]{0:T(512)}, u32[]{:S(2)}) copy-start(f32[432]{0:T(512)} %m2_ref.1) | copy-start | bytes 5188
  58.9 26.7 %all-to-all-start.1 = ((bf16[128,40,128]{2,1,0:T(8,128)(2,1)}), bf16[128,40,128]{2,1,0:T(8,128)(2,1)S(1)}, u32[]{:S(2)}, u32[]{:S(2)}) async-start(bf16[128,40,128]{2,1,0:T(8,128)(2,1)} %get-tuple-element.45), calls=%async_computation.1 | async-start | bytes 2621440 | tf_op jit(solution)/shard_map/all_to_all | solution.py:396
  63.4 1.3 %copy-start.10 = (bf16[4,18,64,128]{3,2,1,0:T(8,128)(2,1)S(1)}, bf16[4,18,64,128]{3,2,1,0:T(8,128)(2,1)}, u32[]{:S(2)}) copy-start(bf16[4,18,64,128]{3,2,1,0:T(8,128)(2,1)} %copy-done.9) | copy-start | bytes 3538948
  66.2 18.4 %collective-permute-start.5 = (f32[16,32,128]{2,1,0:T(8,128)S(1)}, f32[16,32,128]{2,1,0:T(8,128)S(1)}, u32[]{:S(2)}, u32[]{:S(2)}) collective-permute-start(f32[16,32,128]{2,1,0:T(8,128)S(1)} %get-tuple-element.43), channel_id=1, source_target_pairs={{0,8},{8,0},{1,9},{9,1},{2,10},{10,2},{3,11},{11,3},{4,12},{12,4},... | collective-permute-start | bytes 786440 | tf_op jit(solution)/shard_map/ppermute | solution.py:382

commit v3 on v2

--- a/solution.py
+++ b/solution.py
@@ -15,12 +15,12 @@
 BF16 = jnp.bfloat16
 
 
-def call(body, outs, scratch=(), flops=0, moved=0):
+def call(body, outs, scratch=(), flops=0, moved=0, limit=20):
     return pl.pallas_call(
         body,
         out_shape=[jax.ShapeDtypeStruct(shape, dtype) for shape, dtype in outs],
         scratch_shapes=list(scratch),
-        compiler_params=pltpu.CompilerParams(vmem_limit_bytes=48 * 1024 * 1024),
+        compiler_params=pltpu.CompilerParams(vmem_limit_bytes=limit * 1024 * 1024),
         cost_estimate=pl.CostEstimate(flops=flops, bytes_accessed=moved, transcendentals=0),
     )
 
@@ -41,7 +41,7 @@
     return jnp.concatenate([x[..., amount:], x[..., :amount]], axis=-1)
 
 
-def arrange(cot_ref, pre_ref, act_ref, cot_out, pre_out, side_out, a_out, b_out, diag_a_out, diag_b_out):
+def arrange(cot_ref, pre_ref, act_ref, cot_out, side_out, a_out, b_out, diag_a_out, diag_b_out):
     dep = lax.axis_index("depth")
     odd = lax.rem(lax.axis_index("height"), 2) == 1
     cots = [cot_ref[:, d, :] for d in range(2)]
@@ -58,11 +58,10 @@
     layer = jnp.swapaxes(act_ref[:, 3 * (1 - dep)].astype(F32), 0, 1).astype(BF16)
     side_out[512:] = layer.reshape(512, 128)
     for d in range(4):
-        rows = jnp.swapaxes(pre_ref[:, d].astype(F32), 0, 1).astype(BF16)
-        pre_out[d] = rows
+        first, final = pre_ref[:, d, 0, :], pre_ref[:, d, 15, :]
         place = slice(256 + 64 * d, 320 + 64 * d)
-        a_out[place] = jnp.where(odd, rows[0], rows[15])
-        b_out[place] = jnp.where(odd, rows[15], rows[0])
+        a_out[place] = jnp.where(odd, first, final)
+        b_out[place] = jnp.where(odd, final, first)
 
 
 def shifts(rows):
@@ -72,7 +71,16 @@
     return before, rows, after
 
 
-def prepare(pre_ref, act_ref, w2_ref, w3_ref, pooled_out, act_out, w2_out, w3_out, t2, t3):
+def prepare(pre_ref, act_ref, w2_ref, w3_ref, m2_ref, m3_ref, pre_out, pooled_out, act_out, w2_out, w3_out, m_out, t2):
+    for d in range(4):
+        pre_out[d] = jnp.swapaxes(pre_ref[:, d].astype(F32), 0, 1).astype(BF16)
+    m_out[...] = jnp.zeros((24, 128), F32)
+    for b in range(3):
+        m_out[b, :] = m2_ref[pl.ds(128 * b, 128)]
+    m_out[3, :48] = m2_ref[pl.ds(384, 48)]
+    for b in range(13):
+        m_out[4 + b, :] = m3_ref[pl.ds(128 * b, 128)]
+    m_out[17, :64] = m3_ref[pl.ds(1664, 64)]
     row = lax.broadcasted_iota(jnp.int32, (256, 128), 0)
     col = lax.broadcasted_iota(jnp.int32, (256, 128), 1)
     pool = jnp.where(row // 2 == col, 0.125, 0.0).astype(BF16)
@@ -83,7 +91,7 @@
                 total = None
                 for i in range(2):
                     for j in range(2):
-                        x = pre_ref[2 * d + i, 4 * t + 2 * half + j].astype(F32)
+                        x = pre_out[2 * d + i, 4 * t + 2 * half + j].astype(F32)
                         x = jnp.where(x > 0, x, SLOPE * x)
                         total = x if total is None else total + x
                 halves.append(total)
@@ -98,12 +106,11 @@
             start = 96 * d + 32 * ow
             act_out[:, start : start + 32, :] = value.astype(BF16)
     t2[...] = jnp.transpose(w2_ref[...])
-    t3[...] = jnp.transpose(w3_ref[...])
     for kd in range(3):
         for oh in range(3):
             for ow in range(3):
                 k = kd * 9 + (2 - oh) * 3 + (2 - ow)
-                block = t3[pl.ds(k, 64, stride=27), :].astype(BF16)
+                block = w3_ref[pl.ds(k, 64, stride=27), :].astype(BF16)
                 tap = oh * 3 + ow
                 w3_out[64 * kd : 64 * kd + 64, 128 * tap : 128 * tap + 128] = block
     zero = jnp.zeros((32, 64), F32)
@@ -174,9 +181,7 @@
         grad_out[b] = jnp.transpose(t3[128 * b : 128 * b + 128, :])
 
 
-def fine(back_ref, pre_ref, a_ref, b_ref, act_ref, side_ref, three_ref,
-         z_out, parts_out, upper, near, parts, t2, stage):
-    dep = lax.axis_index("depth")
+def cotangent(back_ref, a_ref, b_ref, pre_rows, upper, z_out):
     odd = lax.rem(lax.axis_index("height"), 2) == 1
     row = lax.broadcasted_iota(jnp.int32, (128, 256), 0)
     col = lax.broadcasted_iota(jnp.int32, (128, 256), 1)
@@ -190,15 +195,22 @@
             upper[:, 2 * t] = y[:, :, 128:]
     for f in range(4):
         place = slice(256 + 64 * f, 320 + 64 * f)
+        rows = pre_rows(f)
         for h in range(18):
             if h == 0:
                 pre = jnp.where(odd, a_ref[place], b_ref[place])
             elif h == 17:
                 pre = jnp.where(odd, b_ref[place], a_ref[place])
             else:
-                pre = pre_ref[f, h - 1]
+                pre = rows[h - 1]
             up = upper[f // 2, (h + 1) // 2]
             z_out[f, h] = jnp.where(pre.astype(F32) > 0, up, SLOPE * up).astype(BF16)
+
+
+def fine(back_ref, pre_ref, a_ref, b_ref, act_ref, side_ref, three_ref, m_ref,
+         parts_out, z_out, upper, near, parts, t2, stage):
+    dep = lax.axis_index("depth")
+    cotangent(back_ref, a_ref, b_ref, lambda f: pre_ref.at[f], upper, z_out)
     layer = side_ref[512:].astype(F32).reshape(16, 32, 128)
     for ow, value in enumerate(shifts(layer)):
         near[:, 32 * ow : 32 * ow + 32, :] = value.astype(BF16)
@@ -241,12 +253,13 @@
             stage[pl.ds(half, 64, stride=2), b, :] = block
     for b in range(14):
         stage[:, 4 + b, :] = three_ref[b]
-    stage[:, 18:, :] = jnp.zeros((128, 6, 128), F32)
+    stage[:, 18:, :] = jnp.broadcast_to(m_ref[:6][None], (128, 6, 128))
     parts_out[...] = stage[...].astype(BF16)
 
 
-def into(z_ref, w2_ref, rows, ship):
+def into(back_ref, pre_ref, a_ref, b_ref, w2_ref, rows, ship, z_ref, upper):
     dep = lax.axis_index("depth")
+    cotangent(back_ref, a_ref, b_ref, lambda f: jnp.swapaxes(pre_ref[:, f].astype(F32), 0, 1), upper, z_ref)
     lane = lax.broadcasted_iota(jnp.int32, (256, 128), 1)
     for jp in range(4):
         acc = [None] * 6
@@ -266,7 +279,7 @@
             for r in range(2):
                 h = 4 * jp + 2 * j + r
                 block = (slice(32 * r, 32 * r + 32), slice(128 * j, 128 * j + 128))
-                ship[h] = jnp.where(dep == 0, acc[5][block], acc[0][block])
+                ship[h] = jnp.where(dep == 0, acc[5][block], acc[0][block]).astype(BF16)
                 for d in range(4):
                     rows[d, h] = acc[d + 1][block]
 
@@ -276,27 +289,22 @@
     for d in range(4):
         rows = rows_ref[d]
         if d in (0, 3):
-            rows = rows + jnp.where(dep == (0 if d == 3 else 1), ship_ref[...], 0.0)
+            rows = rows + jnp.where(dep == (0 if d == 3 else 1), ship_ref[...].astype(F32), 0.0)
         out_ref[:, d] = (scale * jnp.swapaxes(rows, 0, 1)).astype(BF16)
 
 
-def reduce(scale_two, scale_three, parts_ref, m2_ref, m3_ref, send_out, own_out, rows):
-    total = jnp.sum(parts_ref[...].astype(F32), axis=0)
-    row = lax.broadcasted_iota(jnp.int32, (24, 128), 0)
+def reduce(scale_two, scale_three, parts_ref, m_ref, send_out, own_out, rows):
+    total = jnp.sum(parts_ref[:, :18, :].astype(F32), axis=0)
+    row = lax.broadcasted_iota(jnp.int32, (18, 128), 0)
     total = total * jnp.where(row < 4, scale_two, scale_three)
     own_out[...] = total
-    rows[...] = jnp.zeros((40, 128), F32)
-    rows[:18] = total[:18]
-    for b in range(3):
-        rows[18 + b, :] = m2_ref[pl.ds(128 * b, 128)]
-    rows[21, :48] = m2_ref[pl.ds(384, 48)]
-    for b in range(13):
-        rows[22 + b, :] = m3_ref[pl.ds(128 * b, 128)]
-    rows[35, :64] = m3_ref[pl.ds(1664, 64)]
-    send_out[...] = jnp.broadcast_to(rows[...].astype(BF16)[None], (128, 40, 128))
-
-
-def update(full_ref, own_ref, w2_ref, w3_ref, m2_ref, m3_ref, w2_out, w3_out, m2_out, m3_out, stage):
+    rows[:18] = total
+    rows[18:30] = m_ref[6:18]
+    rows[30:] = jnp.zeros((2, 128), F32)
+    send_out[...] = jnp.broadcast_to(rows[...].astype(BF16)[None], (128, 32, 128))
+
+
+def update(full_ref, first_ref, own_ref, w2_ref, w3_ref, m2_ref, m3_ref, w2_out, w3_out, m2_out, m3_out, stage):
     w2 = w2_ref[...]
     w3 = w3_ref[...]
     grad = full_ref[:, :18, :].astype(F32)
@@ -307,17 +315,19 @@
     rate_two = LEARN * (TRUST * jnp.sqrt(jnp.sum(w2 * w2, keepdims=True)) / (norm_two + EPSILON))
     rate_three = LEARN * (TRUST * jnp.sqrt(jnp.sum(w3 * w3, keepdims=True)) / (norm_three + EPSILON))
     rate = jnp.where(row < 4, rate_two, rate_three)
-    stage[...] = MOMENTUM * full_ref[:, 18:36, :].astype(F32) + rate[None] * grad
+    stage[:, :6, :] = MOMENTUM * first_ref[:, 18:, :].astype(F32)
+    stage[:, 6:, :] = MOMENTUM * full_ref[:, 18:30, :].astype(F32)
+    stage[...] += rate[None] * grad
     for b in range(13):
-        cols = slice(128 * b, 128 * b + 128)
-        w3_out[:, cols] = w3[:, cols] - stage[:, 4 + b, :]
-    w3_out[:, 1664:] = w3[:, 1664:] - stage[:, 17, :64]
+        rows = slice(128 * b, 128 * b + 128)
+        w3_out[rows] = w3[rows] - jnp.transpose(stage[:, 4 + b, :])
+    w3_out[1664:] = w3[1664:] - jnp.transpose(stage[:, 17, :])[:64]
     halves = []
     for half in range(2):
         blocks = [stage[pl.ds(half, 64, stride=2), b, :] for b in range(4)]
         halves.append(jnp.concatenate(blocks, axis=1)[:, :432])
     w2_out[...] = w2 - jnp.concatenate(halves, axis=1)
-    own = rate * own_ref[:18]
+    own = rate * own_ref[...]
     for b in range(3):
         m2_out[pl.ds(128 * b, 128)] = MOMENTUM * m2_ref[pl.ds(128 * b, 128)] + own[b]
     m2_out[pl.ds(384, 48)] = MOMENTUM * m2_ref[pl.ds(384, 48)] + own[3, :48]
@@ -332,9 +342,9 @@
     volumes = lax.axis_size("dp")
     pre, act, cot = pre_two[0], act_one[0], cot_three[0]
 
-    cot_rows, pre_rows, send_side, send_a, send_b, send_da, send_db = call(
+    cot_rows, send_side, send_a, send_b, send_da, send_db = call(
         arrange,
-        [((2, 128, 512), BF16), ((4, 16, 64, 128), BF16), ((1024, 128), BF16), ((512, 128), BF16),
+        [((2, 128, 512), BF16), ((1024, 128), BF16), ((512, 128), BF16),
          ((512, 128), BF16), ((128, 128), BF16), ((128, 128), BF16)],
         moved=4_000_000,
     )(cot, pre, act)
@@ -351,12 +361,12 @@
     got_da = lax.ppermute(send_da, ("depth", "height"), cross_a)
     got_db = lax.ppermute(send_db, ("depth", "height"), cross_b)
 
-    pooled, acts, wide_two, wide_three = call(
+    pre_rows, pooled, acts, wide_two, wide_three, moments = call(
         prepare,
-        [((128, 512), BF16), ((16, 384, 128), BF16), ((192, 768), BF16), ((192, 1152), BF16)],
-        [pltpu.VMEM((864, 64), F32), pltpu.VMEM((1728, 128), F32)],
+        [((4, 16, 64, 128), BF16), ((128, 512), BF16), ((16, 384, 128), BF16), ((192, 768), BF16), ((192, 1152), BF16), ((24, 128), F32)],
+        [pltpu.VMEM((864, 64), F32)],
         flops=100_000_000, moved=8_000_000,
-    )(pre_rows, act, weight_two, weight_three)
+    )(pre, act, weight_two, weight_three.T, moment_two, moment_three)
 
     back, part_three = call(
         lambda *refs: coarse(scale_three, *refs),
@@ -366,41 +376,44 @@
         flops=2_000_000_000, moved=4_000_000,
     )(cot_rows, side, got_a, got_b, got_da, got_db, wide_three, pooled)
 
-    cot_two, parts = call(
+    parts, = call(
         fine,
-        [((4, 18, 64, 128), BF16), ((128, 24, 128), BF16)],
-        [pltpu.VMEM((2, 10, 64, 128), F32), pltpu.VMEM((16, 96, 128), BF16), pltpu.VMEM((3, 96, 192), F32),
+        [((128, 24, 128), BF16)],
+        [pltpu.VMEM((4, 18, 64, 128), BF16), pltpu.VMEM((2, 10, 64, 128), F32), pltpu.VMEM((16, 96, 128), BF16), pltpu.VMEM((3, 96, 192), F32),
          pltpu.VMEM((944, 64), F32), pltpu.VMEM((128, 24, 128), F32)],
         flops=2_000_000_000, moved=6_000_000,
-    )(back, pre_rows, got_a, got_b, acts, side, part_three)
-
+    )(back, pre_rows, got_a, got_b, acts, side, part_three, moments)
+
+    parts = lax.all_to_all(parts, AXES, 0, 0, tiled=True)
     into_rows, ship = call(
         into,
-        [((4, 16, 32, 128), F32), ((16, 32, 128), F32)],
+        [((4, 16, 32, 128), F32), ((16, 32, 128), BF16)],
+        [pltpu.VMEM((4, 18, 64, 128), BF16), pltpu.VMEM((2, 10, 64, 128), F32)],
         flops=4_000_000_000, moved=6_000_000,
-    )(cot_two, wide_two)
+    )(back, pre, got_a, got_b, wide_two)
     ship = lax.ppermute(ship, "depth", swap)
+    parts, into_rows, ship = lax.optimization_barrier((parts, into_rows, ship))
     grad_input, = call(
         lambda *refs: finish(scale_two, *refs),
         [((32, 4, 16, 128), BF16)],
         moved=2_000_000,
     )(into_rows, ship)
 
-    parts = lax.all_to_all(parts, AXES, 0, 0, tiled=True)
     send, own = call(
         lambda *refs: reduce(scale_two / volumes, scale_three / volumes, *refs),
-        [((128, 40, 128), BF16), ((24, 128), F32)],
-        [pltpu.VMEM((40, 128), F32)],
+        [((128, 32, 128), BF16), ((18, 128), F32)],
+        [pltpu.VMEM((32, 128), F32)],
         moved=2_000_000,
-    )(parts, moment_two, moment_three)
+    )(parts, moments)
+    own, w2, w3 = lax.optimization_barrier((own, weight_two, weight_three))
     full = lax.all_to_all(send, AXES, 0, 0, tiled=True)
     new_weight_two, new_weight_three, new_moment_two, new_moment_three = call(
         update,
-        [(weight_two.shape, F32), (weight_three.shape, F32), (moment_two.shape, F32), (moment_three.shape, F32)],
+        [(weight_two.shape, F32), (weight_three.shape[::-1], F32), (moment_two.shape, F32), (moment_three.shape, F32)],
         [pltpu.VMEM((128, 18, 128), F32)],
         moved=4_000_000,
-    )(full, own, weight_two, weight_three, moment_two, moment_three)
-    return (grad_input[None], new_weight_two, new_weight_three, new_moment_two, new_moment_three)
+    )(full, parts, own, w2, w3.T, moment_two, moment_three)
+    return (grad_input[None], new_weight_two, new_weight_three.T, new_moment_two, new_moment_three)
 
 
 def solution(mesh):

time: 89.8 us -> 85.7 us (0.954)
  blocking collectives: 29.5 us -> 0 us
  starting transfers between devices: 16.9 us -> 31.5 us
  waiting for transfers between devices: 16.9 us -> 29 us
  Pallas kernels: 17.3 us -> 16.4 us
    all_to_all x1 -> x0, blocking collectives: 29.5 us -> none  [local(): parts = lax.all_to_all(parts, AXES, 0, 0, tiled=True)]
    all_to_all x1, waiting for transfers between devices: 0.01 us -> 17 us  [local(): full = lax.all_to_all(send, AXES, 0, 0, tiled=True)]
    all_to_all x0 -> x1, starting transfers between devices: none -> 13.1 us  [local(): parts = lax.all_to_all(parts, AXES, 0, 0, tiled=True)]
    ppermute x1, waiting for transfers between devices: 16.9 us -> 8.24 us  [local(): ship = lax.ppermute(ship, 'depth', swap)]
    all_to_all x0 -> x1, waiting for transfers between devices: none -> 3.73 us  [local(): parts = lax.all_to_all(parts, AXES, 0, 0, tiled=True)]
    all_to_all x1, starting transfers between devices: 4.45 us -> 5.99 us  [local(): full = lax.all_to_all(send, AXES, 0, 0, tiled=True)]
    pallas_call x1, Pallas kernels: 1.28 us -> 0.21 us  [local(): call(lambda *refs: reduce(scale_two / volumes, scale_three / volumes, *re...]
    pallas_call x5, Pallas kernels: 11.2 us -> 12.3 us  [the longest x1 3.7 us: local(): call(fine, [((128, 24, 128), BF16)], [pltpu.VMEM((4, 18, 64, 128), BF16),...]
  transfers between devices with their start and end apart: 7 -> 8, of which waited for: 1 -> 3; matrix products, arithmetic and copies ran while one was open for 2% -> 0% of each run, Pallas kernels for 4% -> 6%
where the time goes in v3:
time: 85.7 us; the launch traced here: 85.3 us
  starting transfers between devices  31.5 us (37%)
  waiting for transfers between devices  29 us (34%)
  Pallas kernels  16.4 us (19%)
  local copies, waits for them, and re-layouts  7.57 us (9%)
    all_to_all x1, waiting for transfers between devices, local(): full = lax.all_to_all(send, AXES, 0, 0, tiled=True)  17 us
    all_to_all x1, starting transfers between devices, local(): parts = lax.all_to_all(parts, AXES, 0, 0, tiled=True)  13.1 us
    ppermute x1, waiting for transfers between devices, local(): ship = lax.ppermute(ship, 'depth', swap)  8.24 us
    unnamed x26, local copies, waits for them, and re-layouts  7.57 us
    all_to_all x1, starting transfers between devices, local(): full = lax.all_to_all(send, AXES, 0, 0, tiled=True)  5.99 us
    ppermute x1, starting transfers between devices, local(): got_da = lax.ppermute(send_da, ('depth', 'height'), cross_a)  4.92 us
    all_to_all x1, waiting for transfers between devices, local(): parts = lax.all_to_all(parts, AXES, 0, 0, tiled=True)  3.73 us
    pallas_call x1, Pallas kernels, local(): call(fine, [((128, 24, 128), BF16)], [pltpu.VMEM((4, 18, 64, 128), BF16),...  3.7 us
  transfers between devices with their start and end apart: 8, of which 3 were waited for; matrix products, arithmetic and copies ran while one was open for 0% of the time, Pallas kernels for 6%

profile of v3, /device:TPU:1, one launch (start us, length us, event | category | flops | bytes accessed | tf_op | source)
XLA Modules:
  0.0 85.3 jit_solution(6033060922432824503)
XLA Ops:
  0.7 1.2 %copy-done = bf16[1,64,4,16,128]{4,3,2,1,0:T(8,128)(2,1)S(1)} copy-done((bf16[1,64,4,16,128]{4,3,2,1,0:T(8,128)(2,1)S(1)}, bf16[1,64,4,16,128]{4,3,2,1,0:T(8,128)(2,1)}, u32[]{:S(2)}) %copy-start) | copy-done | bytes 1048600
  1.9 1.0 %copy-done.4 = bf16[1,32,4,16,128]{4,3,2,1,0:T(8,128)(2,1)S(1)} copy-done((bf16[1,32,4,16,128]{4,3,2,1,0:T(8,128)(2,1)S(1)}, bf16[1,32,4,16,128]{4,3,2,1,0:T(8,128)(2,1)}, u32[]{:S(2)}) %copy-start.4) | copy-done | bytes 524312
  2.9 0.9 %copy-done.10 = bf16[1,128,2,512]{3,2,1,0:T(2,128)(2,1)S(1)} copy-done((bf16[1,128,2,512]{3,2,1,0:T(2,128)(2,1)S(1)}, bf16[1,128,2,512]{3,2,1,0:T(2,128)(2,1)}, u32[]{:S(2)}) %copy-start.10) | copy-done | bytes 262168
  3.9 2.1 %shard_map.110 = (bf16[2,128,512]{2,1,0:T(8,128)(2,1)S(1)}, bf16[1024,128]{1,0:T(8,128)(2,1)S(1)}, bf16[512,128]{1,0:T(8,128)(2,1)S(1)}, bf16[512,128]{1,0:T(8,1...) custom-call(bf16[128,2,512]{2,1,0:T(2,128)(2,1)S(1)} %bitcast.14, ...), custom_call_target="tpu_custom_call" | custom-call | bytes 4000000 | tf_op jit(solution)/shard_map/pallas_call | solution.py:345
  6.0 2.2 %collective-permute-start = (bf16[1024,128]{1,0:T(8,128)(2,1)S(1)}, bf16[1024,128]{1,0:T(8,128)(2,1)S(1)}, u32[]{:S(2)}, u32[]{:S(2)}) collective-permute-start(bf16[1024,128]{1,0:T(8,128)(2,1)S(1)} %get-tuple-element.34), channel_id=1, source_target_pairs={{0,8},{8,0},{1,9},{9,1},{2,10},{10,2},{3,11},{11,3},{4,12},{12,4},... | collective-permute-start | bytes 786440 | tf_op jit(solution)/shard_map/ppermute | solution.py:358
  8.2 2.6 %collective-permute-start.1 = (bf16[512,128]{1,0:T(8,128)(2,1)S(1)}, bf16[512,128]{1,0:T(8,128)(2,1)S(1)}, u32[]{:S(2)}, u32[]{:S(2)}) collective-permute-start(bf16[512,128]{1,0:T(8,128)(2,1)S(1)} %get-tuple-element.35), channel_id=1, source_target_pairs={{0,1},{1,0},{2,3},{3,2},{4,5},{5,4},{6,7},{7,6},{8,9},{9,8},{10,11... | collective-permute-start | bytes 393224 | tf_op jit(solution)/shard_map/ppermute | solution.py:359
  10.8 0.7 collective-permute-start.2
  11.5 4.9 %collective-permute-start.3 = (bf16[128,128]{1,0:T(8,128)(2,1)S(1)}, bf16[128,128]{1,0:T(8,128)(2,1)S(1)}, u32[]{:S(2)}, u32[]{:S(2)}) collective-permute-start(bf16[128,128]{1,0:T(8,128)(2,1)S(1)} %get-tuple-element.37), channel_id=1, source_target_pairs={{0,9},{1,8},{2,11},{3,10},{4,13},{5,12},{6,15},{7,14},{8,1},{9,0},... | collective-permute-start | bytes 98312 | tf_op jit(solution)/shard_map/ppermute | solution.py:361
  16.4 0.7 collective-permute-start.4
  17.1 0.0 copy-start.2
  17.1 1.2 %copy-done.2 = f32[128,1728]{0,1:T(8,128)S(1)} copy-done((f32[128,1728]{0,1:T(8,128)S(1)}, f32[128,1728]{0,1:T(8,128)}, u32[]{:S(2)}) %copy-start.2) | copy-done | bytes 884760
  18.3 1.6 %shard_map.111 = (bf16[4,16,64,128]{3,2,1,0:T(8,128)(2,1)S(1)}, bf16[128,512]{1,0:T(8,128)(2,1)S(1)}, bf16[16,384,128]{2,1,0:T(8,128)(2,1)S(1)}, bf16[192,768]{1...) custom-call(bf16[64,4,16,128]{3,2,1,0:T(8,128)(2,1)S(1)} %bitcast.8, ...), custom_call_target="tpu_custom_call" | custom-call | flops 100000000 | bytes 8000000 | tf_op jit(solution)/shard_map/pallas_call | solution.py:364
  19.9 0.0 collective-permute-done.3.refs_4_
  19.9 0.0 collective-permute-done.4.refs_5_
  19.9 0.0 collective-permute-done.1.refs_2_.a_ref
  19.9 0.0 collective-permute-done.2.refs_3_.b_ref
  20.0 0.0 collective-permute-done.refs_1_.side_ref
  20.0 2.8 %shard_map.112 = (bf16[2,64,768]{2,1,0:T(8,128)(2,1)S(1)}, f32[14,128,128]{2,1,0:T(8,128)S(1)}) custom-call(bf16[2,128,512]{2,1,0:T(8,128)(2,1)S(1)} %get-tuple-element.33.refs_0_, bf16[1024,128]{1,0:T(8,128)(2,1)S(1)} %collective-permute-done.refs_1_.side_ref, bf16[512,128]{1,0:T(8,128)(2,1)S(1)} %collective-permute-done.1.refs_2_.a_ref, ...), custom_call_target="tpu_custom_call" | custom-call | flops 2000000000 | bytes 4000000 | tf_op jit(solution)/shard_map/pallas_call | solution.py:371
  22.8 3.7 %shard_map.113 = bf16[128,24,128]{2,1,0:T(8,128)(2,1)} custom-call(bf16[2,64,768]{2,1,0:T(8,128)(2,1)S(1)} %get-tuple-element.41.back_ref, bf16[4,16,64,128]{3,2,1,0:T(8,128)(2,1)S(1)} %get-tuple-element.42.pre_ref, bf16[512,128]{1,0:T(8,128)(2,1)S(1)} %collective-permute-done.1.refs_2_.a_ref, bf16[512,128]{1,0:T(8,128)(2,1)S(1)} %collective-permute-done.2.refs_3_.b_ref, ...), custom_call_target="tpu_custom_call" | custom-call | flops 2000000000 | bytes 6000000 | tf_op jit(solution)/shard_map/pallas_call | solution.py:379
  26.5 13.1 %all-to-all-start = ((bf16[128,24,128]{2,1,0:T(8,128)(2,1)}), bf16[128,24,128]{2,1,0:T(8,128)(2,1)S(1)}, u32[]{:S(2)}, u32[]{:S(2)}) async-start(bf16[128,24,128]{2,1,0:T(8,128)(2,1)} %shard_map.113), calls=%async_computation | async-start | bytes 1572864 | tf_op jit(solution)/shard_map/all_to_all | solution.py:387
  39.6 2.2 %shard_map.114 = (f32[4,16,32,128]{3,2,1,0:T(8,128)S(1)}, bf16[16,32,128]{2,1,0:T(8,128)(2,1)S(1)}) custom-call(bf16[2,64,768]{2,1,0:T(8,128)(2,1)S(1)} %get-tuple-element.41.back_ref, bf16[64,4,16,128]{3,2,1,0:T(8,128)(2,1)S(1)} %bitcast.9, bf16[512,128]{1,0:T(8,128)(2,1)S(1)} %collective-permute-done.1.refs_2_.a_ref, ...), custom_call_target="tpu_custom_call" | custom-call | flops 4000000000 | bytes 6000000 | tf_op jit(solution)/shard_map/pallas_call | solution.py:388
  41.8 1.0 %copy-done.7 = f32[4,16,32,128]{3,2,1,0:T(8,128)} copy-done((f32[4,16,32,128]{3,2,1,0:T(8,128)}, f32[4,16,32,128]{3,2,1,0:T(8,128)S(1)}, u32[]{:S(2)}) %copy-start.7) | copy-done | bytes 1048600
  42.8 1.4 %collective-permute-start.5 = (bf16[16,32,128]{2,1,0:T(8,128)(2,1)S(1)}, bf16[16,32,128]{2,1,0:T(8,128)(2,1)S(1)}, u32[]{:S(2)}, u32[]{:S(2)}) collective-permute-start(bf16[16,32,128]{2,1,0:T(8,128)(2,1)S(1)} %get-tuple-element.48), channel_id=1, source_target_pairs={{0,8},{8,0},{1,9},{9,1},{2,10},{10,2},{3,11},{11,3},{4,12},{12,4},... | collective-permute-start | bytes 393224 | tf_op jit(solution)/shard_map/ppermute | solution.py:394
  44.2 8.2 %collective-permute-done.5.refs_1_ = bf16[16,32,128]{2,1,0:T(8,128)(2,1)S(1)} collective-permute-done((bf16[16,32,128]{2,1,0:T(8,128)(2,1)S(1)}, bf16[16,32,128]{2,1,0:T(8,128)(2,1)S(1)}, u32[]{:S(2)}, u32[]{:S(2)}) %collective-permute-start.5) | collective-permute-done | bytes 131104 | tf_op jit(solution)/shard_map/ppermute | solution.py:394
  52.4 3.7 %all-to-all-done.refs_0_.first_ref = bf16[128,24,128]{2,1,0:T(8,128)(2,1)S(1)} async-done(((bf16[128,24,128]{2,1,0:T(8,128)(2,1)}), bf16[128,24,128]{2,1,0:T(8,128)(2,1)S(1)}, u32[]{:S(2)}, u32[]{:S(2)}) %all-to-all-start) | async-done | bytes 786464 | tf_op jit(solution)/shard_map/all_to_all | solution.py:387
  56.1 0.2 shard_map.116
  56.4 0.9 %copy-done.6 = bf16[128,32,128]{2,1,0:T(8,128)(2,1)} copy-done((bf16[128,32,128]{2,1,0:T(8,128)(2,1)}, bf16[128,32,128]{2,1,0:T(8,128)(2,1)S(1)}, u32[]{:S(2)}) %copy-start.6) | copy-done | bytes 1048600
  57.3 6.0 %all-to-all-start.1 = ((bf16[128,32,128]{2,1,0:T(8,128)(2,1)}), bf16[128,32,128]{2,1,0:T(8,128)(2,1)S(1)}, u32[]{:S(2)}, u32[]{:S(2)}) async-start(bf16[128,32,128]{2,1,0:T(8,128)(2,1)} %copy-done.6), calls=%async_computation.1 | async-start | bytes 2097152 | tf_op jit(solution)/shard_map/all_to_all | solution.py:409
  63.3 1.2 %copy-done.8 = f32[4,16,32,128]{3,2,1,0:T(8,128)S(1)} copy-done((f32[4,16,32,128]{3,2,1,0:T(8,128)S(1)}, f32[4,16,32,128]{3,2,1,0:T(8,128)}, u32[]{:S(2)}) %copy-start.8) | copy-done | bytes 1048600
  64.5 1.1 %shard_map.115 = bf16[32,4,16,128]{3,2,1,0:T(8,128)(2,1)} custom-call(f32[4,16,32,128]{3,2,1,0:T(8,128)S(1)} %copy-done.8, bf16[16,32,128]{2,1,0:T(8,128)(2,1)S(1)} %collective-permute-done.5.refs_1_), custom_call_target="tpu_custom_call" | custom-call | bytes 2000000 | tf_op jit(solution)/shard_map/pallas_call | solution.py:396
  65.6 17.0 %all-to-all-done.1.full_ref = bf16[128,32,128]{2,1,0:T(8,128)(2,1)S(1)} async-done(((bf16[128,32,128]{2,1,0:T(8,128)(2,1)}), bf16[128,32,128]{2,1,0:T(8,128)(2,1)S(1)}, u32[]{:S(2)}, u32[]{:S(2)}) %all-to-all-start.1) | async-done | bytes 1048608 | tf_op jit(solution)/shard_map/all_to_all | solution.py:409
  82.6 2.7 %shard_map.117 = (f32[64,864]{1,0:T(8,128)}, f32[1728,128]{1,0:T(8,128)}, f32[432]{0:T(512)}, f32[1728]{0:T(1024)}) custom-call(bf16[128,32,128]{2,1,0:T(8,128)(2,1)S(1)} %all-to-all-done.1.full_ref, bf16[128,24,128]{2,1,0:T(8,128)(2,1)S(1)} %all-to-all-done.refs_0_.first_ref, f32[18,128]{1,0:T(8,128)S(1)} %get-tuple-element.54.own_ref, ...), custom_call_target="tpu_custom_call" | custom-call | bytes 4000000 | tf_op jit(solution)/shard_map/pallas_call | solution.py:410
  (18 shorter events, 0.0 us)
Async XLA Ops:
  0.6 16.4 %copy-start.12 = (f32[432]{0:T(512)S(1)}, f32[432]{0:T(512)}, u32[]{:S(2)}) copy-start(f32[432]{0:T(512)} %m2_ref.3) | copy-start | bytes 5188
  0.6 1.2 %copy-start = (bf16[1,64,4,16,128]{4,3,2,1,0:T(8,128)(2,1)S(1)}, bf16[1,64,4,16,128]{4,3,2,1,0:T(8,128)(2,1)}, u32[]{:S(2)}) copy-start(bf16[1,64,4,16,128]{4,3,2,1,0:T(8,128)(2,1)} %param.8) | copy-start | bytes 3145732
  1.9 1.0 %copy-start.4 = (bf16[1,32,4,16,128]{4,3,2,1,0:T(8,128)(2,1)S(1)}, bf16[1,32,4,16,128]{4,3,2,1,0:T(8,128)(2,1)}, u32[]{:S(2)}) copy-start(bf16[1,32,4,16,128]{4,3,2,1,0:T(8,128)(2,1)} %param.7) | copy-start | bytes 1572868
  2.9 0.9 %copy-start.10 = (bf16[1,128,2,512]{3,2,1,0:T(2,128)(2,1)S(1)}, bf16[1,128,2,512]{3,2,1,0:T(2,128)(2,1)}, u32[]{:S(2)}) copy-start(bf16[1,128,2,512]{3,2,1,0:T(2,128)(2,1)} %param.9) | copy-start | bytes 786436
  3.9 13.2 %copy-start.1 = (bf16[1,64,4,16,128]{4,3,2,1,0:T(8,128)(2,1)S(1)}, bf16[1,64,4,16,128]{4,3,2,1,0:T(8,128)(2,1)}, u32[]{:S(2)}) copy-start(bf16[1,64,4,16,128]{4,3,2,1,0:T(8,128)(2,1)} %param.8) | copy-start | bytes 3145732
  3.9 13.2 %copy-start.5 = (bf16[1,32,4,16,128]{4,3,2,1,0:T(8,128)(2,1)S(1)}, bf16[1,32,4,16,128]{4,3,2,1,0:T(8,128)(2,1)}, u32[]{:S(2)}) copy-start(bf16[1,32,4,16,128]{4,3,2,1,0:T(8,128)(2,1)} %param.7) | copy-start | bytes 1572868
  3.9 13.2 %copy-start.9 = (f32[64,864]{1,0:T(8,128)S(1)}, f32[64,864]{1,0:T(8,128)}, u32[]{:S(2)}) copy-start(f32[64,864]{1,0:T(8,128)} %w2_ref.2) | copy-start | bytes 663556
  3.9 13.2 %copy-start.11 = (f32[1728]{0:T(1024)S(1)}, f32[1728]{0:T(1024)}, u32[]{:S(2)}) copy-start(f32[1728]{0:T(1024)} %m3_ref.3) | copy-start | bytes 20740
  6.0 14.0 %collective-permute-start = (bf16[1024,128]{1,0:T(8,128)(2,1)S(1)}, bf16[1024,128]{1,0:T(8,128)(2,1)S(1)}, u32[]{:S(2)}, u32[]{:S(2)}) collective-permute-start(bf16[1024,128]{1,0:T(8,128)(2,1)S(1)} %get-tuple-element.34), channel_id=1, source_target_pairs={{0,8},{8,0},{1,9},{9,1},{2,10},{10,2},{3,11},{11,3},{4,12},{12,4},... | collective-permute-start | bytes 786440 | tf_op jit(solution)/shard_map/ppermute | solution.py:358
  8.2 11.7 %collective-permute-start.1 = (bf16[512,128]{1,0:T(8,128)(2,1)S(1)}, bf16[512,128]{1,0:T(8,128)(2,1)S(1)}, u32[]{:S(2)}, u32[]{:S(2)}) collective-permute-start(bf16[512,128]{1,0:T(8,128)(2,1)S(1)} %get-tuple-element.35), channel_id=1, source_target_pairs={{0,1},{1,0},{2,3},{3,2},{4,5},{5,4},{6,7},{7,6},{8,9},{9,8},{10,11... | collective-permute-start | bytes 393224 | tf_op jit(solution)/shard_map/ppermute | solution.py:359
  10.8 9.1 %collective-permute-start.2 = (bf16[512,128]{1,0:T(8,128)(2,1)S(1)}, bf16[512,128]{1,0:T(8,128)(2,1)S(1)}, u32[]{:S(2)}, u32[]{:S(2)}) collective-permute-start(bf16[512,128]{1,0:T(8,128)(2,1)S(1)} %get-tuple-element.36), channel_id=1, source_target_pairs={{1,2},{2,1},{3,4},{4,3},{5,6},{6,5},{9,10},{10,9},{11,12},{12,11},... | collective-permute-start | bytes 393224 | tf_op jit(solution)/shard_map/ppermute | solution.py:360
  11.5 8.4 %collective-permute-start.3 = (bf16[128,128]{1,0:T(8,128)(2,1)S(1)}, bf16[128,128]{1,0:T(8,128)(2,1)S(1)}, u32[]{:S(2)}, u32[]{:S(2)}) collective-permute-start(bf16[128,128]{1,0:T(8,128)(2,1)S(1)} %get-tuple-element.37), channel_id=1, source_target_pairs={{0,9},{1,8},{2,11},{3,10},{4,13},{5,12},{6,15},{7,14},{8,1},{9,0},... | collective-permute-start | bytes 98312 | tf_op jit(solution)/shard_map/ppermute | solution.py:361
  16.4 3.5 %collective-permute-start.4 = (bf16[128,128]{1,0:T(8,128)(2,1)S(1)}, bf16[128,128]{1,0:T(8,128)(2,1)S(1)}, u32[]{:S(2)}, u32[]{:S(2)}) collective-permute-start(bf16[128,128]{1,0:T(8,128)(2,1)S(1)} %get-tuple-element.38), channel_id=1, source_target_pairs={{1,10},{2,9},{3,12},{4,11},{5,14},{6,13},{9,2},{10,1},{11,4},{12,3... | collective-permute-start | bytes 98312 | tf_op jit(solution)/shard_map/ppermute | solution.py:362
  17.1 1.2 %copy-start.2 = (f32[128,1728]{0,1:T(8,128)S(1)}, f32[128,1728]{0,1:T(8,128)}, u32[]{:S(2)}) copy-start(f32[128,1728]{0,1:T(8,128)} %param.11) | copy-start | bytes 2654212
  26.5 29.7 %all-to-all-start = ((bf16[128,24,128]{2,1,0:T(8,128)(2,1)}), bf16[128,24,128]{2,1,0:T(8,128)(2,1)S(1)}, u32[]{:S(2)}, u32[]{:S(2)}) async-start(bf16[128,24,128]{2,1,0:T(8,128)(2,1)} %shard_map.113), calls=%async_computation | async-start | bytes 1572864 | tf_op jit(solution)/shard_map/all_to_all | solution.py:387
  41.8 1.0 %copy-start.7 = (f32[4,16,32,128]{3,2,1,0:T(8,128)}, f32[4,16,32,128]{3,2,1,0:T(8,128)S(1)}, u32[]{:S(2)}) copy-start(f32[4,16,32,128]{3,2,1,0:T(8,128)S(1)} %get-tuple-element.49.refs_0_) | copy-start | bytes 3145732
  42.8 9.6 %collective-permute-start.5 = (bf16[16,32,128]{2,1,0:T(8,128)(2,1)S(1)}, bf16[16,32,128]{2,1,0:T(8,128)(2,1)S(1)}, u32[]{:S(2)}, u32[]{:S(2)}) collective-permute-start(bf16[16,32,128]{2,1,0:T(8,128)(2,1)S(1)} %get-tuple-element.48), channel_id=1, source_target_pairs={{0,8},{8,0},{1,9},{9,1},{2,10},{10,2},{3,11},{11,3},{4,12},{12,4},... | collective-permute-start | bytes 393224 | tf_op jit(solution)/shard_map/ppermute | solution.py:394
  56.3 1.0 %copy-start.6 = (bf16[128,32,128]{2,1,0:T(8,128)(2,1)}, bf16[128,32,128]{2,1,0:T(8,128)(2,1)S(1)}, u32[]{:S(2)}) copy-start(bf16[128,32,128]{2,1,0:T(8,128)(2,1)S(1)} %get-tuple-element.52) | copy-start | bytes 3145732
  57.3 25.3 %copy-start.3 = (f32[128,1728]{0,1:T(8,128)S(1)}, f32[128,1728]{0,1:T(8,128)}, u32[]{:S(2)}) copy-start(f32[128,1728]{0,1:T(8,128)} %param.11) | copy-start | bytes 2654212
  57.3 25.3 %all-to-all-start.1 = ((bf16[128,32,128]{2,1,0:T(8,128)(2,1)}), bf16[128,32,128]{2,1,0:T(8,128)(2,1)S(1)}, u32[]{:S(2)}, u32[]{:S(2)}) async-start(bf16[128,32,128]{2,1,0:T(8,128)(2,1)} %copy-done.6), calls=%async_computation.1 | async-start | bytes 2097152 | tf_op jit(solution)/shard_map/all_to_all | solution.py:409
  63.3 1.2 %copy-start.8 = (f32[4,16,32,128]{3,2,1,0:T(8,128)S(1)}, f32[4,16,32,128]{3,2,1,0:T(8,128)}, u32[]{:S(2)}) copy-start(f32[4,16,32,128]{3,2,1,0:T(8,128)} %copy-done.7) | copy-start | bytes 3145732

commit v4 on v3

--- a/solution.py
+++ b/solution.py
@@ -15,9 +15,11 @@
 BF16 = jnp.bfloat16
 
 
-def call(body, outs, scratch=(), flops=0, moved=0, limit=20):
+def call(body, outs, scratch=(), flops=0, moved=0, limit=20, far=None):
+    extra = {} if far is None else dict(in_specs=[pl.BlockSpec(memory_space=pl.ANY)] * far)
     return pl.pallas_call(
         body,
+        **extra,
         out_shape=[jax.ShapeDtypeStruct(shape, dtype) for shape, dtype in outs],
         scratch_shapes=list(scratch),
         compiler_params=pltpu.CompilerParams(vmem_limit_bytes=limit * 1024 * 1024),
@@ -41,8 +43,17 @@
     return jnp.concatenate([x[..., amount:], x[..., :amount]], axis=-1)
 
 
-def arrange(cot_ref, pre_ref, act_ref, cot_out, side_out, a_out, b_out, diag_a_out, diag_b_out):
+def arrange(cot_far, pre_far, act_far, cot_out, side_out, a_out, b_out, diag_a_out, diag_b_out,
+            cot_ref, pre_ref, act_ref, sems):
     dep = lax.axis_index("depth")
+    loads = [
+        pltpu.make_async_copy(cot_far, cot_ref, sems.at[0]),
+        pltpu.make_async_copy(act_far.at[:, 3 * (1 - dep)], act_ref, sems.at[1]),
+        pltpu.make_async_copy(pre_far, pre_ref, sems.at[2]),
+    ]
+    for load in loads:
+        load.start()
+    loads[0].wait()
     odd = lax.rem(lax.axis_index("height"), 2) == 1
     cots = [cot_ref[:, d, :] for d in range(2)]
     for d in range(2):
@@ -55,8 +66,10 @@
     diag_b_out[...] = jnp.where(odd, near[:, 384:], near[:, :128])
     for t in range(4):
         side_out[128 * t : 128 * t + 128] = near[:, 128 * t : 128 * t + 128]
-    layer = jnp.swapaxes(act_ref[:, 3 * (1 - dep)].astype(F32), 0, 1).astype(BF16)
+    loads[1].wait()
+    layer = jnp.swapaxes(act_ref[...].astype(F32), 0, 1).astype(BF16)
     side_out[512:] = layer.reshape(512, 128)
+    loads[2].wait()
     for d in range(4):
         first, final = pre_ref[:, d, 0, :], pre_ref[:, d, 15, :]
         place = slice(256 + 64 * d, 320 + 64 * d)
@@ -346,7 +359,9 @@
         arrange,
         [((2, 128, 512), BF16), ((1024, 128), BF16), ((512, 128), BF16),
          ((512, 128), BF16), ((128, 128), BF16), ((128, 128), BF16)],
-        moved=4_000_000,
+        [pltpu.VMEM((128, 2, 512), BF16), pltpu.VMEM((64, 4, 16, 128), BF16), pltpu.VMEM((32, 16, 128), BF16),
+         pltpu.SemaphoreType.DMA((3,))],
+        moved=4_000_000, far=3, limit=62,
     )(cot, pre, act)
     tall = lax.axis_size("height")
     swap = [(0, 1), (1, 0)]

time: 85.7 us -> 84.4 us (0.985)
  local copies, waits for them, and re-layouts: 7.57 us -> 5.22 us
    unnamed x26 -> x28, local copies, waits for them, and re-layouts: 7.57 us -> 5.22 us
    pallas_call x1, Pallas kernels: 2.1 us -> 3.85 us  [local(): call(arrange, [((2, 128, 512), BF16), ((1024, 128), BF16), ((512, 128), B...]
    pallas_call x1, Pallas kernels: 3.7 us -> 2.82 us  [local(): call(fine, [((128, 24, 128), BF16)], [pltpu.VMEM((4, 18, 64, 128), BF16),...]
where the time goes in v4:
time: 84.4 us; the launch traced here: 84.1 us
  starting transfers between devices  31.7 us (38%)
  waiting for transfers between devices  29 us (34%)
  Pallas kernels  17.2 us (20%)
  local copies, waits for them, and re-layouts  5.22 us (6%)
  between operations  0.9 us (1%)
    all_to_all x1, waiting for transfers between devices, local(): full = lax.all_to_all(send, AXES, 0, 0, tiled=True)  17 us
    all_to_all x1, starting transfers between devices, local(): parts = lax.all_to_all(parts, AXES, 0, 0, tiled=True)  13.3 us
    ppermute x1, waiting for transfers between devices, local(): ship = lax.ppermute(ship, 'depth', swap)  8.28 us
    all_to_all x1, starting transfers between devices, local(): full = lax.all_to_all(send, AXES, 0, 0, tiled=True)  5.99 us
    unnamed x28, local copies, waits for them, and re-layouts  5.22 us
    ppermute x1, starting transfers between devices, local(): got_da = lax.ppermute(send_da, ('depth', 'height'), cross_a)  4.92 us
    pallas_call x1, Pallas kernels, local(): call(arrange, [((2, 128, 512), BF16), ((1024, 128), BF16), ((512, 128), B...  3.85 us
    all_to_all x1, waiting for transfers between devices, local(): parts = lax.all_to_all(parts, AXES, 0, 0, tiled=True)  3.73 us
  transfers between devices with their start and end apart: 8, of which 3 were waited for; matrix products, arithmetic and copies ran while one was open for 0% of the time, Pallas kernels for 6%

profile of v4, /device:TPU:1, one launch (start us, length us, event | category | flops | bytes accessed | tf_op | source)
XLA Modules:
  0.0 84.1 jit_solution(13568954336456419694)
XLA Ops:
  0.7 3.9 %shard_map.110 = (bf16[2,128,512]{2,1,0:T(8,128)(2,1)}, bf16[1024,128]{1,0:T(8,128)(2,1)}, bf16[512,128]{1,0:T(8,128)(2,1)}, bf16[512,128]{1,0:T(8,128)(2,1)}, b...) custom-call(bf16[128,2,512]{2,1,0:T(2,128)(2,1)} %bitcast.15, bf16[64,4,16,128]{3,2,1,0:T(8,128)(2,1)} %bitcast.7, ...), custom_call_target="tpu_custom_call" | custom-call | bytes 4000000 | tf_op jit(solution)/shard_map/pallas_call | solution.py:358
  4.5 2.2 %collective-permute-start = (bf16[1024,128]{1,0:T(8,128)(2,1)}, bf16[1024,128]{1,0:T(8,128)(2,1)S(1)}, u32[]{:S(2)}, u32[]{:S(2)}) collective-permute-start(bf16[1024,128]{1,0:T(8,128)(2,1)} %get-tuple-element.34), channel_id=1, source_target_pairs={{0,8},{8,0},{1,9},{9,1},{2,10},{10,2},{3,11},{11,3},{4,12},{12,4},... | collective-permute-start | bytes 786440 | tf_op jit(solution)/shard_map/ppermute | solution.py:373
  6.7 2.6 %collective-permute-start.1 = (bf16[512,128]{1,0:T(8,128)(2,1)}, bf16[512,128]{1,0:T(8,128)(2,1)S(1)}, u32[]{:S(2)}, u32[]{:S(2)}) collective-permute-start(bf16[512,128]{1,0:T(8,128)(2,1)} %get-tuple-element.35), channel_id=1, source_target_pairs={{0,1},{1,0},{2,3},{3,2},{4,5},{5,4},{6,7},{7,6},{8,9},{9,8},{10,11... | collective-permute-start | bytes 393224 | tf_op jit(solution)/shard_map/ppermute | solution.py:374
  9.4 0.7 collective-permute-start.2
  10.0 4.9 %collective-permute-start.3 = (bf16[128,128]{1,0:T(8,128)(2,1)}, bf16[128,128]{1,0:T(8,128)(2,1)S(1)}, u32[]{:S(2)}, u32[]{:S(2)}) collective-permute-start(bf16[128,128]{1,0:T(8,128)(2,1)} %get-tuple-element.37), channel_id=1, source_target_pairs={{0,9},{1,8},{2,11},{3,10},{4,13},{5,12},{6,15},{7,14},{8,1},{9,0},... | collective-permute-start | bytes 98312 | tf_op jit(solution)/shard_map/ppermute | solution.py:376
  15.0 0.7 collective-permute-start.4
  15.7 0.0 copy-start.1
  15.7 1.2 %copy-done.1 = f32[128,1728]{0,1:T(8,128)S(1)} copy-done((f32[128,1728]{0,1:T(8,128)S(1)}, f32[128,1728]{0,1:T(8,128)}, u32[]{:S(2)}) %copy-start.1) | copy-done | bytes 884760
  16.8 1.6 %shard_map.111 = (bf16[4,16,64,128]{3,2,1,0:T(8,128)(2,1)S(1)}, bf16[128,512]{1,0:T(8,128)(2,1)S(1)}, bf16[16,384,128]{2,1,0:T(8,128)(2,1)S(1)}, bf16[192,768]{1...) custom-call(bf16[64,4,16,128]{3,2,1,0:T(8,128)(2,1)S(1)} %bitcast.8, ...), custom_call_target="tpu_custom_call" | custom-call | flops 100000000 | bytes 8000000 | tf_op jit(solution)/shard_map/pallas_call | solution.py:379
  18.5 0.0 collective-permute-done.3.refs_4_
  18.5 0.0 collective-permute-done.4.refs_5_
  18.5 0.0 collective-permute-done.1.refs_2_.a_ref
  18.5 0.0 collective-permute-done.2.refs_3_.b_ref
  18.5 0.0 copy-start.12
  18.5 0.0 collective-permute-done.refs_1_.side_ref
  18.5 2.8 %shard_map.112 = (bf16[2,64,768]{2,1,0:T(8,128)(2,1)S(1)}, f32[14,128,128]{2,1,0:T(8,128)S(1)}) custom-call(bf16[2,128,512]{2,1,0:T(8,128)(2,1)S(1)} %copy-done.11, bf16[1024,128]{1,0:T(8,128)(2,1)S(1)} %collective-permute-done.refs_1_.side_ref, bf16[512,128]{1,0:T(8,128)(2,1)S(1)} %collective-permute-done.1.refs_2_.a_ref, ...), custom_call_target="tpu_custom_call" | custom-call | flops 2000000000 | bytes 4000000 | tf_op jit(solution)/shard_map/pallas_call | solution.py:386
  21.4 2.8 %shard_map.113 = bf16[128,24,128]{2,1,0:T(8,128)(2,1)S(1)} custom-call(bf16[2,64,768]{2,1,0:T(8,128)(2,1)S(1)} %get-tuple-element.41.back_ref, bf16[4,16,64,128]{3,2,1,0:T(8,128)(2,1)S(1)} %get-tuple-element.42.pre_ref, bf16[512,128]{1,0:T(8,128)(2,1)S(1)} %collective-permute-done.1.refs_2_.a_ref, bf16[512,128]{1,0:T(8,128)(2,1)S(1)} %collective-permute-done.2.refs_3_.b_ref, ...), custom_call_target="tpu_custom_call" | custom-call | flops 2000000000 | bytes 6000000 | tf_op jit(solution)/shard_map/pallas_call | solution.py:394
  24.2 0.0 copy-start.8
  24.2 0.9 %copy-done.8 = bf16[128,24,128]{2,1,0:T(8,128)(2,1)} copy-done((bf16[128,24,128]{2,1,0:T(8,128)(2,1)}, bf16[128,24,128]{2,1,0:T(8,128)(2,1)S(1)}, u32[]{:S(2)}) %copy-start.8) | copy-done | bytes 786456
  25.1 13.3 %all-to-all-start = ((bf16[128,24,128]{2,1,0:T(8,128)(2,1)}), bf16[128,24,128]{2,1,0:T(8,128)(2,1)S(1)}, u32[]{:S(2)}, u32[]{:S(2)}) async-start(bf16[128,24,128]{2,1,0:T(8,128)(2,1)} %copy-done.8), calls=%async_computation | async-start | bytes 1572864 | tf_op jit(solution)/shard_map/all_to_all | solution.py:402
  38.4 2.2 %shard_map.114 = (f32[4,16,32,128]{3,2,1,0:T(8,128)S(1)}, bf16[16,32,128]{2,1,0:T(8,128)(2,1)S(1)}) custom-call(bf16[2,64,768]{2,1,0:T(8,128)(2,1)S(1)} %get-tuple-element.41.back_ref, bf16[64,4,16,128]{3,2,1,0:T(8,128)(2,1)S(1)} %bitcast.9, bf16[512,128]{1,0:T(8,128)(2,1)S(1)} %collective-permute-done.1.refs_2_.a_ref, bf16[512,128]{1,0:T(8,128)(2,1)S(1)} %copy-done.13, ...), custom_call_target="tpu_custom_call" | custom-call | flops 4000000000 | bytes 6000000 | tf_op jit(solution)/shard_map/pallas_call | solution.py:403
  40.5 1.0 %copy-done.5 = f32[4,16,32,128]{3,2,1,0:T(8,128)} copy-done((f32[4,16,32,128]{3,2,1,0:T(8,128)}, f32[4,16,32,128]{3,2,1,0:T(8,128)S(1)}, u32[]{:S(2)}) %copy-start.5) | copy-done | bytes 1048600
  41.5 1.4 %collective-permute-start.5 = (bf16[16,32,128]{2,1,0:T(8,128)(2,1)S(1)}, bf16[16,32,128]{2,1,0:T(8,128)(2,1)S(1)}, u32[]{:S(2)}, u32[]{:S(2)}) collective-permute-start(bf16[16,32,128]{2,1,0:T(8,128)(2,1)S(1)} %get-tuple-element.48), channel_id=1, source_target_pairs={{0,8},{8,0},{1,9},{9,1},{2,10},{10,2},{3,11},{11,3},{4,12},{12,4},... | collective-permute-start | bytes 393224 | tf_op jit(solution)/shard_map/ppermute | solution.py:409
  42.9 8.3 %collective-permute-done.5.refs_1_ = bf16[16,32,128]{2,1,0:T(8,128)(2,1)S(1)} collective-permute-done((bf16[16,32,128]{2,1,0:T(8,128)(2,1)S(1)}, bf16[16,32,128]{2,1,0:T(8,128)(2,1)S(1)}, u32[]{:S(2)}, u32[]{:S(2)}) %collective-permute-start.5) | collective-permute-done | bytes 131104 | tf_op jit(solution)/shard_map/ppermute | solution.py:409
  51.2 3.7 %all-to-all-done.refs_0_.first_ref = bf16[128,24,128]{2,1,0:T(8,128)(2,1)S(1)} async-done(((bf16[128,24,128]{2,1,0:T(8,128)(2,1)}), bf16[128,24,128]{2,1,0:T(8,128)(2,1)S(1)}, u32[]{:S(2)}, u32[]{:S(2)}) %all-to-all-start) | async-done | bytes 786464 | tf_op jit(solution)/shard_map/all_to_all | solution.py:402
  54.9 0.2 shard_map.116
  55.1 0.9 %copy-done.4 = bf16[128,32,128]{2,1,0:T(8,128)(2,1)} copy-done((bf16[128,32,128]{2,1,0:T(8,128)(2,1)}, bf16[128,32,128]{2,1,0:T(8,128)(2,1)S(1)}, u32[]{:S(2)}) %copy-start.4) | copy-done | bytes 1048600
  56.1 6.0 %all-to-all-start.1 = ((bf16[128,32,128]{2,1,0:T(8,128)(2,1)}), bf16[128,32,128]{2,1,0:T(8,128)(2,1)S(1)}, u32[]{:S(2)}, u32[]{:S(2)}) async-start(bf16[128,32,128]{2,1,0:T(8,128)(2,1)} %copy-done.4), calls=%async_computation.1 | async-start | bytes 2097152 | tf_op jit(solution)/shard_map/all_to_all | solution.py:424
  62.1 1.2 %copy-done.6 = f32[4,16,32,128]{3,2,1,0:T(8,128)S(1)} copy-done((f32[4,16,32,128]{3,2,1,0:T(8,128)S(1)}, f32[4,16,32,128]{3,2,1,0:T(8,128)}, u32[]{:S(2)}) %copy-start.6) | copy-done | bytes 1048600
  63.3 1.1 %shard_map.115 = bf16[32,4,16,128]{3,2,1,0:T(8,128)(2,1)} custom-call(f32[4,16,32,128]{3,2,1,0:T(8,128)S(1)} %copy-done.6, bf16[16,32,128]{2,1,0:T(8,128)(2,1)S(1)} %collective-permute-done.5.refs_1_), custom_call_target="tpu_custom_call" | custom-call | bytes 2000000 | tf_op jit(solution)/shard_map/pallas_call | solution.py:411
  64.4 17.0 %all-to-all-done.1.full_ref = bf16[128,32,128]{2,1,0:T(8,128)(2,1)S(1)} async-done(((bf16[128,32,128]{2,1,0:T(8,128)(2,1)}), bf16[128,32,128]{2,1,0:T(8,128)(2,1)S(1)}, u32[]{:S(2)}, u32[]{:S(2)}) %all-to-all-start.1) | async-done | bytes 1048608 | tf_op jit(solution)/shard_map/all_to_all | solution.py:424
  81.4 2.7 %shard_map.117 = (f32[64,864]{1,0:T(8,128)}, f32[1728,128]{1,0:T(8,128)}, f32[432]{0:T(512)}, f32[1728]{0:T(1024)}) custom-call(bf16[128,32,128]{2,1,0:T(8,128)(2,1)S(1)} %all-to-all-done.1.full_ref, bf16[128,24,128]{2,1,0:T(8,128)(2,1)S(1)} %all-to-all-done.refs_0_.first_ref, f32[18,128]{1,0:T(8,128)S(1)} %get-tuple-element.54.own_ref, ...), custom_call_target="tpu_custom_call" | custom-call | bytes 4000000 | tf_op jit(solution)/shard_map/pallas_call | solution.py:425
  (20 shorter events, 0.0 us)
Async XLA Ops:
  0.6 15.0 %copy-start = (bf16[1,64,4,16,128]{4,3,2,1,0:T(8,128)(2,1)S(1)}, bf16[1,64,4,16,128]{4,3,2,1,0:T(8,128)(2,1)}, u32[]{:S(2)}) copy-start(bf16[1,64,4,16,128]{4,3,2,1,0:T(8,128)(2,1)} %param.8) | copy-start | bytes 3145732
  0.6 15.0 %copy-start.3 = (bf16[1,32,4,16,128]{4,3,2,1,0:T(8,128)(2,1)S(1)}, bf16[1,32,4,16,128]{4,3,2,1,0:T(8,128)(2,1)}, u32[]{:S(2)}) copy-start(bf16[1,32,4,16,128]{4,3,2,1,0:T(8,128)(2,1)} %param.7) | copy-start | bytes 1572868
  0.7 15.0 %copy-start.9 = (f32[1728]{0:T(1024)S(1)}, f32[1728]{0:T(1024)}, u32[]{:S(2)}) copy-start(f32[1728]{0:T(1024)} %m3_ref.3) | copy-start | bytes 20740
  0.7 15.0 %copy-start.10 = (f32[432]{0:T(512)S(1)}, f32[432]{0:T(512)}, u32[]{:S(2)}) copy-start(f32[432]{0:T(512)} %m2_ref.3) | copy-start | bytes 5188
  0.7 15.0 %copy-start.7 = (f32[64,864]{1,0:T(8,128)S(1)}, f32[64,864]{1,0:T(8,128)}, u32[]{:S(2)}) copy-start(f32[64,864]{1,0:T(8,128)} %w2_ref.2) | copy-start | bytes 663556
  4.5 14.0 %collective-permute-start = (bf16[1024,128]{1,0:T(8,128)(2,1)}, bf16[1024,128]{1,0:T(8,128)(2,1)S(1)}, u32[]{:S(2)}, u32[]{:S(2)}) collective-permute-start(bf16[1024,128]{1,0:T(8,128)(2,1)} %get-tuple-element.34), channel_id=1, source_target_pairs={{0,8},{8,0},{1,9},{9,1},{2,10},{10,2},{3,11},{11,3},{4,12},{12,4},... | collective-permute-start | bytes 786440 | tf_op jit(solution)/shard_map/ppermute | solution.py:373
  6.7 11.7 %collective-permute-start.1 = (bf16[512,128]{1,0:T(8,128)(2,1)}, bf16[512,128]{1,0:T(8,128)(2,1)S(1)}, u32[]{:S(2)}, u32[]{:S(2)}) collective-permute-start(bf16[512,128]{1,0:T(8,128)(2,1)} %get-tuple-element.35), channel_id=1, source_target_pairs={{0,1},{1,0},{2,3},{3,2},{4,5},{5,4},{6,7},{7,6},{8,9},{9,8},{10,11... | collective-permute-start | bytes 393224 | tf_op jit(solution)/shard_map/ppermute | solution.py:374
  9.4 9.1 %collective-permute-start.2 = (bf16[512,128]{1,0:T(8,128)(2,1)}, bf16[512,128]{1,0:T(8,128)(2,1)S(1)}, u32[]{:S(2)}, u32[]{:S(2)}) collective-permute-start(bf16[512,128]{1,0:T(8,128)(2,1)} %get-tuple-element.36), channel_id=1, source_target_pairs={{1,2},{2,1},{3,4},{4,3},{5,6},{6,5},{9,10},{10,9},{11,12},{12,11},... | collective-permute-start | bytes 393224 | tf_op jit(solution)/shard_map/ppermute | solution.py:375
  10.0 8.4 %collective-permute-start.3 = (bf16[128,128]{1,0:T(8,128)(2,1)}, bf16[128,128]{1,0:T(8,128)(2,1)S(1)}, u32[]{:S(2)}, u32[]{:S(2)}) collective-permute-start(bf16[128,128]{1,0:T(8,128)(2,1)} %get-tuple-element.37), channel_id=1, source_target_pairs={{0,9},{1,8},{2,11},{3,10},{4,13},{5,12},{6,15},{7,14},{8,1},{9,0},... | collective-permute-start | bytes 98312 | tf_op jit(solution)/shard_map/ppermute | solution.py:376
  15.0 3.5 %collective-permute-start.4 = (bf16[128,128]{1,0:T(8,128)(2,1)}, bf16[128,128]{1,0:T(8,128)(2,1)S(1)}, u32[]{:S(2)}, u32[]{:S(2)}) collective-permute-start(bf16[128,128]{1,0:T(8,128)(2,1)} %get-tuple-element.38), channel_id=1, source_target_pairs={{1,10},{2,9},{3,12},{4,11},{5,14},{6,13},{9,2},{10,1},{11,4},{12,3... | collective-permute-start | bytes 98312 | tf_op jit(solution)/shard_map/ppermute | solution.py:377
  15.7 1.2 %copy-start.1 = (f32[128,1728]{0,1:T(8,128)S(1)}, f32[128,1728]{0,1:T(8,128)}, u32[]{:S(2)}) copy-start(f32[128,1728]{0,1:T(8,128)} %param.11) | copy-start | bytes 2654212
  16.8 1.7 %copy-start.11 = (bf16[2,128,512]{2,1,0:T(8,128)(2,1)S(1)}, bf16[2,128,512]{2,1,0:T(8,128)(2,1)}, u32[]{:S(2)}) copy-start(bf16[2,128,512]{2,1,0:T(8,128)(2,1)} %get-tuple-element.33.refs_0_) | copy-start | bytes 786436
  18.5 2.8 %copy-start.12 = (bf16[512,128]{1,0:T(8,128)(2,1)}, bf16[512,128]{1,0:T(8,128)(2,1)S(1)}, u32[]{:S(2)}) copy-start(bf16[512,128]{1,0:T(8,128)(2,1)S(1)} %collective-permute-done.2.refs_3_.b_ref) | copy-start | bytes 393220
  24.2 0.9 %copy-start.8 = (bf16[128,24,128]{2,1,0:T(8,128)(2,1)}, bf16[128,24,128]{2,1,0:T(8,128)(2,1)S(1)}, u32[]{:S(2)}) copy-start(bf16[128,24,128]{2,1,0:T(8,128)(2,1)S(1)} %shard_map.113) | copy-start | bytes 2359300
  25.1 13.3 %copy-start.13 = (bf16[512,128]{1,0:T(8,128)(2,1)S(1)}, bf16[512,128]{1,0:T(8,128)(2,1)}, u32[]{:S(2)}) copy-start(bf16[512,128]{1,0:T(8,128)(2,1)} %copy-done.12) | copy-start | bytes 393220
  25.1 29.9 %all-to-all-start = ((bf16[128,24,128]{2,1,0:T(8,128)(2,1)}), bf16[128,24,128]{2,1,0:T(8,128)(2,1)S(1)}, u32[]{:S(2)}, u32[]{:S(2)}) async-start(bf16[128,24,128]{2,1,0:T(8,128)(2,1)} %copy-done.8), calls=%async_computation | async-start | bytes 1572864 | tf_op jit(solution)/shard_map/all_to_all | solution.py:402
  40.5 1.0 %copy-start.5 = (f32[4,16,32,128]{3,2,1,0:T(8,128)}, f32[4,16,32,128]{3,2,1,0:T(8,128)S(1)}, u32[]{:S(2)}) copy-start(f32[4,16,32,128]{3,2,1,0:T(8,128)S(1)} %get-tuple-element.49.refs_0_) | copy-start | bytes 3145732
  41.5 9.7 %collective-permute-start.5 = (bf16[16,32,128]{2,1,0:T(8,128)(2,1)S(1)}, bf16[16,32,128]{2,1,0:T(8,128)(2,1)S(1)}, u32[]{:S(2)}, u32[]{:S(2)}) collective-permute-start(bf16[16,32,128]{2,1,0:T(8,128)(2,1)S(1)} %get-tuple-element.48), channel_id=1, source_target_pairs={{0,8},{8,0},{1,9},{9,1},{2,10},{10,2},{3,11},{11,3},{4,12},{12,4},... | collective-permute-start | bytes 393224 | tf_op jit(solution)/shard_map/ppermute | solution.py:409
  55.1 1.0 %copy-start.4 = (bf16[128,32,128]{2,1,0:T(8,128)(2,1)}, bf16[128,32,128]{2,1,0:T(8,128)(2,1)S(1)}, u32[]{:S(2)}) copy-start(bf16[128,32,128]{2,1,0:T(8,128)(2,1)S(1)} %get-tuple-element.52) | copy-start | bytes 3145732
  56.1 25.3 %copy-start.2 = (f32[128,1728]{0,1:T(8,128)S(1)}, f32[128,1728]{0,1:T(8,128)}, u32[]{:S(2)}) copy-start(f32[128,1728]{0,1:T(8,128)} %param.11) | copy-start | bytes 2654212
  56.1 25.3 %all-to-all-start.1 = ((bf16[128,32,128]{2,1,0:T(8,128)(2,1)}), bf16[128,32,128]{2,1,0:T(8,128)(2,1)S(1)}, u32[]{:S(2)}, u32[]{:S(2)}) async-start(bf16[128,32,128]{2,1,0:T(8,128)(2,1)} %copy-done.4), calls=%async_computation.1 | async-start | bytes 2097152 | tf_op jit(solution)/shard_map/all_to_all | solution.py:424
  62.1 1.2 %copy-start.6 = (f32[4,16,32,128]{3,2,1,0:T(8,128)S(1)}, f32[4,16,32,128]{3,2,1,0:T(8,128)}, u32[]{:S(2)}) copy-start(f32[4,16,32,128]{3,2,1,0:T(8,128)} %copy-done.5) | copy-start | bytes 3145732

commit v5 on v4

--- a/solution.py
+++ b/solution.py
@@ -15,16 +15,22 @@
 BF16 = jnp.bfloat16
 
 
-def call(body, outs, scratch=(), flops=0, moved=0, limit=20, far=None):
-    extra = {} if far is None else dict(in_specs=[pl.BlockSpec(memory_space=pl.ANY)] * far)
-    return pl.pallas_call(
-        body,
-        **extra,
-        out_shape=[jax.ShapeDtypeStruct(shape, dtype) for shape, dtype in outs],
-        scratch_shapes=list(scratch),
-        compiler_params=pltpu.CompilerParams(vmem_limit_bytes=limit * 1024 * 1024),
-        cost_estimate=pl.CostEstimate(flops=flops, bytes_accessed=moved, transcendentals=0),
-    )
+def call(body, outs, scratch=(), flops=0, moved=0, far=(), far_out=()):
+    def run(*args):
+        return pl.pallas_call(
+            body,
+            out_shape=[
+                pltpu.HBM(shape, dtype) if i in far_out else jax.ShapeDtypeStruct(shape, dtype)
+                for i, (shape, dtype) in enumerate(outs)
+            ],
+            in_specs=[pl.BlockSpec(memory_space=pltpu.HBM if i in far else pltpu.VMEM) for i in range(len(args))],
+            out_specs=[pl.BlockSpec(memory_space=pltpu.HBM if i in far_out else pltpu.VMEM) for i in range(len(outs))],
+            scratch_shapes=list(scratch),
+            compiler_params=pltpu.CompilerParams(vmem_limit_bytes=20 * 1024 * 1024),
+            cost_estimate=pl.CostEstimate(flops=flops, bytes_accessed=moved, transcendentals=0),
+        )(*(pltpu.with_memory_space_constraint(x, pltpu.HBM) if i in far else x for i, x in enumerate(args)))
+
+    return run
 
 
 def dot_nt(a, b):
@@ -46,11 +52,9 @@
 def arrange(cot_far, pre_far, act_far, cot_out, side_out, a_out, b_out, diag_a_out, diag_b_out,
             cot_ref, pre_ref, act_ref, sems):
     dep = lax.axis_index("depth")
-    loads = [
-        pltpu.make_async_copy(cot_far, cot_ref, sems.at[0]),
-        pltpu.make_async_copy(act_far.at[:, 3 * (1 - dep)], act_ref, sems.at[1]),
-        pltpu.make_async_copy(pre_far, pre_ref, sems.at[2]),
-    ]
+    loads = [pltpu.make_async_copy(cot_far, cot_ref, sems.at[0])]
+    loads += [pltpu.make_async_copy(act_far.at[:, 3 * (1 - dep)], act_ref, sems.at[1])]
+    loads += [pltpu.make_async_copy(pre_far.at[:, d], pre_ref.at[:, d], sems.at[2 + d]) for d in range(4)]
     for load in loads:
         load.start()
     loads[0].wait()
@@ -62,15 +66,16 @@
         a_out[128 * d : 128 * d + 128] = jnp.where(odd, top, bottom)
         b_out[128 * d : 128 * d + 128] = jnp.where(odd, bottom, top)
     near = jnp.where(dep == 0, cots[1], cots[0])
-    diag_a_out[...] = jnp.where(odd, near[:, :128], near[:, 384:])
+    diag_a_out[:128] = jnp.where(odd, near[:, :128], near[:, 384:])
+    diag_a_out[128:] = jnp.zeros((384, 128), BF16)
     diag_b_out[...] = jnp.where(odd, near[:, 384:], near[:, :128])
     for t in range(4):
         side_out[128 * t : 128 * t + 128] = near[:, 128 * t : 128 * t + 128]
     loads[1].wait()
     layer = jnp.swapaxes(act_ref[...].astype(F32), 0, 1).astype(BF16)
     side_out[512:] = layer.reshape(512, 128)
-    loads[2].wait()
     for d in range(4):
+        loads[2 + d].wait()
         first, final = pre_ref[:, d, 0, :], pre_ref[:, d, 15, :]
         place = slice(256 + 64 * d, 320 + 64 * d)
         a_out[place] = jnp.where(odd, first, final)
@@ -84,7 +89,13 @@
     return before, rows, after
 
 
-def prepare(pre_ref, act_ref, w2_ref, w3_ref, m2_ref, m3_ref, pre_out, pooled_out, act_out, w2_out, w3_out, m_out, t2):
+def prepare(pre_ref, act_ref, w2_ref, w3_far, m2_ref, m3_ref, pre_out, pooled_out, act_out, w2_out, w3_out, m_out,
+            t2, w3_ref, sems):
+    loads = []
+    for i in range(6):
+        rows = slice(288 * i, 288 * i + 288)
+        loads.append(pltpu.make_async_copy(w3_far.at[rows], w3_ref.at[rows], sems.at[i]))
+        loads[i].start()
     for d in range(4):
         pre_out[d] = jnp.swapaxes(pre_ref[:, d].astype(F32), 0, 1).astype(BF16)
     m_out[...] = jnp.zeros((24, 128), F32)
@@ -119,6 +130,8 @@
             start = 96 * d + 32 * ow
             act_out[:, start : start + 32, :] = value.astype(BF16)
     t2[...] = jnp.transpose(w2_ref[...])
+    for load in loads:
+        load.wait()
     for kd in range(3):
         for oh in range(3):
             for ow in range(3):
@@ -139,7 +152,7 @@
                 w2_out[start : start + 32, 256 * ow : 256 * ow + 256] = jnp.concatenate(blocks, axis=1).astype(BF16)
 
 
-def coarse(scale, own_ref, side_ref, a_ref, b_ref, da_ref, db_ref, w3_ref, pooled_ref,
+def coarse(scale, own_ref, side_ref, a_ref, da_ref, b_ref, db_ref, w3_ref, pooled_ref,
            back_out, grad_out, s_buf, back, parts, t3):
     dep = lax.axis_index("depth")
     hgt = lax.axis_index("height")
@@ -165,7 +178,7 @@
     for z in range(2):
         rows = slice(128 * z, 128 * z + 128)
         taps(z, slice_of([own_ref[z]], a_ref[rows], b_ref[rows]))
-    taps(2, slice_of([side_ref[128 * t : 128 * t + 128] for t in range(4)], da_ref[...], db_ref[...]))
+    taps(2, slice_of([side_ref[128 * t : 128 * t + 128] for t in range(4)], da_ref[:128], db_ref[...]))
     y0 = dot_nn(w3_ref[64:192, :], s_buf[0])
     y1 = dot_nn(w3_ref[0:128, :], s_buf[1])
     back[0] = y0[:64] + y1[:64]
@@ -220,8 +233,8 @@
             z_out[f, h] = jnp.where(pre.astype(F32) > 0, up, SLOPE * up).astype(BF16)
 
 
-def fine(back_ref, pre_ref, a_ref, b_ref, act_ref, side_ref, three_ref, m_ref,
-         parts_out, z_out, upper, near, parts, t2, stage):
+def fine(back_ref, pre_ref, a_ref, b_ref, act_ref, side_ref, three_ref,
+         mine_out, theirs_out, z_out, upper, near, parts, t2, stage):
     dep = lax.axis_index("depth")
     cotangent(back_ref, a_ref, b_ref, lambda f: pre_ref.at[f], upper, z_out)
     layer = side_ref[512:].astype(F32).reshape(16, 32, 128)
@@ -266,14 +279,30 @@
             stage[pl.ds(half, 64, stride=2), b, :] = block
     for b in range(14):
         stage[:, 4 + b, :] = three_ref[b]
-    stage[:, 18:, :] = jnp.broadcast_to(m_ref[:6][None], (128, 6, 128))
-    parts_out[...] = stage[...].astype(BF16)
-
-
-def into(back_ref, pre_ref, a_ref, b_ref, w2_ref, rows, ship, z_ref, upper):
+    stage[:, 18:, :] = jnp.zeros((128, 6, 128), F32)
+    core = lax.rem(lax.axis_index("dp"), 2)
+    for x in range(4):
+        place = slice(16 * x, 16 * x + 16)
+        mine_out[place] = stage[pl.ds(32 * x + 16 * core, 16)]
+        theirs_out[place] = stage[pl.ds(32 * x + 16 * (1 - core), 16)].astype(BF16)
+
+
+def combine(mine_ref, got_ref, parts_far, packed, sems):
+    leave = []
+    for i in range(4):
+        piece = slice(16 * i, 16 * i + 16)
+        packed[piece] = (mine_ref[piece] + got_ref[piece].astype(F32)).astype(BF16)
+        leave.append(pltpu.make_async_copy(packed.at[piece], parts_far.at[piece], sems.at[i]))
+        leave[i].start()
+    for copy in leave:
+        copy.wait()
+
+
+def into(back_ref, pre_ref, a_ref, b_ref, w2_ref, rows_far, ship, z_ref, upper, rows, sems):
     dep = lax.axis_index("depth")
     cotangent(back_ref, a_ref, b_ref, lambda f: jnp.swapaxes(pre_ref[:, f].astype(F32), 0, 1), upper, z_ref)
     lane = lax.broadcasted_iota(jnp.int32, (256, 128), 1)
+    leave = []
     for jp in range(4):
         acc = [None] * 6
         for z in range(4):
@@ -295,6 +324,11 @@
                 ship[h] = jnp.where(dep == 0, acc[5][block], acc[0][block]).astype(BF16)
                 for d in range(4):
                     rows[d, h] = acc[d + 1][block]
+        piece = (slice(None), slice(4 * jp, 4 * jp + 4))
+        leave.append(pltpu.make_async_copy(rows.at[piece], rows_far.at[piece], sems.at[jp]))
+        leave[jp].start()
+    for copy in leave:
+        copy.wait()
 
 
 def finish(scale, rows_ref, ship_ref, out_ref):
@@ -306,35 +340,42 @@
         out_ref[:, d] = (scale * jnp.swapaxes(rows, 0, 1)).astype(BF16)
 
 
-def reduce(scale_two, scale_three, parts_ref, m_ref, send_out, own_out, rows):
+def reduce(scale_two, scale_three, parts_ref, m_ref, send_far, own_out, rows, block, sems):
     total = jnp.sum(parts_ref[:, :18, :].astype(F32), axis=0)
     row = lax.broadcasted_iota(jnp.int32, (18, 128), 0)
     total = total * jnp.where(row < 4, scale_two, scale_three)
     own_out[...] = total
     rows[:18] = total
-    rows[18:30] = m_ref[6:18]
-    rows[30:] = jnp.zeros((2, 128), F32)
-    send_out[...] = jnp.broadcast_to(rows[...].astype(BF16)[None], (128, 32, 128))
-
-
-def update(full_ref, first_ref, own_ref, w2_ref, w3_ref, m2_ref, m3_ref, w2_out, w3_out, m2_out, m3_out, stage):
+    rows[18:36] = m_ref[:18]
+    rows[36:] = jnp.zeros((4, 128), F32)
+    block[...] = jnp.broadcast_to(rows[...].astype(BF16)[None], (16, 40, 128))
+    leave = [pltpu.make_async_copy(block, send_far.at[16 * i : 16 * i + 16], sems.at[i]) for i in range(4)]
+    for copy in leave:
+        copy.start()
+    for copy in leave:
+        copy.wait()
+
+
+def update(full_ref, other_ref, own_ref, w2_ref, w3_ref, m2_ref, m3_ref, w2_out, w3_out, m2_out, m3_out, stage):
     w2 = w2_ref[...]
     w3 = w3_ref[...]
-    grad = full_ref[:, :18, :].astype(F32)
-    square = jnp.sum(grad * grad, axis=0)
+    both = full_ref, other_ref
+    grads = [ref[:, :18, :].astype(F32) for ref in both]
+    square = sum(jnp.sum(grad * grad, axis=0) for grad in grads)
     row = lax.broadcasted_iota(jnp.int32, (18, 128), 0)
     norm_two = jnp.sqrt(jnp.sum(jnp.where(row < 4, square, 0.0), keepdims=True))
     norm_three = jnp.sqrt(jnp.sum(jnp.where(row < 4, 0.0, square), keepdims=True))
     rate_two = LEARN * (TRUST * jnp.sqrt(jnp.sum(w2 * w2, keepdims=True)) / (norm_two + EPSILON))
     rate_three = LEARN * (TRUST * jnp.sqrt(jnp.sum(w3 * w3, keepdims=True)) / (norm_three + EPSILON))
     rate = jnp.where(row < 4, rate_two, rate_three)
-    stage[:, :6, :] = MOMENTUM * first_ref[:, 18:, :].astype(F32)
-    stage[:, 6:, :] = MOMENTUM * full_ref[:, 18:30, :].astype(F32)
-    stage[...] += rate[None] * grad
-    for b in range(13):
-        rows = slice(128 * b, 128 * b + 128)
-        w3_out[rows] = w3[rows] - jnp.transpose(stage[:, 4 + b, :])
-    w3_out[1664:] = w3[1664:] - jnp.transpose(stage[:, 17, :])[:64]
+    core = lax.rem(lax.axis_index("dp"), 2)
+    for ref, grad, side in zip(both, grads, (core, 1 - core)):
+        moved = MOMENTUM * ref[:, 18:36, :].astype(F32) + rate[None] * grad
+        for x in range(4):
+            stage[pl.ds(32 * x + 16 * side, 16)] = moved[16 * x : 16 * x + 16]
+    for b in range(14):
+        rows = slice(128 * b, min(128 * b + 128, 1728))
+        w3_out[rows] = w3[rows] - jnp.transpose(stage[:, 4 + b, :])[: rows.stop - rows.start]
     halves = []
     for half in range(2):
         blocks = [stage[pl.ds(half, 64, stride=2), b, :] for b in range(4)]
@@ -358,10 +399,10 @@
     cot_rows, send_side, send_a, send_b, send_da, send_db = call(
         arrange,
         [((2, 128, 512), BF16), ((1024, 128), BF16), ((512, 128), BF16),
-         ((512, 128), BF16), ((128, 128), BF16), ((128, 128), BF16)],
+         ((512, 128), BF16), ((512, 128), BF16), ((128, 128), BF16)],
         [pltpu.VMEM((128, 2, 512), BF16), pltpu.VMEM((64, 4, 16, 128), BF16), pltpu.VMEM((32, 16, 128), BF16),
-         pltpu.SemaphoreType.DMA((3,))],
-        moved=4_000_000, far=3, limit=62,
+         pltpu.SemaphoreType.DMA((6,))],
+        moved=4_000_000, far=(0, 1, 2),
     )(cot, pre, act)
     tall = lax.axis_size("height")
     swap = [(0, 1), (1, 0)]
@@ -372,15 +413,15 @@
     )
     side = lax.ppermute(send_side, "depth", swap)
     got_a = lax.ppermute(send_a, "height", pairs_a)
+    got_da = lax.ppermute(send_da, ("depth", "height"), cross_a)
     got_b = lax.ppermute(send_b, "height", pairs_b)
-    got_da = lax.ppermute(send_da, ("depth", "height"), cross_a)
     got_db = lax.ppermute(send_db, ("depth", "height"), cross_b)
 
     pre_rows, pooled, acts, wide_two, wide_three, moments = call(
         prepare,
         [((4, 16, 64, 128), BF16), ((128, 512), BF16), ((16, 384, 128), BF16), ((192, 768), BF16), ((192, 1152), BF16), ((24, 128), F32)],
-        [pltpu.VMEM((864, 64), F32)],
-        flops=100_000_000, moved=8_000_000,
+        [pltpu.VMEM((864, 64), F32), pltpu.VMEM((1728, 128), F32), pltpu.SemaphoreType.DMA((6,))],
+        flops=100_000_000, moved=8_000_000, far=(3,),
     )(pre, act, weight_two, weight_three.T, moment_two, moment_three)
 
     back, part_three = call(
@@ -389,22 +430,33 @@
         [pltpu.VMEM((3, 1152, 768), BF16), pltpu.VMEM((2, 64, 768), F32), pltpu.VMEM((3, 64, 1152), F32),
          pltpu.VMEM((1792, 128), F32)],
         flops=2_000_000_000, moved=4_000_000,
-    )(cot_rows, side, got_a, got_b, got_da, got_db, wide_three, pooled)
-
-    parts, = call(
+    )(cot_rows, side, got_a, got_da, got_b, got_db, wide_three, pooled)
+
+    mine, theirs = call(
         fine,
-        [((128, 24, 128), BF16)],
+        [((64, 24, 128), F32), ((64, 24, 128), BF16)],
         [pltpu.VMEM((4, 18, 64, 128), BF16), pltpu.VMEM((2, 10, 64, 128), F32), pltpu.VMEM((16, 96, 128), BF16), pltpu.VMEM((3, 96, 192), F32),
          pltpu.VMEM((944, 64), F32), pltpu.VMEM((128, 24, 128), F32)],
         flops=2_000_000_000, moved=6_000_000,
-    )(back, pre_rows, got_a, got_b, acts, side, part_three, moments)
-
-    parts = lax.all_to_all(parts, AXES, 0, 0, tiled=True)
+    )(back, pre_rows, got_a, got_b, acts, side, part_three)
+
+    cores = [(i, i ^ 1) for i in range(lax.axis_size("dp"))]
+    plane = lax.axis_size(("depth", "height"))
+    groups = [[i * plane + j for i in range(k, lax.axis_size("dp"), 2) for j in range(plane)] for k in range(2)]
+    got = lax.ppermute(theirs, "dp", cores)
+    parts, = call(
+        combine,
+        [((64, 24, 128), BF16)],
+        [pltpu.VMEM((64, 24, 128), BF16), pltpu.SemaphoreType.DMA((4,))],
+        moved=2_000_000, far_out=(0,),
+    )(mine, got)
+    parts = lax.all_to_all(parts, AXES, 0, 0, axis_index_groups=groups, tiled=True)
     into_rows, ship = call(
         into,
         [((4, 16, 32, 128), F32), ((16, 32, 128), BF16)],
-        [pltpu.VMEM((4, 18, 64, 128), BF16), pltpu.VMEM((2, 10, 64, 128), F32)],
-        flops=4_000_000_000, moved=6_000_000,
+        [pltpu.VMEM((4, 18, 64, 128), BF16), pltpu.VMEM((2, 10, 64, 128), F32), pltpu.VMEM((4, 16, 32, 128), F32),
+         pltpu.SemaphoreType.DMA((4,))],
+        flops=4_000_000_000, moved=6_000_000, far_out=(0,),
     )(back, pre, got_a, got_b, wide_two)
     ship = lax.ppermute(ship, "depth", swap)
     parts, into_rows, ship = lax.optimization_barrier((parts, into_rows, ship))
@@ -416,18 +468,19 @@
 
     send, own = call(
         lambda *refs: reduce(scale_two / volumes, scale_three / volumes, *refs),
-        [((128, 32, 128), BF16), ((18, 128), F32)],
-        [pltpu.VMEM((32, 128), F32)],
-        moved=2_000_000,
+        [((64, 40, 128), BF16), ((18, 128), F32)],
+        [pltpu.VMEM((40, 128), F32), pltpu.VMEM((16, 40, 128), BF16), pltpu.SemaphoreType.DMA((4,))],
+        moved=2_000_000, far_out=(0,),
     )(parts, moments)
     own, w2, w3 = lax.optimization_barrier((own, weight_two, weight_three))
-    full = lax.all_to_all(send, AXES, 0, 0, tiled=True)
+    full = lax.all_to_all(send, AXES, 0, 0, axis_index_groups=groups, tiled=True)
+    other = lax.ppermute(full, "dp", cores)
     new_weight_two, new_weight_three, new_moment_two, new_moment_three = call(
         update,
         [(weight_two.shape, F32), (weight_three.shape[::-1], F32), (moment_two.shape, F32), (moment_three.shape, F32)],
         [pltpu.VMEM((128, 18, 128), F32)],
         moved=4_000_000,
-    )(full, parts, own, w2, w3.T, moment_two, moment_three)
+    )(full, other, own, w2, w3.T, moment_two, moment_three)
     return (grad_input[None], new_weight_two, new_weight_three.T, new_moment_two, new_moment_three)
 
 

time: 84.4 us -> 79.5 us (0.942)
  blocking collectives: 0 us -> 19.3 us
  waiting for transfers between devices: 29 us -> 13.2 us
  starting transfers between devices: 31.7 us -> 24.9 us
  local copies, waits for them, and re-layouts: 5.22 us -> 0.03 us
  Pallas kernels: 17.2 us -> 20.9 us
    all_to_all x2 -> x1, waiting for transfers between devices: 20.7 us -> 0.8 us  [local(): lax.all_to_all(parts, AXES, 0, 0, axis_index_groups=groups, tiled=True)]
    all_to_all x0 -> x1, blocking collectives: none -> 19.3 us  [local(): lax.all_to_all(send, AXES, 0, 0, axis_index_groups=groups, tiled=True)]
    all_to_all x2 -> x1, starting transfers between devices: 19.3 us -> 10.3 us  [local(): lax.all_to_all(parts, AXES, 0, 0, axis_index_groups=groups, tiled=True)]
    ppermute x0 -> x2, starting transfers between devices: none -> 7.46 us  [the longest x1 4.58 us: local(): got = lax.ppermute(theirs, 'dp', cores)]
    unnamed x28 -> x14, local copies, waits for them, and re-layouts: 5.22 us -> 0.03 us
    ppermute x1, starting transfers between devices: 4.92 us -> 0.01 us  [local(): got_da = lax.ppermute(send_da, ('depth', 'height'), cross_a)]
    ppermute x1, waiting for transfers between devices: 0.01 us -> 4.2 us  [local(): got_a = lax.ppermute(send_a, 'height', pairs_a)]
    pallas_call x8 -> x9, Pallas kernels: 17.2 us -> 20.9 us  [run(): pl.pallas_call(body, out_shape=[pltpu.HBM(shape, dtype) if i in far_out e...]
  transfers between devices with their start and end apart: 8 -> 9, of which waited for: 3 -> 5; matrix products, arithmetic and copies ran while one was open for 0% -> 0% of each run, Pallas kernels for 6% -> 9%
where the time goes in v5:
time: 79.5 us; the launch traced here: 79.1 us
  starting transfers between devices  24.9 us (31%)
  Pallas kernels  20.9 us (26%)
  blocking collectives  19.3 us (24%)
  waiting for transfers between devices  13.2 us (17%)
  between operations  0.83 us (1%)
    pallas_call x9, Pallas kernels, run(): pl.pallas_call(body, out_shape=[pltpu.HBM(shape, dtype) if i in far_out e...  20.9 us
    all_to_all x1, blocking collectives, local(): lax.all_to_all(send, AXES, 0, 0, axis_index_groups=groups, tiled=True)  19.3 us
    all_to_all x1, starting transfers between devices, local(): lax.all_to_all(parts, AXES, 0, 0, axis_index_groups=groups, tiled=True)  10.3 us
    ppermute x1, waiting for transfers between devices, local(): ship = lax.ppermute(ship, 'depth', swap)  6.23 us
    ppermute x1, starting transfers between devices, local(): got = lax.ppermute(theirs, 'dp', cores)  4.58 us
    ppermute x1, waiting for transfers between devices, local(): got_a = lax.ppermute(send_a, 'height', pairs_a)  4.2 us
    ppermute x1, starting transfers between devices, local(): other = lax.ppermute(full, 'dp', cores)  2.88 us
    ppermute x1, starting transfers between devices, local(): got_a = lax.ppermute(send_a, 'height', pairs_a)  2.62 us
  transfers between devices with their start and end apart: 9, of which 5 were waited for; matrix products, arithmetic and copies ran while one was open for 0% of the time, Pallas kernels for 9%

profile of v5, /device:TPU:1, one launch (start us, length us, event | category | flops | bytes accessed | tf_op | source)
XLA Modules:
  0.0 79.1 jit_solution(17858037935480510265)
XLA Ops:
  0.6 0.0 copy-start
  0.7 3.2 %shard_map.110 = (bf16[2,128,512]{2,1,0:T(8,128)(2,1)S(1)}, bf16[1024,128]{1,0:T(8,128)(2,1)S(1)}, bf16[512,128]{1,0:T(8,128)(2,1)S(1)}, bf16[512,128]{1,0:T(8,1...) custom-call(bf16[128,2,512]{2,1,0:T(2,128)(2,1)} %bitcast.15, bf16[64,4,16,128]{3,2,1,0:T(8,128)(2,1)} %bitcast.7, ...), custom_call_target="tpu_custom_call" | custom-call | bytes 4000000 | tf_op jit(solution)/shard_map/pallas_call | solution.py:20
  3.9 2.2 %collective-permute-start = (bf16[1024,128]{1,0:T(8,128)(2,1)S(1)}, bf16[1024,128]{1,0:T(8,128)(2,1)S(1)}, u32[]{:S(2)}, u32[]{:S(2)}) collective-permute-start(bf16[1024,128]{1,0:T(8,128)(2,1)S(1)} %get-tuple-element.36), channel_id=1, source_target_pairs={{0,8},{8,0},{1,9},{9,1},{2,10},{10,2},{3,11},{11,3},{4,12},{12,4},... | collective-permute-start | bytes 786440 | tf_op jit(solution)/shard_map/ppermute | solution.py:414
  6.1 2.6 %collective-permute-start.1 = (bf16[512,128]{1,0:T(8,128)(2,1)S(1)}, bf16[512,128]{1,0:T(8,128)(2,1)S(1)}, u32[]{:S(2)}, u32[]{:S(2)}) collective-permute-start(bf16[512,128]{1,0:T(8,128)(2,1)S(1)} %get-tuple-element.37), channel_id=1, source_target_pairs={{0,1},{1,0},{2,3},{3,2},{4,5},{5,4},{6,7},{7,6},{8,9},{9,8},{10,11... | collective-permute-start | bytes 393224 | tf_op jit(solution)/shard_map/ppermute | solution.py:415
  8.8 0.0 collective-permute-start.2
  8.8 0.7 collective-permute-start.3
  9.4 0.7 collective-permute-start.4
  10.2 2.9 %shard_map.111 = (bf16[4,16,64,128]{3,2,1,0:T(8,128)(2,1)S(1)}, bf16[128,512]{1,0:T(8,128)(2,1)S(1)}, bf16[16,384,128]{2,1,0:T(8,128)(2,1)S(1)}, bf16[192,768]{1...) custom-call(bf16[64,4,16,128]{3,2,1,0:T(8,128)(2,1)S(1)} %bitcast.8, ...), custom_call_target="tpu_custom_call" | custom-call | flops 100000000 | bytes 8000000 | tf_op jit(solution)/shard_map/pallas_call | solution.py:20
  13.1 0.0 collective-permute-done.4.refs_5_
  13.1 4.2 %collective-permute-done.1.refs_2_.a_ref = bf16[512,128]{1,0:T(8,128)(2,1)S(1)} collective-permute-done((bf16[512,128]{1,0:T(8,128)(2,1)S(1)}, bf16[512,128]{1,0:T(8,128)(2,1)S(1)}, u32[]{:S(2)}, u32[]{:S(2)}) %collective-permute-start.1) | collective-permute-done | bytes 131104 | tf_op jit(solution)/shard_map/ppermute | solution.py:415
  17.3 0.0 collective-permute-done.2.refs_3_
  17.3 0.0 collective-permute-done.3.refs_4_.b_ref
  17.3 0.0 collective-permute-done.refs_1_.side_ref
  17.3 2.8 %shard_map.112 = (bf16[2,64,768]{2,1,0:T(8,128)(2,1)S(1)}, f32[14,128,128]{2,1,0:T(8,128)S(1)}) custom-call(bf16[2,128,512]{2,1,0:T(8,128)(2,1)S(1)} %get-tuple-element.35.refs_0_, bf16[1024,128]{1,0:T(8,128)(2,1)S(1)} %collective-permute-done.refs_1_.side_ref, bf16[512,128]{1,0:T(8,128)(2,1)S(1)} %collective-permute-done.1.refs_2_.a_ref, ...), custom_call_target="tpu_custom_call" | custom-call | flops 2000000000 | bytes 4000000 | tf_op jit(solution)/shard_map/pallas_call | solution.py:20
  20.2 3.1 %shard_map.113 = (f32[64,24,128]{2,1,0:T(8,128)S(1)}, bf16[64,24,128]{2,1,0:T(8,128)(2,1)S(1)}) custom-call(bf16[2,64,768]{2,1,0:T(8,128)(2,1)S(1)} %get-tuple-element.43.back_ref, bf16[4,16,64,128]{3,2,1,0:T(8,128)(2,1)S(1)} %get-tuple-element.44.pre_ref, bf16[512,128]{1,0:T(8,128)(2,1)S(1)} %collective-permute-done.1.refs_2_.a_ref, ...), custom_call_target="tpu_custom_call" | custom-call | flops 2000000000 | bytes 6000000 | tf_op jit(solution)/shard_map/pallas_call | solution.py:20
  23.3 4.6 %collective-permute-start.5 = (bf16[64,24,128]{2,1,0:T(8,128)(2,1)S(1)}, bf16[64,24,128]{2,1,0:T(8,128)(2,1)S(1)}, u32[]{:S(2)}, u32[]{:S(2)}) collective-permute-start(bf16[64,24,128]{2,1,0:T(8,128)(2,1)S(1)} %get-tuple-element.48), channel_id=1, source_target_pairs={{0,16},{16,0},{32,48},{48,32},{64,80},{80,64},{96,112},{112,96},{1... | collective-permute-start | bytes 1179656 | tf_op jit(solution)/shard_map/ppermute | solution.py:446
  27.8 1.3 %collective-permute-done.5.got_ref = bf16[64,24,128]{2,1,0:T(8,128)(2,1)S(1)} collective-permute-done((bf16[64,24,128]{2,1,0:T(8,128)(2,1)S(1)}, bf16[64,24,128]{2,1,0:T(8,128)(2,1)S(1)}, u32[]{:S(2)}, u32[]{:S(2)}) %collective-permute-start.5) | collective-permute-done | bytes 393248 | tf_op jit(solution)/shard_map/ppermute | solution.py:446
  29.2 0.8 shard_map.114
  30.0 10.3 %all-to-all-start = ((bf16[64,24,128]{2,1,0:T(8,128)(2,1)}), bf16[64,24,128]{2,1,0:T(8,128)(2,1)S(1)}, u32[]{:S(2)}, u32[]{:S(2)}) async-start(bf16[64,24,128]{2,1,0:T(8,128)(2,1)} %shard_map.114), calls=%async_computation | async-start | bytes 786432 | tf_op jit(solution)/shard_map/all_to_all | solution.py:453
  40.3 3.1 %shard_map.115 = (f32[4,16,32,128]{3,2,1,0:T(8,128)}, bf16[16,32,128]{2,1,0:T(8,128)(2,1)S(1)}) custom-call(bf16[2,64,768]{2,1,0:T(8,128)(2,1)S(1)} %get-tuple-element.43.back_ref, bf16[64,4,16,128]{3,2,1,0:T(8,128)(2,1)S(1)} %bitcast.9, bf16[512,128]{1,0:T(8,128)(2,1)S(1)} %collective-permute-done.1.refs_2_.a_ref, ...), custom_call_target="tpu_custom_call" | custom-call | flops 4000000000 | bytes 6000000 | tf_op jit(solution)/shard_map/pallas_call | solution.py:20
  43.5 0.0 copy-start.3
  43.5 0.9 %collective-permute-start.6 = (bf16[16,32,128]{2,1,0:T(8,128)(2,1)S(1)}, bf16[16,32,128]{2,1,0:T(8,128)(2,1)S(1)}, u32[]{:S(2)}, u32[]{:S(2)}) collective-permute-start(bf16[16,32,128]{2,1,0:T(8,128)(2,1)S(1)} %get-tuple-element.51), channel_id=1, source_target_pairs={{0,8},{8,0},{1,9},{9,1},{2,10},{10,2},{3,11},{11,3},{4,12},{12,4},... | collective-permute-start | bytes 393224 | tf_op jit(solution)/shard_map/ppermute | solution.py:461
  44.4 6.2 %collective-permute-done.6.refs_1_ = bf16[16,32,128]{2,1,0:T(8,128)(2,1)S(1)} collective-permute-done((bf16[16,32,128]{2,1,0:T(8,128)(2,1)S(1)}, bf16[16,32,128]{2,1,0:T(8,128)(2,1)S(1)}, u32[]{:S(2)}, u32[]{:S(2)}) %collective-permute-start.6) | collective-permute-done | bytes 131104 | tf_op jit(solution)/shard_map/ppermute | solution.py:461
  50.6 0.8 %all-to-all-done.refs_0_ = bf16[64,24,128]{2,1,0:T(8,128)(2,1)S(1)} async-done(((bf16[64,24,128]{2,1,0:T(8,128)(2,1)}), bf16[64,24,128]{2,1,0:T(8,128)(2,1)S(1)}, u32[]{:S(2)}, u32[]{:S(2)}) %all-to-all-start) | async-done | bytes 393248 | tf_op jit(solution)/shard_map/all_to_all | solution.py:453
  51.4 1.0 %shard_map.117 = (bf16[64,40,128]{2,1,0:T(8,128)(2,1)}, f32[18,128]{1,0:T(8,128)S(1)}) custom-call(bf16[64,24,128]{2,1,0:T(8,128)(2,1)S(1)} %all-to-all-done.refs_0_, f32[24,128]{1,0:T(8,128)S(1)} %get-tuple-element.55.refs_1_), custom_call_target="tpu_custom_call" | custom-call | bytes 2000000 | tf_op jit(solution)/shard_map/pallas_call | solution.py:20
  52.4 0.0 copy-start.1
  52.4 19.3 %all_to_all.10.full_ref = bf16[64,40,128]{2,1,0:T(8,128)(2,1)S(1)} all-to-all(bf16[64,40,128]{2,1,0:T(8,128)(2,1)} %get-tuple-element.56), channel_id=1, replica_groups={{0,1,2,3,4,5,6,7,8,9,10,11,12,13,14,15,32,33,34,35,36,37,38,39,40,41,42..., dimensions={0} | all-to-all | bytes 1310720 | tf_op jit(solution)/shard_map/all_to_all | solution.py:476
  71.7 2.9 %collective-permute-start.7 = (bf16[64,40,128]{2,1,0:T(8,128)(2,1)S(1)}, bf16[64,40,128]{2,1,0:T(8,128)(2,1)S(1)}, u32[]{:S(2)}, u32[]{:S(2)}) collective-permute-start(bf16[64,40,128]{2,1,0:T(8,128)(2,1)S(1)} %all_to_all.10.full_ref), channel_id=1, source_target_pairs={{0,16},{16,0},{32,48},{48,32},{64,80},{80,64},{96,112},{112,96},{1... | collective-permute-start | bytes 1966088 | tf_op jit(solution)/shard_map/ppermute | solution.py:477
  74.6 1.1 %shard_map.116 = bf16[32,4,16,128]{3,2,1,0:T(8,128)(2,1)} custom-call(f32[4,16,32,128]{3,2,1,0:T(8,128)S(1)} %copy-done.3, bf16[16,32,128]{2,1,0:T(8,128)(2,1)S(1)} %collective-permute-done.6.refs_1_), custom_call_target="tpu_custom_call" | custom-call | bytes 2000000 | tf_op jit(solution)/shard_map/pallas_call | solution.py:20
  75.7 0.6 collective-permute-done.7.other_ref
  76.3 0.0 copy-done.1
  76.3 2.8 %shard_map.118 = (f32[64,864]{1,0:T(8,128)}, f32[1728,128]{1,0:T(8,128)}, f32[432]{0:T(512)}, f32[1728]{0:T(1024)}) custom-call(bf16[64,40,128]{2,1,0:T(8,128)(2,1)S(1)} %all_to_all.10.full_ref, bf16[64,40,128]{2,1,0:T(8,128)(2,1)S(1)} %collective-permute-done.7.other_ref, f32[18,128]{1,0:T(8,128)S(1)} %get-tuple-element.58.own_ref, ...), custom_call_target="tpu_custom_call" | custom-call | bytes 4000000 | tf_op jit(solution)/shard_map/pallas_call | solution.py:20
  (10 shorter events, 0.0 us)
Async XLA Ops:
  0.6 9.5 %copy-start = (bf16[1,64,4,16,128]{4,3,2,1,0:T(8,128)(2,1)S(1)}, bf16[1,64,4,16,128]{4,3,2,1,0:T(8,128)(2,1)}, u32[]{:S(2)}) copy-start(bf16[1,64,4,16,128]{4,3,2,1,0:T(8,128)(2,1)} %param.8) | copy-start | bytes 3145732
  0.6 9.5 %copy-start.2 = (bf16[1,32,4,16,128]{4,3,2,1,0:T(8,128)(2,1)S(1)}, bf16[1,32,4,16,128]{4,3,2,1,0:T(8,128)(2,1)}, u32[]{:S(2)}) copy-start(bf16[1,32,4,16,128]{4,3,2,1,0:T(8,128)(2,1)} %param.7) | copy-start | bytes 1572868
  0.7 9.5 %copy-start.5 = (f32[1728]{0:T(1024)S(1)}, f32[1728]{0:T(1024)}, u32[]{:S(2)}) copy-start(f32[1728]{0:T(1024)} %m3_ref.3) | copy-start | bytes 20740
  0.7 9.5 %copy-start.6 = (f32[432]{0:T(512)S(1)}, f32[432]{0:T(512)}, u32[]{:S(2)}) copy-start(f32[432]{0:T(512)} %m2_ref.3) | copy-start | bytes 5188
  0.7 9.5 %copy-start.4 = (f32[64,864]{1,0:T(8,128)S(1)}, f32[64,864]{1,0:T(8,128)}, u32[]{:S(2)}) copy-start(f32[64,864]{1,0:T(8,128)} %w2_ref.2) | copy-start | bytes 663556
  3.9 13.4 %collective-permute-start = (bf16[1024,128]{1,0:T(8,128)(2,1)S(1)}, bf16[1024,128]{1,0:T(8,128)(2,1)S(1)}, u32[]{:S(2)}, u32[]{:S(2)}) collective-permute-start(bf16[1024,128]{1,0:T(8,128)(2,1)S(1)} %get-tuple-element.36), channel_id=1, source_target_pairs={{0,8},{8,0},{1,9},{9,1},{2,10},{10,2},{3,11},{11,3},{4,12},{12,4},... | collective-permute-start | bytes 786440 | tf_op jit(solution)/shard_map/ppermute | solution.py:414
  6.1 11.1 %collective-permute-start.1 = (bf16[512,128]{1,0:T(8,128)(2,1)S(1)}, bf16[512,128]{1,0:T(8,128)(2,1)S(1)}, u32[]{:S(2)}, u32[]{:S(2)}) collective-permute-start(bf16[512,128]{1,0:T(8,128)(2,1)S(1)} %get-tuple-element.37), channel_id=1, source_target_pairs={{0,1},{1,0},{2,3},{3,2},{4,5},{5,4},{6,7},{7,6},{8,9},{9,8},{10,11... | collective-permute-start | bytes 393224 | tf_op jit(solution)/shard_map/ppermute | solution.py:415
  8.8 8.5 %collective-permute-start.2 = (bf16[512,128]{1,0:T(8,128)(2,1)S(1)}, bf16[512,128]{1,0:T(8,128)(2,1)S(1)}, u32[]{:S(2)}, u32[]{:S(2)}) collective-permute-start(bf16[512,128]{1,0:T(8,128)(2,1)S(1)} %get-tuple-element.38), channel_id=1, source_target_pairs={{0,9},{1,8},{2,11},{3,10},{4,13},{5,12},{6,15},{7,14},{8,1},{9,0},... | collective-permute-start | bytes 393224 | tf_op jit(solution)/shard_map/ppermute | solution.py:416
  8.8 8.5 %collective-permute-start.3 = (bf16[512,128]{1,0:T(8,128)(2,1)S(1)}, bf16[512,128]{1,0:T(8,128)(2,1)S(1)}, u32[]{:S(2)}, u32[]{:S(2)}) collective-permute-start(bf16[512,128]{1,0:T(8,128)(2,1)S(1)} %get-tuple-element.39), channel_id=1, source_target_pairs={{1,2},{2,1},{3,4},{4,3},{5,6},{6,5},{9,10},{10,9},{11,12},{12,11},... | collective-permute-start | bytes 393224 | tf_op jit(solution)/shard_map/ppermute | solution.py:417
  9.4 3.6 %collective-permute-start.4 = (bf16[128,128]{1,0:T(8,128)(2,1)S(1)}, bf16[128,128]{1,0:T(8,128)(2,1)S(1)}, u32[]{:S(2)}, u32[]{:S(2)}) collective-permute-start(bf16[128,128]{1,0:T(8,128)(2,1)S(1)} %get-tuple-element.40), channel_id=1, source_target_pairs={{1,10},{2,9},{3,12},{4,11},{5,14},{6,13},{9,2},{10,1},{11,4},{12,3... | collective-permute-start | bytes 98312 | tf_op jit(solution)/shard_map/ppermute | solution.py:418
  23.3 5.9 %collective-permute-start.5 = (bf16[64,24,128]{2,1,0:T(8,128)(2,1)S(1)}, bf16[64,24,128]{2,1,0:T(8,128)(2,1)S(1)}, u32[]{:S(2)}, u32[]{:S(2)}) collective-permute-start(bf16[64,24,128]{2,1,0:T(8,128)(2,1)S(1)} %get-tuple-element.48), channel_id=1, source_target_pairs={{0,16},{16,0},{32,48},{48,32},{64,80},{80,64},{96,112},{112,96},{1... | collective-permute-start | bytes 1179656 | tf_op jit(solution)/shard_map/ppermute | solution.py:446
  30.0 21.4 %all-to-all-start = ((bf16[64,24,128]{2,1,0:T(8,128)(2,1)}), bf16[64,24,128]{2,1,0:T(8,128)(2,1)S(1)}, u32[]{:S(2)}, u32[]{:S(2)}) async-start(bf16[64,24,128]{2,1,0:T(8,128)(2,1)} %shard_map.114), calls=%async_computation | async-start | bytes 786432 | tf_op jit(solution)/shard_map/all_to_all | solution.py:453
  43.5 31.1 %copy-start.3 = (f32[4,16,32,128]{3,2,1,0:T(8,128)S(1)}, f32[4,16,32,128]{3,2,1,0:T(8,128)}, u32[]{:S(2)}) copy-start(f32[4,16,32,128]{3,2,1,0:T(8,128)} %get-tuple-element.52.refs_0_) | copy-start | bytes 3145732
  43.5 7.2 %collective-permute-start.6 = (bf16[16,32,128]{2,1,0:T(8,128)(2,1)S(1)}, bf16[16,32,128]{2,1,0:T(8,128)(2,1)S(1)}, u32[]{:S(2)}, u32[]{:S(2)}) collective-permute-start(bf16[16,32,128]{2,1,0:T(8,128)(2,1)S(1)} %get-tuple-element.51), channel_id=1, source_target_pairs={{0,8},{8,0},{1,9},{9,1},{2,10},{10,2},{3,11},{11,3},{4,12},{12,4},... | collective-permute-start | bytes 393224 | tf_op jit(solution)/shard_map/ppermute | solution.py:461
  52.4 23.9 %copy-start.1 = (f32[128,1728]{0,1:T(8,128)S(1)}, f32[128,1728]{0,1:T(8,128)}, u32[]{:S(2)}) copy-start(f32[128,1728]{0,1:T(8,128)} %param.11) | copy-start | bytes 2654212
  71.7 4.6 %collective-permute-start.7 = (bf16[64,40,128]{2,1,0:T(8,128)(2,1)S(1)}, bf16[64,40,128]{2,1,0:T(8,128)(2,1)S(1)}, u32[]{:S(2)}, u32[]{:S(2)}) collective-permute-start(bf16[64,40,128]{2,1,0:T(8,128)(2,1)S(1)} %all_to_all.10.full_ref), channel_id=1, source_target_pairs={{0,16},{16,0},{32,48},{48,32},{64,80},{80,64},{96,112},{112,96},{1... | collective-permute-start | bytes 1966088 | tf_op jit(solution)/shard_map/ppermute | solution.py:477

commit v6 on v5

--- a/solution.py
+++ b/solution.py
@@ -101,10 +101,10 @@
     m_out[...] = jnp.zeros((24, 128), F32)
     for b in range(3):
         m_out[b, :] = m2_ref[pl.ds(128 * b, 128)]
-    m_out[3, :48] = m2_ref[pl.ds(384, 48)]
     for b in range(13):
-        m_out[4 + b, :] = m3_ref[pl.ds(128 * b, 128)]
-    m_out[17, :64] = m3_ref[pl.ds(1664, 64)]
+        m_out[3 + b, :] = m3_ref[pl.ds(128 * b, 128)]
+    m_out[16, :64] = m3_ref[pl.ds(1664, 64)]
+    m_out[16, 64:112] = m2_ref[pl.ds(384, 48)]
     row = lax.broadcasted_iota(jnp.int32, (256, 128), 0)
     col = lax.broadcasted_iota(jnp.int32, (256, 128), 1)
     pool = jnp.where(row // 2 == col, 0.125, 0.0).astype(BF16)
@@ -233,7 +233,7 @@
             z_out[f, h] = jnp.where(pre.astype(F32) > 0, up, SLOPE * up).astype(BF16)
 
 
-def fine(back_ref, pre_ref, a_ref, b_ref, act_ref, side_ref, three_ref,
+def fine(back_ref, pre_ref, a_ref, b_ref, act_ref, side_ref, three_ref, m_ref,
          mine_out, theirs_out, z_out, upper, near, parts, t2, stage):
     dep = lax.axis_index("depth")
     cotangent(back_ref, a_ref, b_ref, lambda f: pre_ref.at[f], upper, z_out)
@@ -279,7 +279,8 @@
             stage[pl.ds(half, 64, stride=2), b, :] = block
     for b in range(14):
         stage[:, 4 + b, :] = three_ref[b]
-    stage[:, 18:, :] = jnp.zeros((128, 6, 128), F32)
+    stage[:, 18:21, :] = jnp.broadcast_to(m_ref[:3][None], (128, 3, 128))
+    stage[:, 21:, :] = jnp.zeros((128, 3, 128), F32)
     core = lax.rem(lax.axis_index("dp"), 2)
     for x in range(4):
         place = slice(16 * x, 16 * x + 16)
@@ -291,7 +292,9 @@
     leave = []
     for i in range(4):
         piece = slice(16 * i, 16 * i + 16)
-        packed[piece] = (mine_ref[piece] + got_ref[piece].astype(F32)).astype(BF16)
+        mine, got = mine_ref[piece], got_ref[piece].astype(F32)
+        rows = [mine[:, :18] + got[:, :18], mine[:, 18:21], got[:, 18:21]]
+        packed[piece] = jnp.concatenate(rows, axis=1).astype(BF16)
         leave.append(pltpu.make_async_copy(packed.at[piece], parts_far.at[piece], sems.at[i]))
         leave[i].start()
     for copy in leave:
@@ -346,9 +349,8 @@
     total = total * jnp.where(row < 4, scale_two, scale_three)
     own_out[...] = total
     rows[:18] = total
-    rows[18:36] = m_ref[:18]
-    rows[36:] = jnp.zeros((4, 128), F32)
-    block[...] = jnp.broadcast_to(rows[...].astype(BF16)[None], (16, 40, 128))
+    rows[18:] = m_ref[3:17]
+    block[...] = jnp.broadcast_to(rows[...].astype(BF16)[None], (16, 32, 128))
     leave = [pltpu.make_async_copy(block, send_far.at[16 * i : 16 * i + 16], sems.at[i]) for i in range(4)]
     for copy in leave:
         copy.start()
@@ -356,7 +358,7 @@
         copy.wait()
 
 
-def update(full_ref, other_ref, own_ref, w2_ref, w3_ref, m2_ref, m3_ref, w2_out, w3_out, m2_out, m3_out, stage):
+def update(full_ref, other_ref, first_ref, own_ref, w2_ref, w3_ref, m2_ref, m3_ref, w2_out, w3_out, m2_out, m3_out, stage):
     w2 = w2_ref[...]
     w3 = w3_ref[...]
     both = full_ref, other_ref
@@ -369,8 +371,15 @@
     rate_three = LEARN * (TRUST * jnp.sqrt(jnp.sum(w3 * w3, keepdims=True)) / (norm_three + EPSILON))
     rate = jnp.where(row < 4, rate_two, rate_three)
     core = lax.rem(lax.axis_index("dp"), 2)
-    for ref, grad, side in zip(both, grads, (core, 1 - core)):
-        moved = MOMENTUM * ref[:, 18:36, :].astype(F32) + rate[None] * grad
+    lane = lax.broadcasted_iota(jnp.int32, (64, 128), 1)
+    for n, (ref, grad, side) in enumerate(zip(both, grads, (core, 1 - core))):
+        head = first_ref[:, 18 + 3 * n : 21 + 3 * n, :].astype(F32)
+        rest = ref[:, 18:, :].astype(F32)
+        tails = rest[:, 13, :]
+        tail_two = jnp.where(lane < 48, shifted(tails, 64), 0.0)
+        tail_three = jnp.where(lane < 64, tails, 0.0)
+        moments = jnp.concatenate([head, tail_two[:, None], rest[:, :13], tail_three[:, None]], axis=1)
+        moved = MOMENTUM * moments + rate[None] * grad
         for x in range(4):
             stage[pl.ds(32 * x + 16 * side, 16)] = moved[16 * x : 16 * x + 16]
     for b in range(14):
@@ -438,7 +447,7 @@
         [pltpu.VMEM((4, 18, 64, 128), BF16), pltpu.VMEM((2, 10, 64, 128), F32), pltpu.VMEM((16, 96, 128), BF16), pltpu.VMEM((3, 96, 192), F32),
          pltpu.VMEM((944, 64), F32), pltpu.VMEM((128, 24, 128), F32)],
         flops=2_000_000_000, moved=6_000_000,
-    )(back, pre_rows, got_a, got_b, acts, side, part_three)
+    )(back, pre_rows, got_a, got_b, acts, side, part_three, moments)
 
     cores = [(i, i ^ 1) for i in range(lax.axis_size("dp"))]
     plane = lax.axis_size(("depth", "height"))
@@ -468,8 +477,8 @@
 
     send, own = call(
         lambda *refs: reduce(scale_two / volumes, scale_three / volumes, *refs),
-        [((64, 40, 128), BF16), ((18, 128), F32)],
-        [pltpu.VMEM((40, 128), F32), pltpu.VMEM((16, 40, 128), BF16), pltpu.SemaphoreType.DMA((4,))],
+        [((64, 32, 128), BF16), ((18, 128), F32)],
+        [pltpu.VMEM((32, 128), F32), pltpu.VMEM((16, 32, 128), BF16), pltpu.SemaphoreType.DMA((4,))],
         moved=2_000_000, far_out=(0,),
     )(parts, moments)
     own, w2, w3 = lax.optimization_barrier((own, weight_two, weight_three))
@@ -480,7 +489,7 @@
         [(weight_two.shape, F32), (weight_three.shape[::-1], F32), (moment_two.shape, F32), (moment_three.shape, F32)],
         [pltpu.VMEM((128, 18, 128), F32)],
         moved=4_000_000,
-    )(full, other, own, w2, w3.T, moment_two, moment_three)
+    )(full, other, parts, own, w2, w3.T, moment_two, moment_three)
     return (grad_input[None], new_weight_two, new_weight_three.T, new_moment_two, new_moment_three)
 
 

time: 79.5 us -> 77.7 us (0.977)
  blocking collectives: 19.3 us -> 17.7 us
    all_to_all x1, blocking collectives: 19.3 us -> 17.7 us  [local(): lax.all_to_all(send, AXES, 0, 0, axis_index_groups=groups, tiled=True)]
where the time goes in v6:
time: 77.7 us; the launch traced here: 77.3 us
  starting transfers between devices  25 us (32%)
  Pallas kernels  20.7 us (27%)
  blocking collectives  17.7 us (23%)
  waiting for transfers between devices  13.1 us (17%)
  between operations  0.82 us (1%)
    pallas_call x9, Pallas kernels, run(): pl.pallas_call(body, out_shape=[pltpu.HBM(shape, dtype) if i in far_out e...  20.7 us
    all_to_all x1, blocking collectives, local(): lax.all_to_all(send, AXES, 0, 0, axis_index_groups=groups, tiled=True)  17.7 us
    all_to_all x1, starting transfers between devices, local(): lax.all_to_all(parts, AXES, 0, 0, axis_index_groups=groups, tiled=True)  10.3 us
    ppermute x1, waiting for transfers between devices, local(): ship = lax.ppermute(ship, 'depth', swap)  6.23 us
    ppermute x1, starting transfers between devices, local(): got = lax.ppermute(theirs, 'dp', cores)  4.59 us
    ppermute x1, waiting for transfers between devices, local(): got_a = lax.ppermute(send_a, 'height', pairs_a)  4.25 us
    ppermute x1, starting transfers between devices, local(): other = lax.ppermute(full, 'dp', cores)  3.01 us
    ppermute x1, starting transfers between devices, local(): got_a = lax.ppermute(send_a, 'height', pairs_a)  2.62 us
  transfers between devices with their start and end apart: 9, of which 5 were waited for; matrix products, arithmetic and copies ran while one was open for 0% of the time, Pallas kernels for 9%

profile of v6, /device:TPU:1, one launch (start us, length us, event | category | flops | bytes accessed | tf_op | source)
XLA Modules:
  0.0 77.3 jit_solution(15416423920131444089)
XLA Ops:
  0.6 0.0 copy-start
  0.6 0.0 copy-start.2
  0.7 0.0 copy-start.5
  0.7 0.0 copy-start.6
  0.7 3.2 %shard_map.110 = (bf16[2,128,512]{2,1,0:T(8,128)(2,1)S(1)}, bf16[1024,128]{1,0:T(8,128)(2,1)S(1)}, bf16[512,128]{1,0:T(8,128)(2,1)S(1)}, bf16[512,128]{1,0:T(8,1...) custom-call(bf16[128,2,512]{2,1,0:T(2,128)(2,1)} %bitcast.15, bf16[64,4,16,128]{3,2,1,0:T(8,128)(2,1)} %bitcast.7, ...), custom_call_target="tpu_custom_call" | custom-call | bytes 4000000 | tf_op jit(solution)/shard_map/pallas_call | solution.py:20
  3.9 2.2 %collective-permute-start = (bf16[1024,128]{1,0:T(8,128)(2,1)S(1)}, bf16[1024,128]{1,0:T(8,128)(2,1)S(1)}, u32[]{:S(2)}, u32[]{:S(2)}) collective-permute-start(bf16[1024,128]{1,0:T(8,128)(2,1)S(1)} %get-tuple-element.36), channel_id=1, source_target_pairs={{0,8},{8,0},{1,9},{9,1},{2,10},{10,2},{3,11},{11,3},{4,12},{12,4},... | collective-permute-start | bytes 786440 | tf_op jit(solution)/shard_map/ppermute | solution.py:423
  6.1 2.6 %collective-permute-start.1 = (bf16[512,128]{1,0:T(8,128)(2,1)S(1)}, bf16[512,128]{1,0:T(8,128)(2,1)S(1)}, u32[]{:S(2)}, u32[]{:S(2)}) collective-permute-start(bf16[512,128]{1,0:T(8,128)(2,1)S(1)} %get-tuple-element.37), channel_id=1, source_target_pairs={{0,1},{1,0},{2,3},{3,2},{4,5},{5,4},{6,7},{7,6},{8,9},{9,8},{10,11... | collective-permute-start | bytes 393224 | tf_op jit(solution)/shard_map/ppermute | solution.py:424
  8.8 0.0 collective-permute-start.2
  8.8 0.7 collective-permute-start.3
  9.4 0.7 collective-permute-start.4
  10.2 2.9 %shard_map.111 = (bf16[4,16,64,128]{3,2,1,0:T(8,128)(2,1)S(1)}, bf16[128,512]{1,0:T(8,128)(2,1)S(1)}, bf16[16,384,128]{2,1,0:T(8,128)(2,1)S(1)}, bf16[192,768]{1...) custom-call(bf16[64,4,16,128]{3,2,1,0:T(8,128)(2,1)S(1)} %bitcast.8, ...), custom_call_target="tpu_custom_call" | custom-call | flops 100000000 | bytes 8000000 | tf_op jit(solution)/shard_map/pallas_call | solution.py:20
  13.0 0.0 collective-permute-done.4.refs_5_
  13.0 4.3 %collective-permute-done.1.refs_2_.a_ref = bf16[512,128]{1,0:T(8,128)(2,1)S(1)} collective-permute-done((bf16[512,128]{1,0:T(8,128)(2,1)S(1)}, bf16[512,128]{1,0:T(8,128)(2,1)S(1)}, u32[]{:S(2)}, u32[]{:S(2)}) %collective-permute-start.1) | collective-permute-done | bytes 131104 | tf_op jit(solution)/shard_map/ppermute | solution.py:424
  17.3 0.0 collective-permute-done.2.refs_3_
  17.3 0.0 collective-permute-done.3.refs_4_.b_ref
  17.3 0.0 collective-permute-done.refs_1_.side_ref
  17.3 2.8 %shard_map.112 = (bf16[2,64,768]{2,1,0:T(8,128)(2,1)S(1)}, f32[14,128,128]{2,1,0:T(8,128)S(1)}) custom-call(bf16[2,128,512]{2,1,0:T(8,128)(2,1)S(1)} %get-tuple-element.35.refs_0_, bf16[1024,128]{1,0:T(8,128)(2,1)S(1)} %collective-permute-done.refs_1_.side_ref, bf16[512,128]{1,0:T(8,128)(2,1)S(1)} %collective-permute-done.1.refs_2_.a_ref, ...), custom_call_target="tpu_custom_call" | custom-call | flops 2000000000 | bytes 4000000 | tf_op jit(solution)/shard_map/pallas_call | solution.py:20
  20.1 3.1 %shard_map.113 = (f32[64,24,128]{2,1,0:T(8,128)S(1)}, bf16[64,24,128]{2,1,0:T(8,128)(2,1)S(1)}) custom-call(bf16[2,64,768]{2,1,0:T(8,128)(2,1)S(1)} %get-tuple-element.43.back_ref, bf16[4,16,64,128]{3,2,1,0:T(8,128)(2,1)S(1)} %get-tuple-element.44.pre_ref, bf16[512,128]{1,0:T(8,128)(2,1)S(1)} %collective-permute-done.1.refs_2_.a_ref, ...), custom_call_target="tpu_custom_call" | custom-call | flops 2000000000 | bytes 6000000 | tf_op jit(solution)/shard_map/pallas_call | solution.py:20
  23.3 4.6 %collective-permute-start.5 = (bf16[64,24,128]{2,1,0:T(8,128)(2,1)S(1)}, bf16[64,24,128]{2,1,0:T(8,128)(2,1)S(1)}, u32[]{:S(2)}, u32[]{:S(2)}) collective-permute-start(bf16[64,24,128]{2,1,0:T(8,128)(2,1)S(1)} %get-tuple-element.49), channel_id=1, source_target_pairs={{0,16},{16,0},{32,48},{48,32},{64,80},{80,64},{96,112},{112,96},{1... | collective-permute-start | bytes 1179656 | tf_op jit(solution)/shard_map/ppermute | solution.py:455
  27.9 1.3 %collective-permute-done.5.got_ref = bf16[64,24,128]{2,1,0:T(8,128)(2,1)S(1)} collective-permute-done((bf16[64,24,128]{2,1,0:T(8,128)(2,1)S(1)}, bf16[64,24,128]{2,1,0:T(8,128)(2,1)S(1)}, u32[]{:S(2)}, u32[]{:S(2)}) %collective-permute-start.5) | collective-permute-done | bytes 393248 | tf_op jit(solution)/shard_map/ppermute | solution.py:455
  29.2 0.8 %shard_map.114 = bf16[64,24,128]{2,1,0:T(8,128)(2,1)} custom-call(f32[64,24,128]{2,1,0:T(8,128)S(1)} %get-tuple-element.48.mine_ref, bf16[64,24,128]{2,1,0:T(8,128)(2,1)S(1)} %collective-permute-done.5.got_ref), custom_call_target="tpu_custom_call" | custom-call | bytes 2000000 | tf_op jit(solution)/shard_map/pallas_call | solution.py:20
  30.0 10.3 %all-to-all-start = ((bf16[64,24,128]{2,1,0:T(8,128)(2,1)}), bf16[64,24,128]{2,1,0:T(8,128)(2,1)S(1)}, u32[]{:S(2)}, u32[]{:S(2)}) async-start(bf16[64,24,128]{2,1,0:T(8,128)(2,1)} %shard_map.114), calls=%async_computation | async-start | bytes 786432 | tf_op jit(solution)/shard_map/all_to_all | solution.py:462
  40.4 3.1 %shard_map.115 = (f32[4,16,32,128]{3,2,1,0:T(8,128)}, bf16[16,32,128]{2,1,0:T(8,128)(2,1)S(1)}) custom-call(bf16[2,64,768]{2,1,0:T(8,128)(2,1)S(1)} %get-tuple-element.43.back_ref, bf16[64,4,16,128]{3,2,1,0:T(8,128)(2,1)S(1)} %bitcast.9, bf16[512,128]{1,0:T(8,128)(2,1)S(1)} %collective-permute-done.1.refs_2_.a_ref, ...), custom_call_target="tpu_custom_call" | custom-call | flops 4000000000 | bytes 6000000 | tf_op jit(solution)/shard_map/pallas_call | solution.py:20
  43.5 0.9 %collective-permute-start.6 = (bf16[16,32,128]{2,1,0:T(8,128)(2,1)S(1)}, bf16[16,32,128]{2,1,0:T(8,128)(2,1)S(1)}, u32[]{:S(2)}, u32[]{:S(2)}) collective-permute-start(bf16[16,32,128]{2,1,0:T(8,128)(2,1)S(1)} %get-tuple-element.52), channel_id=1, source_target_pairs={{0,8},{8,0},{1,9},{9,1},{2,10},{10,2},{3,11},{11,3},{4,12},{12,4},... | collective-permute-start | bytes 393224 | tf_op jit(solution)/shard_map/ppermute | solution.py:470
  44.4 6.2 %collective-permute-done.6.refs_1_ = bf16[16,32,128]{2,1,0:T(8,128)(2,1)S(1)} collective-permute-done((bf16[16,32,128]{2,1,0:T(8,128)(2,1)S(1)}, bf16[16,32,128]{2,1,0:T(8,128)(2,1)S(1)}, u32[]{:S(2)}, u32[]{:S(2)}) %collective-permute-start.6) | collective-permute-done | bytes 131104 | tf_op jit(solution)/shard_map/ppermute | solution.py:470
  50.7 0.8 %all-to-all-done.refs_0_.first_ref = bf16[64,24,128]{2,1,0:T(8,128)(2,1)S(1)} async-done(((bf16[64,24,128]{2,1,0:T(8,128)(2,1)}), bf16[64,24,128]{2,1,0:T(8,128)(2,1)S(1)}, u32[]{:S(2)}, u32[]{:S(2)}) %all-to-all-start) | async-done | bytes 393248 | tf_op jit(solution)/shard_map/all_to_all | solution.py:462
  51.5 0.9 %shard_map.117 = (bf16[64,32,128]{2,1,0:T(8,128)(2,1)}, f32[18,128]{1,0:T(8,128)S(1)}) custom-call(bf16[64,24,128]{2,1,0:T(8,128)(2,1)S(1)} %all-to-all-done.refs_0_.first_ref, f32[24,128]{1,0:T(8,128)S(1)} %get-tuple-element.47.m_ref.refs_1_), custom_call_target="tpu_custom_call" | custom-call | bytes 2000000 | tf_op jit(solution)/shard_map/pallas_call | solution.py:20
  52.4 17.7 %all_to_all.10.full_ref = bf16[64,32,128]{2,1,0:T(8,128)(2,1)S(1)} all-to-all(bf16[64,32,128]{2,1,0:T(8,128)(2,1)} %get-tuple-element.56), channel_id=1, replica_groups={{0,1,2,3,4,5,6,7,8,9,10,11,12,13,14,15,32,33,34,35,36,37,38,39,40,41,42..., dimensions={0} | all-to-all | bytes 1048576 | tf_op jit(solution)/shard_map/all_to_all | solution.py:485
  70.0 3.0 %collective-permute-start.7 = (bf16[64,32,128]{2,1,0:T(8,128)(2,1)S(1)}, bf16[64,32,128]{2,1,0:T(8,128)(2,1)S(1)}, u32[]{:S(2)}, u32[]{:S(2)}) collective-permute-start(bf16[64,32,128]{2,1,0:T(8,128)(2,1)S(1)} %all_to_all.10.full_ref), channel_id=1, source_target_pairs={{0,16},{16,0},{32,48},{48,32},{64,80},{80,64},{96,112},{112,96},{1... | collective-permute-start | bytes 1572872 | tf_op jit(solution)/shard_map/ppermute | solution.py:486
  73.0 1.1 %shard_map.116 = bf16[32,4,16,128]{3,2,1,0:T(8,128)(2,1)} custom-call(f32[4,16,32,128]{3,2,1,0:T(8,128)S(1)} %copy-done.3, bf16[16,32,128]{2,1,0:T(8,128)(2,1)S(1)} %collective-permute-done.6.refs_1_), custom_call_target="tpu_custom_call" | custom-call | bytes 2000000 | tf_op jit(solution)/shard_map/pallas_call | solution.py:20
  74.1 0.5 collective-permute-done.7.other_ref
  74.6 2.7 %shard_map.118 = (f32[64,864]{1,0:T(8,128)}, f32[1728,128]{1,0:T(8,128)}, f32[432]{0:T(512)}, f32[1728]{0:T(1024)}) custom-call(bf16[64,32,128]{2,1,0:T(8,128)(2,1)S(1)} %all_to_all.10.full_ref, bf16[64,32,128]{2,1,0:T(8,128)(2,1)S(1)} %collective-permute-done.7.other_ref, bf16[64,24,128]{2,1,0:T(8,128)(2,1)S(1)} %all-to-all-done.refs_0_.first_ref, ...), custom_call_target="tpu_custom_call" | custom-call | bytes 4000000 | tf_op jit(solution)/shard_map/pallas_call | solution.py:20
  (10 shorter events, 0.0 us)
Async XLA Ops:
  0.6 9.5 %copy-start = (bf16[1,64,4,16,128]{4,3,2,1,0:T(8,128)(2,1)S(1)}, bf16[1,64,4,16,128]{4,3,2,1,0:T(8,128)(2,1)}, u32[]{:S(2)}) copy-start(bf16[1,64,4,16,128]{4,3,2,1,0:T(8,128)(2,1)} %param.8) | copy-start | bytes 3145732
  0.6 9.5 %copy-start.2 = (bf16[1,32,4,16,128]{4,3,2,1,0:T(8,128)(2,1)S(1)}, bf16[1,32,4,16,128]{4,3,2,1,0:T(8,128)(2,1)}, u32[]{:S(2)}) copy-start(bf16[1,32,4,16,128]{4,3,2,1,0:T(8,128)(2,1)} %param.7) | copy-start | bytes 1572868
  0.7 9.5 %copy-start.5 = (f32[1728]{0:T(1024)S(1)}, f32[1728]{0:T(1024)}, u32[]{:S(2)}) copy-start(f32[1728]{0:T(1024)} %m3_ref.3) | copy-start | bytes 20740
  0.7 9.5 %copy-start.6 = (f32[432]{0:T(512)S(1)}, f32[432]{0:T(512)}, u32[]{:S(2)}) copy-start(f32[432]{0:T(512)} %m2_ref.3) | copy-start | bytes 5188
  0.7 9.5 %copy-start.4 = (f32[64,864]{1,0:T(8,128)S(1)}, f32[64,864]{1,0:T(8,128)}, u32[]{:S(2)}) copy-start(f32[64,864]{1,0:T(8,128)} %w2_ref.2) | copy-start | bytes 663556
  3.9 13.4 %collective-permute-start = (bf16[1024,128]{1,0:T(8,128)(2,1)S(1)}, bf16[1024,128]{1,0:T(8,128)(2,1)S(1)}, u32[]{:S(2)}, u32[]{:S(2)}) collective-permute-start(bf16[1024,128]{1,0:T(8,128)(2,1)S(1)} %get-tuple-element.36), channel_id=1, source_target_pairs={{0,8},{8,0},{1,9},{9,1},{2,10},{10,2},{3,11},{11,3},{4,12},{12,4},... | collective-permute-start | bytes 786440 | tf_op jit(solution)/shard_map/ppermute | solution.py:423
  6.1 11.1 %collective-permute-start.1 = (bf16[512,128]{1,0:T(8,128)(2,1)S(1)}, bf16[512,128]{1,0:T(8,128)(2,1)S(1)}, u32[]{:S(2)}, u32[]{:S(2)}) collective-permute-start(bf16[512,128]{1,0:T(8,128)(2,1)S(1)} %get-tuple-element.37), channel_id=1, source_target_pairs={{0,1},{1,0},{2,3},{3,2},{4,5},{5,4},{6,7},{7,6},{8,9},{9,8},{10,11... | collective-permute-start | bytes 393224 | tf_op jit(solution)/shard_map/ppermute | solution.py:424
  8.8 8.5 %collective-permute-start.2 = (bf16[512,128]{1,0:T(8,128)(2,1)S(1)}, bf16[512,128]{1,0:T(8,128)(2,1)S(1)}, u32[]{:S(2)}, u32[]{:S(2)}) collective-permute-start(bf16[512,128]{1,0:T(8,128)(2,1)S(1)} %get-tuple-element.38), channel_id=1, source_target_pairs={{0,9},{1,8},{2,11},{3,10},{4,13},{5,12},{6,15},{7,14},{8,1},{9,0},... | collective-permute-start | bytes 393224 | tf_op jit(solution)/shard_map/ppermute | solution.py:425
  8.8 8.5 %collective-permute-start.3 = (bf16[512,128]{1,0:T(8,128)(2,1)S(1)}, bf16[512,128]{1,0:T(8,128)(2,1)S(1)}, u32[]{:S(2)}, u32[]{:S(2)}) collective-permute-start(bf16[512,128]{1,0:T(8,128)(2,1)S(1)} %get-tuple-element.39), channel_id=1, source_target_pairs={{1,2},{2,1},{3,4},{4,3},{5,6},{6,5},{9,10},{10,9},{11,12},{12,11},... | collective-permute-start | bytes 393224 | tf_op jit(solution)/shard_map/ppermute | solution.py:426
  9.4 3.6 %collective-permute-start.4 = (bf16[128,128]{1,0:T(8,128)(2,1)S(1)}, bf16[128,128]{1,0:T(8,128)(2,1)S(1)}, u32[]{:S(2)}, u32[]{:S(2)}) collective-permute-start(bf16[128,128]{1,0:T(8,128)(2,1)S(1)} %get-tuple-element.40), channel_id=1, source_target_pairs={{1,10},{2,9},{3,12},{4,11},{5,14},{6,13},{9,2},{10,1},{11,4},{12,3... | collective-permute-start | bytes 98312 | tf_op jit(solution)/shard_map/ppermute | solution.py:427
  23.3 5.9 %collective-permute-start.5 = (bf16[64,24,128]{2,1,0:T(8,128)(2,1)S(1)}, bf16[64,24,128]{2,1,0:T(8,128)(2,1)S(1)}, u32[]{:S(2)}, u32[]{:S(2)}) collective-permute-start(bf16[64,24,128]{2,1,0:T(8,128)(2,1)S(1)} %get-tuple-element.49), channel_id=1, source_target_pairs={{0,16},{16,0},{32,48},{48,32},{64,80},{80,64},{96,112},{112,96},{1... | collective-permute-start | bytes 1179656 | tf_op jit(solution)/shard_map/ppermute | solution.py:455
  30.0 21.4 %all-to-all-start = ((bf16[64,24,128]{2,1,0:T(8,128)(2,1)}), bf16[64,24,128]{2,1,0:T(8,128)(2,1)S(1)}, u32[]{:S(2)}, u32[]{:S(2)}) async-start(bf16[64,24,128]{2,1,0:T(8,128)(2,1)} %shard_map.114), calls=%async_computation | async-start | bytes 786432 | tf_op jit(solution)/shard_map/all_to_all | solution.py:462
  43.5 29.5 %copy-start.3 = (f32[4,16,32,128]{3,2,1,0:T(8,128)S(1)}, f32[4,16,32,128]{3,2,1,0:T(8,128)}, u32[]{:S(2)}) copy-start(f32[4,16,32,128]{3,2,1,0:T(8,128)} %get-tuple-element.53.refs_0_) | copy-start | bytes 3145732
  43.5 7.2 %collective-permute-start.6 = (bf16[16,32,128]{2,1,0:T(8,128)(2,1)S(1)}, bf16[16,32,128]{2,1,0:T(8,128)(2,1)S(1)}, u32[]{:S(2)}, u32[]{:S(2)}) collective-permute-start(bf16[16,32,128]{2,1,0:T(8,128)(2,1)S(1)} %get-tuple-element.52), channel_id=1, source_target_pairs={{0,8},{8,0},{1,9},{9,1},{2,10},{10,2},{3,11},{11,3},{4,12},{12,4},... | collective-permute-start | bytes 393224 | tf_op jit(solution)/shard_map/ppermute | solution.py:470
  51.5 23.1 %copy-start.1 = (f32[128,1728]{0,1:T(8,128)S(1)}, f32[128,1728]{0,1:T(8,128)}, u32[]{:S(2)}) copy-start(f32[128,1728]{0,1:T(8,128)} %param.11) | copy-start | bytes 2654212
  70.0 4.5 %collective-permute-start.7 = (bf16[64,32,128]{2,1,0:T(8,128)(2,1)S(1)}, bf16[64,32,128]{2,1,0:T(8,128)(2,1)S(1)}, u32[]{:S(2)}, u32[]{:S(2)}) collective-permute-start(bf16[64,32,128]{2,1,0:T(8,128)(2,1)S(1)} %all_to_all.10.full_ref), channel_id=1, source_target_pairs={{0,16},{16,0},{32,48},{48,32},{64,80},{80,64},{96,112},{112,96},{1... | collective-permute-start | bytes 1572872 | tf_op jit(solution)/shard_map/ppermute | solution.py:486

commit v7 on v6

--- a/solution.py
+++ b/solution.py
@@ -49,12 +49,13 @@
     return jnp.concatenate([x[..., amount:], x[..., :amount]], axis=-1)
 
 
-def arrange(cot_far, pre_far, act_far, cot_out, side_out, a_out, b_out, diag_a_out, diag_b_out,
+def arrange(cot_far, pre_far, act_far, w3_far, cot_out, side_out, a_out, b_out, diag_a_out, diag_b_out, w3_out,
             cot_ref, pre_ref, act_ref, sems):
     dep = lax.axis_index("depth")
     loads = [pltpu.make_async_copy(cot_far, cot_ref, sems.at[0])]
     loads += [pltpu.make_async_copy(act_far.at[:, 3 * (1 - dep)], act_ref, sems.at[1])]
     loads += [pltpu.make_async_copy(pre_far.at[:, d], pre_ref.at[:, d], sems.at[2 + d]) for d in range(4)]
+    loads += [pltpu.make_async_copy(w3_far, w3_out, sems.at[6])]
     for load in loads:
         load.start()
     loads[0].wait()
@@ -80,6 +81,7 @@
         place = slice(256 + 64 * d, 320 + 64 * d)
         a_out[place] = jnp.where(odd, first, final)
         b_out[place] = jnp.where(odd, final, first)
+    loads[6].wait()
 
 
 def shifts(rows):
@@ -89,13 +91,8 @@
     return before, rows, after
 
 
-def prepare(pre_ref, act_ref, w2_ref, w3_far, m2_ref, m3_ref, pre_out, pooled_out, act_out, w2_out, w3_out, m_out,
-            t2, w3_ref, sems):
-    loads = []
-    for i in range(6):
-        rows = slice(288 * i, 288 * i + 288)
-        loads.append(pltpu.make_async_copy(w3_far.at[rows], w3_ref.at[rows], sems.at[i]))
-        loads[i].start()
+def prepare(pre_ref, act_ref, w2_ref, w3_ref, m2_ref, m3_ref, pre_out, pooled_out, act_out, w2_out, w3_out, m_out,
+            t2):
     for d in range(4):
         pre_out[d] = jnp.swapaxes(pre_ref[:, d].astype(F32), 0, 1).astype(BF16)
     m_out[...] = jnp.zeros((24, 128), F32)
@@ -116,7 +113,7 @@
                 for i in range(2):
                     for j in range(2):
                         x = pre_out[2 * d + i, 4 * t + 2 * half + j].astype(F32)
-                        x = jnp.where(x > 0, x, SLOPE * x)
+                        x = jnp.maximum(x, SLOPE * x)
                         total = x if total is None else total + x
                 halves.append(total)
             total = jnp.concatenate(halves, axis=1)
@@ -130,8 +127,6 @@
             start = 96 * d + 32 * ow
             act_out[:, start : start + 32, :] = value.astype(BF16)
     t2[...] = jnp.transpose(w2_ref[...])
-    for load in loads:
-        load.wait()
     for kd in range(3):
         for oh in range(3):
             for ow in range(3):
@@ -234,7 +229,7 @@
 
 
 def fine(back_ref, pre_ref, a_ref, b_ref, act_ref, side_ref, three_ref, m_ref,
-         mine_out, theirs_out, z_out, upper, near, parts, t2, stage):
+         mine_out, theirs_out, z_out, upper, near, parts, t2, stage, small):
     dep = lax.axis_index("depth")
     cotangent(back_ref, a_ref, b_ref, lambda f: pre_ref.at[f], upper, z_out)
     layer = side_ref[512:].astype(F32).reshape(16, 32, 128)
@@ -270,22 +265,25 @@
                 t2[pl.ds(k, 32, stride=27), :] = parts[od, 32 * ow : 32 * ow + 32, 64 * oh : 64 * oh + 64]
     t2[864:] = jnp.zeros((80, 64), F32)
     tail = lax.broadcasted_iota(jnp.int32, (64, 128), 1) < 48
+    core = lax.rem(lax.axis_index("dp"), 2)
     for half in range(2):
         for b in range(4):
             start = 432 * half + 128 * b
             block = jnp.transpose(t2[start : start + 128, :])
             if b == 3:
                 block = jnp.where(tail, block, 0.0)
-            stage[pl.ds(half, 64, stride=2), b, :] = block
-    for b in range(14):
-        stage[:, 4 + b, :] = three_ref[b]
-    stage[:, 18:21, :] = jnp.broadcast_to(m_ref[:3][None], (128, 3, 128))
-    stage[:, 21:, :] = jnp.zeros((128, 3, 128), F32)
-    core = lax.rem(lax.axis_index("dp"), 2)
-    for x in range(4):
-        place = slice(16 * x, 16 * x + 16)
-        mine_out[place] = stage[pl.ds(32 * x + 16 * core, 16)]
-        theirs_out[place] = stage[pl.ds(32 * x + 16 * (1 - core), 16)].astype(BF16)
+            small[b, pl.ds(half, 64, stride=2), :] = block
+    for out, side in ((mine_out, core), (stage, 1 - core)):
+        for x in range(4):
+            rows = pl.ds(pl.multiple_of(32 * x + 16 * side, 16), 16)
+            place = slice(16 * x, 16 * x + 16)
+            for b in range(4):
+                out[place, b, :] = small[b, rows, :]
+            for b in range(14):
+                out[place, 4 + b, :] = three_ref[b, rows, :]
+        out[:, 18:21, :] = jnp.broadcast_to(m_ref[:3][None], (64, 3, 128))
+        out[:, 21:, :] = jnp.zeros((64, 3, 128), F32)
+    theirs_out[...] = stage[...].astype(BF16)
 
 
 def combine(mine_ref, got_ref, parts_far, packed, sems):
@@ -405,14 +403,15 @@
     volumes = lax.axis_size("dp")
     pre, act, cot = pre_two[0], act_one[0], cot_three[0]
 
-    cot_rows, send_side, send_a, send_b, send_da, send_db = call(
+    cot_rows, send_side, send_a, send_b, send_da, send_db, w3_near = call(
         arrange,
         [((2, 128, 512), BF16), ((1024, 128), BF16), ((512, 128), BF16),
-         ((512, 128), BF16), ((512, 128), BF16), ((128, 128), BF16)],
+         ((512, 128), BF16), ((512, 128), BF16), ((128, 128), BF16),
+         ((1728, 128), F32)],
         [pltpu.VMEM((128, 2, 512), BF16), pltpu.VMEM((64, 4, 16, 128), BF16), pltpu.VMEM((32, 16, 128), BF16),
-         pltpu.SemaphoreType.DMA((6,))],
-        moved=4_000_000, far=(0, 1, 2),
-    )(cot, pre, act)
+         pltpu.SemaphoreType.DMA((7,))],
+        moved=4_000_000, far=(0, 1, 2, 3),
+    )(cot, pre, act, weight_three.T)
     tall = lax.axis_size("height")
     swap = [(0, 1), (1, 0)]
     pairs_a = [(h, h ^ 1) for h in range(tall)]
@@ -429,9 +428,9 @@
     pre_rows, pooled, acts, wide_two, wide_three, moments = call(
         prepare,
         [((4, 16, 64, 128), BF16), ((128, 512), BF16), ((16, 384, 128), BF16), ((192, 768), BF16), ((192, 1152), BF16), ((24, 128), F32)],
-        [pltpu.VMEM((864, 64), F32), pltpu.VMEM((1728, 128), F32), pltpu.SemaphoreType.DMA((6,))],
-        flops=100_000_000, moved=8_000_000, far=(3,),
-    )(pre, act, weight_two, weight_three.T, moment_two, moment_three)
+        [pltpu.VMEM((864, 64), F32)],
+        flops=100_000_000, moved=8_000_000,
+    )(pre, act, weight_two, w3_near, moment_two, moment_three)
 
     back, part_three = call(
         lambda *refs: coarse(scale_three, *refs),
@@ -445,7 +444,7 @@
         fine,
         [((64, 24, 128), F32), ((64, 24, 128), BF16)],
         [pltpu.VMEM((4, 18, 64, 128), BF16), pltpu.VMEM((2, 10, 64, 128), F32), pltpu.VMEM((16, 96, 128), BF16), pltpu.VMEM((3, 96, 192), F32),
-         pltpu.VMEM((944, 64), F32), pltpu.VMEM((128, 24, 128), F32)],
+         pltpu.VMEM((944, 64), F32), pltpu.VMEM((64, 24, 128), F32), pltpu.VMEM((4, 128, 128), F32)],
         flops=2_000_000_000, moved=6_000_000,
     )(back, pre_rows, got_a, got_b, acts, side, part_three, moments)
 

time: 77.7 us -> 77.3 us (level)
  Pallas kernels: 20.7 us -> 19.1 us
  waiting for transfers between devices: 13.1 us -> 14.4 us
    pallas_call x9, Pallas kernels: 20.7 us -> 19.1 us  [run(): pl.pallas_call(body, out_shape=[pltpu.HBM(shape, dtype) if i in far_out e...]
    ppermute x1, waiting for transfers between devices: 4.25 us -> 5.56 us  [local(): got_a = lax.ppermute(send_a, 'height', pairs_a)]
  transfers between devices with their start and end apart: 9 -> 9, of which waited for: 5 -> 5; matrix products, arithmetic and copies ran while one was open for 0% -> 0% of each run, Pallas kernels for 9% -> 7%
where the time goes in v7:
time: 77.3 us; the launch traced here: 77 us
  starting transfers between devices  25 us (32%)
  Pallas kernels  19.1 us (25%)
  blocking collectives  17.7 us (23%)
  waiting for transfers between devices  14.4 us (19%)
  between operations  0.82 us (1%)
    pallas_call x9, Pallas kernels, run(): pl.pallas_call(body, out_shape=[pltpu.HBM(shape, dtype) if i in far_out e...  19.1 us
    all_to_all x1, blocking collectives, local(): lax.all_to_all(send, AXES, 0, 0, axis_index_groups=groups, tiled=True)  17.7 us
    all_to_all x1, starting transfers between devices, local(): lax.all_to_all(parts, AXES, 0, 0, axis_index_groups=groups, tiled=True)  10.3 us
    ppermute x1, waiting for transfers between devices, local(): ship = lax.ppermute(ship, 'depth', swap)  6.23 us
    ppermute x1, waiting for transfers between devices, local(): got_a = lax.ppermute(send_a, 'height', pairs_a)  5.56 us
    ppermute x1, starting transfers between devices, local(): got = lax.ppermute(theirs, 'dp', cores)  4.58 us
    ppermute x1, starting transfers between devices, local(): other = lax.ppermute(full, 'dp', cores)  3.01 us
    ppermute x1, starting transfers between devices, local(): got_a = lax.ppermute(send_a, 'height', pairs_a)  2.62 us
  transfers between devices with their start and end apart: 9, of which 5 were waited for; matrix products, arithmetic and copies ran while one was open for 0% of the time, Pallas kernels for 7%

profile of v7, /device:TPU:1, one launch (start us, length us, event | category | flops | bytes accessed | tf_op | source)
XLA Modules:
  0.0 77.0 jit_solution(13112044834067190520)
XLA Ops:
  0.6 0.0 copy-start
  0.6 0.0 copy-start.2
  0.7 0.0 copy-start.5
  0.7 0.0 copy-start.6
  0.7 3.3 %shard_map.110 = (bf16[2,128,512]{2,1,0:T(8,128)(2,1)S(1)}, bf16[1024,128]{1,0:T(8,128)(2,1)S(1)}, bf16[512,128]{1,0:T(8,128)(2,1)S(1)}, bf16[512,128]{1,0:T(8,1...) custom-call(bf16[128,2,512]{2,1,0:T(2,128)(2,1)} %bitcast.15, ...), custom_call_target="tpu_custom_call" | custom-call | bytes 4000000 | tf_op jit(solution)/shard_map/pallas_call | solution.py:20
  4.0 2.2 %collective-permute-start = (bf16[1024,128]{1,0:T(8,128)(2,1)S(1)}, bf16[1024,128]{1,0:T(8,128)(2,1)S(1)}, u32[]{:S(2)}, u32[]{:S(2)}) collective-permute-start(bf16[1024,128]{1,0:T(8,128)(2,1)S(1)} %get-tuple-element.37), channel_id=1, source_target_pairs={{0,8},{8,0},{1,9},{9,1},{2,10},{10,2},{3,11},{11,3},{4,12},{12,4},... | collective-permute-start | bytes 786440 | tf_op jit(solution)/shard_map/ppermute | solution.py:422
  6.2 2.6 %collective-permute-start.1 = (bf16[512,128]{1,0:T(8,128)(2,1)S(1)}, bf16[512,128]{1,0:T(8,128)(2,1)S(1)}, u32[]{:S(2)}, u32[]{:S(2)}) collective-permute-start(bf16[512,128]{1,0:T(8,128)(2,1)S(1)} %get-tuple-element.38), channel_id=1, source_target_pairs={{0,1},{1,0},{2,3},{3,2},{4,5},{5,4},{6,7},{7,6},{8,9},{9,8},{10,11... | collective-permute-start | bytes 393224 | tf_op jit(solution)/shard_map/ppermute | solution.py:423
  8.8 0.0 collective-permute-start.2
  8.8 0.7 collective-permute-start.3
  9.4 0.7 collective-permute-start.4
  10.2 1.6 %shard_map.111 = (bf16[4,16,64,128]{3,2,1,0:T(8,128)(2,1)S(1)}, bf16[128,512]{1,0:T(8,128)(2,1)S(1)}, bf16[16,384,128]{2,1,0:T(8,128)(2,1)S(1)}, bf16[192,768]{1...) custom-call(bf16[64,4,16,128]{3,2,1,0:T(8,128)(2,1)S(1)} %bitcast.8, ...), custom_call_target="tpu_custom_call" | custom-call | flops 100000000 | bytes 8000000 | tf_op jit(solution)/shard_map/pallas_call | solution.py:20
  11.7 0.0 collective-permute-done.4.refs_5_
  11.7 5.6 %collective-permute-done.1.refs_2_.a_ref = bf16[512,128]{1,0:T(8,128)(2,1)S(1)} collective-permute-done((bf16[512,128]{1,0:T(8,128)(2,1)S(1)}, bf16[512,128]{1,0:T(8,128)(2,1)S(1)}, u32[]{:S(2)}, u32[]{:S(2)}) %collective-permute-start.1) | collective-permute-done | bytes 131104 | tf_op jit(solution)/shard_map/ppermute | solution.py:423
  17.3 0.0 collective-permute-done.2.refs_3_
  17.3 0.0 collective-permute-done.3.refs_4_.b_ref
  17.3 0.0 collective-permute-done.refs_1_.side_ref
  17.3 2.8 %shard_map.112 = (bf16[2,64,768]{2,1,0:T(8,128)(2,1)S(1)}, f32[14,128,128]{2,1,0:T(8,128)S(1)}) custom-call(bf16[2,128,512]{2,1,0:T(8,128)(2,1)S(1)} %get-tuple-element.36.refs_0_, bf16[1024,128]{1,0:T(8,128)(2,1)S(1)} %collective-permute-done.refs_1_.side_ref, bf16[512,128]{1,0:T(8,128)(2,1)S(1)} %collective-permute-done.1.refs_2_.a_ref, ...), custom_call_target="tpu_custom_call" | custom-call | flops 2000000000 | bytes 4000000 | tf_op jit(solution)/shard_map/pallas_call | solution.py:20
  20.2 2.8 %shard_map.113 = (f32[64,24,128]{2,1,0:T(8,128)S(1)}, bf16[64,24,128]{2,1,0:T(8,128)(2,1)S(1)}) custom-call(bf16[2,64,768]{2,1,0:T(8,128)(2,1)S(1)} %get-tuple-element.45.back_ref, bf16[4,16,64,128]{3,2,1,0:T(8,128)(2,1)S(1)} %get-tuple-element.46.pre_ref, bf16[512,128]{1,0:T(8,128)(2,1)S(1)} %collective-permute-done.1.refs_2_.a_ref, ...), custom_call_target="tpu_custom_call" | custom-call | flops 2000000000 | bytes 6000000 | tf_op jit(solution)/shard_map/pallas_call | solution.py:20
  23.0 4.6 %collective-permute-start.5 = (bf16[64,24,128]{2,1,0:T(8,128)(2,1)S(1)}, bf16[64,24,128]{2,1,0:T(8,128)(2,1)S(1)}, u32[]{:S(2)}, u32[]{:S(2)}) collective-permute-start(bf16[64,24,128]{2,1,0:T(8,128)(2,1)S(1)} %get-tuple-element.51), channel_id=1, source_target_pairs={{0,16},{16,0},{32,48},{48,32},{64,80},{80,64},{96,112},{112,96},{1... | collective-permute-start | bytes 1179656 | tf_op jit(solution)/shard_map/ppermute | solution.py:454
  27.6 1.3 %collective-permute-done.5.got_ref = bf16[64,24,128]{2,1,0:T(8,128)(2,1)S(1)} collective-permute-done((bf16[64,24,128]{2,1,0:T(8,128)(2,1)S(1)}, bf16[64,24,128]{2,1,0:T(8,128)(2,1)S(1)}, u32[]{:S(2)}, u32[]{:S(2)}) %collective-permute-start.5) | collective-permute-done | bytes 393248 | tf_op jit(solution)/shard_map/ppermute | solution.py:454
  28.9 0.8 %shard_map.114 = bf16[64,24,128]{2,1,0:T(8,128)(2,1)} custom-call(f32[64,24,128]{2,1,0:T(8,128)S(1)} %get-tuple-element.50.mine_ref, bf16[64,24,128]{2,1,0:T(8,128)(2,1)S(1)} %collective-permute-done.5.got_ref), custom_call_target="tpu_custom_call" | custom-call | bytes 2000000 | tf_op jit(solution)/shard_map/pallas_call | solution.py:20
  29.7 10.3 %all-to-all-start = ((bf16[64,24,128]{2,1,0:T(8,128)(2,1)}), bf16[64,24,128]{2,1,0:T(8,128)(2,1)S(1)}, u32[]{:S(2)}, u32[]{:S(2)}) async-start(bf16[64,24,128]{2,1,0:T(8,128)(2,1)} %shard_map.114), calls=%async_computation | async-start | bytes 786432 | tf_op jit(solution)/shard_map/all_to_all | solution.py:461
  40.1 3.1 %shard_map.115 = (f32[4,16,32,128]{3,2,1,0:T(8,128)}, bf16[16,32,128]{2,1,0:T(8,128)(2,1)S(1)}) custom-call(bf16[2,64,768]{2,1,0:T(8,128)(2,1)S(1)} %get-tuple-element.45.back_ref, bf16[64,4,16,128]{3,2,1,0:T(8,128)(2,1)S(1)} %bitcast.9, bf16[512,128]{1,0:T(8,128)(2,1)S(1)} %collective-permute-done.1.refs_2_.a_ref, ...), custom_call_target="tpu_custom_call" | custom-call | flops 4000000000 | bytes 6000000 | tf_op jit(solution)/shard_map/pallas_call | solution.py:20
  43.2 0.9 %collective-permute-start.6 = (bf16[16,32,128]{2,1,0:T(8,128)(2,1)S(1)}, bf16[16,32,128]{2,1,0:T(8,128)(2,1)S(1)}, u32[]{:S(2)}, u32[]{:S(2)}) collective-permute-start(bf16[16,32,128]{2,1,0:T(8,128)(2,1)S(1)} %get-tuple-element.54), channel_id=1, source_target_pairs={{0,8},{8,0},{1,9},{9,1},{2,10},{10,2},{3,11},{11,3},{4,12},{12,4},... | collective-permute-start | bytes 393224 | tf_op jit(solution)/shard_map/ppermute | solution.py:469
  44.1 6.2 %collective-permute-done.6.refs_1_ = bf16[16,32,128]{2,1,0:T(8,128)(2,1)S(1)} collective-permute-done((bf16[16,32,128]{2,1,0:T(8,128)(2,1)S(1)}, bf16[16,32,128]{2,1,0:T(8,128)(2,1)S(1)}, u32[]{:S(2)}, u32[]{:S(2)}) %collective-permute-start.6) | collective-permute-done | bytes 131104 | tf_op jit(solution)/shard_map/ppermute | solution.py:469
  50.3 0.8 %all-to-all-done.refs_0_.first_ref = bf16[64,24,128]{2,1,0:T(8,128)(2,1)S(1)} async-done(((bf16[64,24,128]{2,1,0:T(8,128)(2,1)}), bf16[64,24,128]{2,1,0:T(8,128)(2,1)S(1)}, u32[]{:S(2)}, u32[]{:S(2)}) %all-to-all-start) | async-done | bytes 393248 | tf_op jit(solution)/shard_map/all_to_all | solution.py:461
  51.1 0.9 %shard_map.117 = (bf16[64,32,128]{2,1,0:T(8,128)(2,1)}, f32[18,128]{1,0:T(8,128)S(1)}) custom-call(bf16[64,24,128]{2,1,0:T(8,128)(2,1)S(1)} %all-to-all-done.refs_0_.first_ref, f32[24,128]{1,0:T(8,128)S(1)} %get-tuple-element.49.m_ref.refs_1_), custom_call_target="tpu_custom_call" | custom-call | bytes 2000000 | tf_op jit(solution)/shard_map/pallas_call | solution.py:20
  52.1 17.7 %all_to_all.10.full_ref = bf16[64,32,128]{2,1,0:T(8,128)(2,1)S(1)} all-to-all(bf16[64,32,128]{2,1,0:T(8,128)(2,1)} %get-tuple-element.58), channel_id=1, replica_groups={{0,1,2,3,4,5,6,7,8,9,10,11,12,13,14,15,32,33,34,35,36,37,38,39,40,41,42..., dimensions={0} | all-to-all | bytes 1048576 | tf_op jit(solution)/shard_map/all_to_all | solution.py:484
  69.7 3.0 %collective-permute-start.7 = (bf16[64,32,128]{2,1,0:T(8,128)(2,1)S(1)}, bf16[64,32,128]{2,1,0:T(8,128)(2,1)S(1)}, u32[]{:S(2)}, u32[]{:S(2)}) collective-permute-start(bf16[64,32,128]{2,1,0:T(8,128)(2,1)S(1)} %all_to_all.10.full_ref), channel_id=1, source_target_pairs={{0,16},{16,0},{32,48},{48,32},{64,80},{80,64},{96,112},{112,96},{1... | collective-permute-start | bytes 1572872 | tf_op jit(solution)/shard_map/ppermute | solution.py:485
  72.7 1.1 %shard_map.116 = bf16[32,4,16,128]{3,2,1,0:T(8,128)(2,1)} custom-call(f32[4,16,32,128]{3,2,1,0:T(8,128)S(1)} %copy-done.3, bf16[16,32,128]{2,1,0:T(8,128)(2,1)S(1)} %collective-permute-done.6.refs_1_), custom_call_target="tpu_custom_call" | custom-call | bytes 2000000 | tf_op jit(solution)/shard_map/pallas_call | solution.py:20
  73.8 0.5 collective-permute-done.7.other_ref
  74.3 2.7 %shard_map.118 = (f32[64,864]{1,0:T(8,128)}, f32[1728,128]{1,0:T(8,128)}, f32[432]{0:T(512)}, f32[1728]{0:T(1024)}) custom-call(bf16[64,32,128]{2,1,0:T(8,128)(2,1)S(1)} %all_to_all.10.full_ref, bf16[64,32,128]{2,1,0:T(8,128)(2,1)S(1)} %collective-permute-done.7.other_ref, bf16[64,24,128]{2,1,0:T(8,128)(2,1)S(1)} %all-to-all-done.refs_0_.first_ref, ...), custom_call_target="tpu_custom_call" | custom-call | bytes 4000000 | tf_op jit(solution)/shard_map/pallas_call | solution.py:20
  (10 shorter events, 0.0 us)
Async XLA Ops:
  0.6 9.5 %copy-start = (bf16[1,64,4,16,128]{4,3,2,1,0:T(8,128)(2,1)S(1)}, bf16[1,64,4,16,128]{4,3,2,1,0:T(8,128)(2,1)}, u32[]{:S(2)}) copy-start(bf16[1,64,4,16,128]{4,3,2,1,0:T(8,128)(2,1)} %param.8) | copy-start | bytes 3145732
  0.6 9.5 %copy-start.2 = (bf16[1,32,4,16,128]{4,3,2,1,0:T(8,128)(2,1)S(1)}, bf16[1,32,4,16,128]{4,3,2,1,0:T(8,128)(2,1)}, u32[]{:S(2)}) copy-start(bf16[1,32,4,16,128]{4,3,2,1,0:T(8,128)(2,1)} %param.7) | copy-start | bytes 1572868
  0.7 9.5 %copy-start.5 = (f32[1728]{0:T(1024)S(1)}, f32[1728]{0:T(1024)}, u32[]{:S(2)}) copy-start(f32[1728]{0:T(1024)} %m3_ref.3) | copy-start | bytes 20740
  0.7 9.5 %copy-start.6 = (f32[432]{0:T(512)S(1)}, f32[432]{0:T(512)}, u32[]{:S(2)}) copy-start(f32[432]{0:T(512)} %m2_ref.3) | copy-start | bytes 5188
  0.7 9.5 %copy-start.4 = (f32[64,864]{1,0:T(8,128)S(1)}, f32[64,864]{1,0:T(8,128)}, u32[]{:S(2)}) copy-start(f32[64,864]{1,0:T(8,128)} %w2_ref.2) | copy-start | bytes 663556
  4.0 13.4 %collective-permute-start = (bf16[1024,128]{1,0:T(8,128)(2,1)S(1)}, bf16[1024,128]{1,0:T(8,128)(2,1)S(1)}, u32[]{:S(2)}, u32[]{:S(2)}) collective-permute-start(bf16[1024,128]{1,0:T(8,128)(2,1)S(1)} %get-tuple-element.37), channel_id=1, source_target_pairs={{0,8},{8,0},{1,9},{9,1},{2,10},{10,2},{3,11},{11,3},{4,12},{12,4},... | collective-permute-start | bytes 786440 | tf_op jit(solution)/shard_map/ppermute | solution.py:422
  6.2 11.1 %collective-permute-start.1 = (bf16[512,128]{1,0:T(8,128)(2,1)S(1)}, bf16[512,128]{1,0:T(8,128)(2,1)S(1)}, u32[]{:S(2)}, u32[]{:S(2)}) collective-permute-start(bf16[512,128]{1,0:T(8,128)(2,1)S(1)} %get-tuple-element.38), channel_id=1, source_target_pairs={{0,1},{1,0},{2,3},{3,2},{4,5},{5,4},{6,7},{7,6},{8,9},{9,8},{10,11... | collective-permute-start | bytes 393224 | tf_op jit(solution)/shard_map/ppermute | solution.py:423
  8.8 8.5 %collective-permute-start.2 = (bf16[512,128]{1,0:T(8,128)(2,1)S(1)}, bf16[512,128]{1,0:T(8,128)(2,1)S(1)}, u32[]{:S(2)}, u32[]{:S(2)}) collective-permute-start(bf16[512,128]{1,0:T(8,128)(2,1)S(1)} %get-tuple-element.39), channel_id=1, source_target_pairs={{0,9},{1,8},{2,11},{3,10},{4,13},{5,12},{6,15},{7,14},{8,1},{9,0},... | collective-permute-start | bytes 393224 | tf_op jit(solution)/shard_map/ppermute | solution.py:424
  8.8 8.5 %collective-permute-start.3 = (bf16[512,128]{1,0:T(8,128)(2,1)S(1)}, bf16[512,128]{1,0:T(8,128)(2,1)S(1)}, u32[]{:S(2)}, u32[]{:S(2)}) collective-permute-start(bf16[512,128]{1,0:T(8,128)(2,1)S(1)} %get-tuple-element.40), channel_id=1, source_target_pairs={{1,2},{2,1},{3,4},{4,3},{5,6},{6,5},{9,10},{10,9},{11,12},{12,11},... | collective-permute-start | bytes 393224 | tf_op jit(solution)/shard_map/ppermute | solution.py:425
  9.4 2.3 %collective-permute-start.4 = (bf16[128,128]{1,0:T(8,128)(2,1)S(1)}, bf16[128,128]{1,0:T(8,128)(2,1)S(1)}, u32[]{:S(2)}, u32[]{:S(2)}) collective-permute-start(bf16[128,128]{1,0:T(8,128)(2,1)S(1)} %get-tuple-element.41), channel_id=1, source_target_pairs={{1,10},{2,9},{3,12},{4,11},{5,14},{6,13},{9,2},{10,1},{11,4},{12,3... | collective-permute-start | bytes 98312 | tf_op jit(solution)/shard_map/ppermute | solution.py:426
  23.0 5.9 %collective-permute-start.5 = (bf16[64,24,128]{2,1,0:T(8,128)(2,1)S(1)}, bf16[64,24,128]{2,1,0:T(8,128)(2,1)S(1)}, u32[]{:S(2)}, u32[]{:S(2)}) collective-permute-start(bf16[64,24,128]{2,1,0:T(8,128)(2,1)S(1)} %get-tuple-element.51), channel_id=1, source_target_pairs={{0,16},{16,0},{32,48},{48,32},{64,80},{80,64},{96,112},{112,96},{1... | collective-permute-start | bytes 1179656 | tf_op jit(solution)/shard_map/ppermute | solution.py:454
  29.7 21.4 %all-to-all-start = ((bf16[64,24,128]{2,1,0:T(8,128)(2,1)}), bf16[64,24,128]{2,1,0:T(8,128)(2,1)S(1)}, u32[]{:S(2)}, u32[]{:S(2)}) async-start(bf16[64,24,128]{2,1,0:T(8,128)(2,1)} %shard_map.114), calls=%async_computation | async-start | bytes 786432 | tf_op jit(solution)/shard_map/all_to_all | solution.py:461
  43.2 29.6 %copy-start.3 = (f32[4,16,32,128]{3,2,1,0:T(8,128)S(1)}, f32[4,16,32,128]{3,2,1,0:T(8,128)}, u32[]{:S(2)}) copy-start(f32[4,16,32,128]{3,2,1,0:T(8,128)} %get-tuple-element.55.refs_0_) | copy-start | bytes 3145732
  43.2 7.2 %collective-permute-start.6 = (bf16[16,32,128]{2,1,0:T(8,128)(2,1)S(1)}, bf16[16,32,128]{2,1,0:T(8,128)(2,1)S(1)}, u32[]{:S(2)}, u32[]{:S(2)}) collective-permute-start(bf16[16,32,128]{2,1,0:T(8,128)(2,1)S(1)} %get-tuple-element.54), channel_id=1, source_target_pairs={{0,8},{8,0},{1,9},{9,1},{2,10},{10,2},{3,11},{11,3},{4,12},{12,4},... | collective-permute-start | bytes 393224 | tf_op jit(solution)/shard_map/ppermute | solution.py:469
  51.1 23.1 %copy-start.1 = (f32[128,1728]{0,1:T(8,128)S(1)}, f32[128,1728]{0,1:T(8,128)}, u32[]{:S(2)}) copy-start(f32[128,1728]{0,1:T(8,128)} %param.11) | copy-start | bytes 2654212
  69.7 4.5 %collective-permute-start.7 = (bf16[64,32,128]{2,1,0:T(8,128)(2,1)S(1)}, bf16[64,32,128]{2,1,0:T(8,128)(2,1)S(1)}, u32[]{:S(2)}, u32[]{:S(2)}) collective-permute-start(bf16[64,32,128]{2,1,0:T(8,128)(2,1)S(1)} %all_to_all.10.full_ref), channel_id=1, source_target_pairs={{0,16},{16,0},{32,48},{48,32},{64,80},{80,64},{96,112},{112,96},{1... | collective-permute-start | bytes 1572872 | tf_op jit(solution)/shard_map/ppermute | solution.py:485

commit v8 on v7

--- a/solution.py
+++ b/solution.py
@@ -55,7 +55,7 @@
     loads = [pltpu.make_async_copy(cot_far, cot_ref, sems.at[0])]
     loads += [pltpu.make_async_copy(act_far.at[:, 3 * (1 - dep)], act_ref, sems.at[1])]
     loads += [pltpu.make_async_copy(pre_far.at[:, d], pre_ref.at[:, d], sems.at[2 + d]) for d in range(4)]
-    loads += [pltpu.make_async_copy(w3_far, w3_out, sems.at[6])]
+    loads += [pltpu.make_async_copy(w3_far, w3_out.at[:1728], sems.at[6])]
     for load in loads:
         load.start()
     loads[0].wait()
@@ -126,7 +126,7 @@
         for ow, value in enumerate(shifts(rows)):
             start = 96 * d + 32 * ow
             act_out[:, start : start + 32, :] = value.astype(BF16)
-    t2[...] = jnp.transpose(w2_ref[...])
+    t2[:864] = jnp.transpose(w2_ref[...])
     for kd in range(3):
         for oh in range(3):
             for ow in range(3):
@@ -382,7 +382,7 @@
             stage[pl.ds(32 * x + 16 * side, 16)] = moved[16 * x : 16 * x + 16]
     for b in range(14):
         rows = slice(128 * b, min(128 * b + 128, 1728))
-        w3_out[rows] = w3[rows] - jnp.transpose(stage[:, 4 + b, :])[: rows.stop - rows.start]
+        w3_out[rows] = w3[rows] - jnp.transpose(stage[:128, 4 + b, :])[: rows.stop - rows.start]
     halves = []
     for half in range(2):
         blocks = [stage[pl.ds(half, 64, stride=2), b, :] for b in range(4)]
@@ -407,7 +407,7 @@
         arrange,
         [((2, 128, 512), BF16), ((1024, 128), BF16), ((512, 128), BF16),
          ((512, 128), BF16), ((512, 128), BF16), ((128, 128), BF16),
-         ((1728, 128), F32)],
+         ((1792, 128), F32)],
         [pltpu.VMEM((128, 2, 512), BF16), pltpu.VMEM((64, 4, 16, 128), BF16), pltpu.VMEM((32, 16, 128), BF16),
          pltpu.SemaphoreType.DMA((7,))],
         moved=4_000_000, far=(0, 1, 2, 3),
@@ -428,7 +428,7 @@
     pre_rows, pooled, acts, wide_two, wide_three, moments = call(
         prepare,
         [((4, 16, 64, 128), BF16), ((128, 512), BF16), ((16, 384, 128), BF16), ((192, 768), BF16), ((192, 1152), BF16), ((24, 128), F32)],
-        [pltpu.VMEM((864, 64), F32)],
+        [pltpu.VMEM((896, 64), F32)],
         flops=100_000_000, moved=8_000_000,
     )(pre, act, weight_two, w3_near, moment_two, moment_three)
 
@@ -444,7 +444,7 @@
         fine,
         [((64, 24, 128), F32), ((64, 24, 128), BF16)],
         [pltpu.VMEM((4, 18, 64, 128), BF16), pltpu.VMEM((2, 10, 64, 128), F32), pltpu.VMEM((16, 96, 128), BF16), pltpu.VMEM((3, 96, 192), F32),
-         pltpu.VMEM((944, 64), F32), pltpu.VMEM((64, 24, 128), F32), pltpu.VMEM((4, 128, 128), F32)],
+         pltpu.VMEM((944, 64), F32), pltpu.VMEM((64, 24, 128), F32), pltpu.VMEM((4, 136, 128), F32)],
         flops=2_000_000_000, moved=6_000_000,
     )(back, pre_rows, got_a, got_b, acts, side, part_three, moments)
 
@@ -486,7 +486,7 @@
     new_weight_two, new_weight_three, new_moment_two, new_moment_three = call(
         update,
         [(weight_two.shape, F32), (weight_three.shape[::-1], F32), (moment_two.shape, F32), (moment_three.shape, F32)],
-        [pltpu.VMEM((128, 18, 128), F32)],
+        [pltpu.VMEM((136, 18, 128), F32)],
         moved=4_000_000,
     )(full, other, parts, own, w2, w3.T, moment_two, moment_three)
     return (grad_input[None], new_weight_two, new_weight_three.T, new_moment_two, new_moment_three)

time: 77.3 us -> 77.4 us (level)
  no operation moved by 1% of the time
where the time goes in v8:
time: 77.4 us; the launch traced here: 77 us
  starting transfers between devices  25 us (32%)
  Pallas kernels  19.1 us (25%)
  blocking collectives  17.7 us (23%)
  waiting for transfers between devices  14.4 us (19%)
  between operations  0.82 us (1%)
    pallas_call x9, Pallas kernels, run(): pl.pallas_call(body, out_shape=[pltpu.HBM(shape, dtype) if i in far_out e...  19.1 us
    all_to_all x1, blocking collectives, local(): lax.all_to_all(send, AXES, 0, 0, axis_index_groups=groups, tiled=True)  17.7 us
    all_to_all x1, starting transfers between devices, local(): lax.all_to_all(parts, AXES, 0, 0, axis_index_groups=groups, tiled=True)  10.3 us
    ppermute x1, waiting for transfers between devices, local(): ship = lax.ppermute(ship, 'depth', swap)  6.23 us
    ppermute x1, waiting for transfers between devices, local(): got_a = lax.ppermute(send_a, 'height', pairs_a)  5.56 us
    ppermute x1, starting transfers between devices, local(): got = lax.ppermute(theirs, 'dp', cores)  4.58 us
    ppermute x1, starting transfers between devices, local(): other = lax.ppermute(full, 'dp', cores)  3 us
    ppermute x1, starting transfers between devices, local(): got_a = lax.ppermute(send_a, 'height', pairs_a)  2.62 us
  transfers between devices with their start and end apart: 9, of which 5 were waited for; matrix products, arithmetic and copies ran while one was open for 0% of the time, Pallas kernels for 7%

profile of v8, /device:TPU:1, one launch (start us, length us, event | category | flops | bytes accessed | tf_op | source)
XLA Modules:
  0.0 77.0 jit_solution(15086018086175519654)
XLA Ops:
  0.6 0.0 copy-start
  0.6 0.0 copy-start.2
  0.7 0.0 copy-start.5
  0.7 0.0 copy-start.6
  0.7 3.3 %shard_map.110 = (bf16[2,128,512]{2,1,0:T(8,128)(2,1)S(1)}, bf16[1024,128]{1,0:T(8,128)(2,1)S(1)}, bf16[512,128]{1,0:T(8,128)(2,1)S(1)}, bf16[512,128]{1,0:T(8,1...) custom-call(bf16[128,2,512]{2,1,0:T(2,128)(2,1)} %bitcast.15, ...), custom_call_target="tpu_custom_call" | custom-call | bytes 4000000 | tf_op jit(solution)/shard_map/pallas_call | solution.py:20
  4.0 2.2 %collective-permute-start = (bf16[1024,128]{1,0:T(8,128)(2,1)S(1)}, bf16[1024,128]{1,0:T(8,128)(2,1)S(1)}, u32[]{:S(2)}, u32[]{:S(2)}) collective-permute-start(bf16[1024,128]{1,0:T(8,128)(2,1)S(1)} %get-tuple-element.37), channel_id=1, source_target_pairs={{0,8},{8,0},{1,9},{9,1},{2,10},{10,2},{3,11},{11,3},{4,12},{12,4},... | collective-permute-start | bytes 786440 | tf_op jit(solution)/shard_map/ppermute | solution.py:422
  6.2 2.6 %collective-permute-start.1 = (bf16[512,128]{1,0:T(8,128)(2,1)S(1)}, bf16[512,128]{1,0:T(8,128)(2,1)S(1)}, u32[]{:S(2)}, u32[]{:S(2)}) collective-permute-start(bf16[512,128]{1,0:T(8,128)(2,1)S(1)} %get-tuple-element.38), channel_id=1, source_target_pairs={{0,1},{1,0},{2,3},{3,2},{4,5},{5,4},{6,7},{7,6},{8,9},{9,8},{10,11... | collective-permute-start | bytes 393224 | tf_op jit(solution)/shard_map/ppermute | solution.py:423
  8.8 0.0 collective-permute-start.2
  8.8 0.7 collective-permute-start.3
  9.4 0.7 collective-permute-start.4
  10.2 1.6 %shard_map.111 = (bf16[4,16,64,128]{3,2,1,0:T(8,128)(2,1)S(1)}, bf16[128,512]{1,0:T(8,128)(2,1)S(1)}, bf16[16,384,128]{2,1,0:T(8,128)(2,1)S(1)}, bf16[192,768]{1...) custom-call(bf16[64,4,16,128]{3,2,1,0:T(8,128)(2,1)S(1)} %bitcast.8, ...), custom_call_target="tpu_custom_call" | custom-call | flops 100000000 | bytes 8000000 | tf_op jit(solution)/shard_map/pallas_call | solution.py:20
  11.7 0.0 collective-permute-done.4.refs_5_
  11.7 5.6 %collective-permute-done.1.refs_2_.a_ref = bf16[512,128]{1,0:T(8,128)(2,1)S(1)} collective-permute-done((bf16[512,128]{1,0:T(8,128)(2,1)S(1)}, bf16[512,128]{1,0:T(8,128)(2,1)S(1)}, u32[]{:S(2)}, u32[]{:S(2)}) %collective-permute-start.1) | collective-permute-done | bytes 131104 | tf_op jit(solution)/shard_map/ppermute | solution.py:423
  17.3 0.0 collective-permute-done.2.refs_3_
  17.3 0.0 collective-permute-done.3.refs_4_.b_ref
  17.3 0.0 collective-permute-done.refs_1_.side_ref
  17.3 2.8 %shard_map.112 = (bf16[2,64,768]{2,1,0:T(8,128)(2,1)S(1)}, f32[14,128,128]{2,1,0:T(8,128)S(1)}) custom-call(bf16[2,128,512]{2,1,0:T(8,128)(2,1)S(1)} %get-tuple-element.36.refs_0_, bf16[1024,128]{1,0:T(8,128)(2,1)S(1)} %collective-permute-done.refs_1_.side_ref, bf16[512,128]{1,0:T(8,128)(2,1)S(1)} %collective-permute-done.1.refs_2_.a_ref, ...), custom_call_target="tpu_custom_call" | custom-call | flops 2000000000 | bytes 4000000 | tf_op jit(solution)/shard_map/pallas_call | solution.py:20
  20.2 2.8 %shard_map.113 = (f32[64,24,128]{2,1,0:T(8,128)S(1)}, bf16[64,24,128]{2,1,0:T(8,128)(2,1)S(1)}) custom-call(bf16[2,64,768]{2,1,0:T(8,128)(2,1)S(1)} %get-tuple-element.45.back_ref, bf16[4,16,64,128]{3,2,1,0:T(8,128)(2,1)S(1)} %get-tuple-element.46.pre_ref, bf16[512,128]{1,0:T(8,128)(2,1)S(1)} %collective-permute-done.1.refs_2_.a_ref, ...), custom_call_target="tpu_custom_call" | custom-call | flops 2000000000 | bytes 6000000 | tf_op jit(solution)/shard_map/pallas_call | solution.py:20
  23.0 4.6 %collective-permute-start.5 = (bf16[64,24,128]{2,1,0:T(8,128)(2,1)S(1)}, bf16[64,24,128]{2,1,0:T(8,128)(2,1)S(1)}, u32[]{:S(2)}, u32[]{:S(2)}) collective-permute-start(bf16[64,24,128]{2,1,0:T(8,128)(2,1)S(1)} %get-tuple-element.51), channel_id=1, source_target_pairs={{0,16},{16,0},{32,48},{48,32},{64,80},{80,64},{96,112},{112,96},{1... | collective-permute-start | bytes 1179656 | tf_op jit(solution)/shard_map/ppermute | solution.py:454
  27.6 1.3 %collective-permute-done.5.got_ref = bf16[64,24,128]{2,1,0:T(8,128)(2,1)S(1)} collective-permute-done((bf16[64,24,128]{2,1,0:T(8,128)(2,1)S(1)}, bf16[64,24,128]{2,1,0:T(8,128)(2,1)S(1)}, u32[]{:S(2)}, u32[]{:S(2)}) %collective-permute-start.5) | collective-permute-done | bytes 393248 | tf_op jit(solution)/shard_map/ppermute | solution.py:454
  28.9 0.8 %shard_map.114 = bf16[64,24,128]{2,1,0:T(8,128)(2,1)} custom-call(f32[64,24,128]{2,1,0:T(8,128)S(1)} %get-tuple-element.50.mine_ref, bf16[64,24,128]{2,1,0:T(8,128)(2,1)S(1)} %collective-permute-done.5.got_ref), custom_call_target="tpu_custom_call" | custom-call | bytes 2000000 | tf_op jit(solution)/shard_map/pallas_call | solution.py:20
  29.7 10.3 %all-to-all-start = ((bf16[64,24,128]{2,1,0:T(8,128)(2,1)}), bf16[64,24,128]{2,1,0:T(8,128)(2,1)S(1)}, u32[]{:S(2)}, u32[]{:S(2)}) async-start(bf16[64,24,128]{2,1,0:T(8,128)(2,1)} %shard_map.114), calls=%async_computation | async-start | bytes 786432 | tf_op jit(solution)/shard_map/all_to_all | solution.py:461
  40.1 3.1 %shard_map.115 = (f32[4,16,32,128]{3,2,1,0:T(8,128)}, bf16[16,32,128]{2,1,0:T(8,128)(2,1)S(1)}) custom-call(bf16[2,64,768]{2,1,0:T(8,128)(2,1)S(1)} %get-tuple-element.45.back_ref, bf16[64,4,16,128]{3,2,1,0:T(8,128)(2,1)S(1)} %bitcast.9, bf16[512,128]{1,0:T(8,128)(2,1)S(1)} %collective-permute-done.1.refs_2_.a_ref, ...), custom_call_target="tpu_custom_call" | custom-call | flops 4000000000 | bytes 6000000 | tf_op jit(solution)/shard_map/pallas_call | solution.py:20
  43.2 0.9 %collective-permute-start.6 = (bf16[16,32,128]{2,1,0:T(8,128)(2,1)S(1)}, bf16[16,32,128]{2,1,0:T(8,128)(2,1)S(1)}, u32[]{:S(2)}, u32[]{:S(2)}) collective-permute-start(bf16[16,32,128]{2,1,0:T(8,128)(2,1)S(1)} %get-tuple-element.54), channel_id=1, source_target_pairs={{0,8},{8,0},{1,9},{9,1},{2,10},{10,2},{3,11},{11,3},{4,12},{12,4},... | collective-permute-start | bytes 393224 | tf_op jit(solution)/shard_map/ppermute | solution.py:469
  44.1 6.2 %collective-permute-done.6.refs_1_ = bf16[16,32,128]{2,1,0:T(8,128)(2,1)S(1)} collective-permute-done((bf16[16,32,128]{2,1,0:T(8,128)(2,1)S(1)}, bf16[16,32,128]{2,1,0:T(8,128)(2,1)S(1)}, u32[]{:S(2)}, u32[]{:S(2)}) %collective-permute-start.6) | collective-permute-done | bytes 131104 | tf_op jit(solution)/shard_map/ppermute | solution.py:469
  50.3 0.8 %all-to-all-done.refs_0_.first_ref = bf16[64,24,128]{2,1,0:T(8,128)(2,1)S(1)} async-done(((bf16[64,24,128]{2,1,0:T(8,128)(2,1)}), bf16[64,24,128]{2,1,0:T(8,128)(2,1)S(1)}, u32[]{:S(2)}, u32[]{:S(2)}) %all-to-all-start) | async-done | bytes 393248 | tf_op jit(solution)/shard_map/all_to_all | solution.py:461
  51.1 0.9 %shard_map.117 = (bf16[64,32,128]{2,1,0:T(8,128)(2,1)}, f32[18,128]{1,0:T(8,128)S(1)}) custom-call(bf16[64,24,128]{2,1,0:T(8,128)(2,1)S(1)} %all-to-all-done.refs_0_.first_ref, f32[24,128]{1,0:T(8,128)S(1)} %get-tuple-element.49.m_ref.refs_1_), custom_call_target="tpu_custom_call" | custom-call | bytes 2000000 | tf_op jit(solution)/shard_map/pallas_call | solution.py:20
  52.1 17.7 %all_to_all.10.full_ref = bf16[64,32,128]{2,1,0:T(8,128)(2,1)S(1)} all-to-all(bf16[64,32,128]{2,1,0:T(8,128)(2,1)} %get-tuple-element.58), channel_id=1, replica_groups={{0,1,2,3,4,5,6,7,8,9,10,11,12,13,14,15,32,33,34,35,36,37,38,39,40,41,42..., dimensions={0} | all-to-all | bytes 1048576 | tf_op jit(solution)/shard_map/all_to_all | solution.py:484
  69.7 3.0 %collective-permute-start.7 = (bf16[64,32,128]{2,1,0:T(8,128)(2,1)S(1)}, bf16[64,32,128]{2,1,0:T(8,128)(2,1)S(1)}, u32[]{:S(2)}, u32[]{:S(2)}) collective-permute-start(bf16[64,32,128]{2,1,0:T(8,128)(2,1)S(1)} %all_to_all.10.full_ref), channel_id=1, source_target_pairs={{0,16},{16,0},{32,48},{48,32},{64,80},{80,64},{96,112},{112,96},{1... | collective-permute-start | bytes 1572872 | tf_op jit(solution)/shard_map/ppermute | solution.py:485
  72.7 1.1 %shard_map.116 = bf16[32,4,16,128]{3,2,1,0:T(8,128)(2,1)} custom-call(f32[4,16,32,128]{3,2,1,0:T(8,128)S(1)} %copy-done.3, bf16[16,32,128]{2,1,0:T(8,128)(2,1)S(1)} %collective-permute-done.6.refs_1_), custom_call_target="tpu_custom_call" | custom-call | bytes 2000000 | tf_op jit(solution)/shard_map/pallas_call | solution.py:20
  73.8 0.5 collective-permute-done.7.other_ref
  74.3 2.7 %shard_map.118 = (f32[64,864]{1,0:T(8,128)}, f32[1728,128]{1,0:T(8,128)}, f32[432]{0:T(512)}, f32[1728]{0:T(1024)}) custom-call(bf16[64,32,128]{2,1,0:T(8,128)(2,1)S(1)} %all_to_all.10.full_ref, bf16[64,32,128]{2,1,0:T(8,128)(2,1)S(1)} %collective-permute-done.7.other_ref, bf16[64,24,128]{2,1,0:T(8,128)(2,1)S(1)} %all-to-all-done.refs_0_.first_ref, ...), custom_call_target="tpu_custom_call" | custom-call | bytes 4000000 | tf_op jit(solution)/shard_map/pallas_call | solution.py:20
  (10 shorter events, 0.0 us)
Async XLA Ops:
  0.6 9.5 %copy-start = (bf16[1,64,4,16,128]{4,3,2,1,0:T(8,128)(2,1)S(1)}, bf16[1,64,4,16,128]{4,3,2,1,0:T(8,128)(2,1)}, u32[]{:S(2)}) copy-start(bf16[1,64,4,16,128]{4,3,2,1,0:T(8,128)(2,1)} %param.8) | copy-start | bytes 3145732
  0.6 9.5 %copy-start.2 = (bf16[1,32,4,16,128]{4,3,2,1,0:T(8,128)(2,1)S(1)}, bf16[1,32,4,16,128]{4,3,2,1,0:T(8,128)(2,1)}, u32[]{:S(2)}) copy-start(bf16[1,32,4,16,128]{4,3,2,1,0:T(8,128)(2,1)} %param.7) | copy-start | bytes 1572868
  0.7 9.5 %copy-start.5 = (f32[1728]{0:T(1024)S(1)}, f32[1728]{0:T(1024)}, u32[]{:S(2)}) copy-start(f32[1728]{0:T(1024)} %m3_ref.3) | copy-start | bytes 20740
  0.7 9.5 %copy-start.6 = (f32[432]{0:T(512)S(1)}, f32[432]{0:T(512)}, u32[]{:S(2)}) copy-start(f32[432]{0:T(512)} %m2_ref.3) | copy-start | bytes 5188
  0.7 9.5 %copy-start.4 = (f32[64,864]{1,0:T(8,128)S(1)}, f32[64,864]{1,0:T(8,128)}, u32[]{:S(2)}) copy-start(f32[64,864]{1,0:T(8,128)} %w2_ref.2) | copy-start | bytes 663556
  4.0 13.4 %collective-permute-start = (bf16[1024,128]{1,0:T(8,128)(2,1)S(1)}, bf16[1024,128]{1,0:T(8,128)(2,1)S(1)}, u32[]{:S(2)}, u32[]{:S(2)}) collective-permute-start(bf16[1024,128]{1,0:T(8,128)(2,1)S(1)} %get-tuple-element.37), channel_id=1, source_target_pairs={{0,8},{8,0},{1,9},{9,1},{2,10},{10,2},{3,11},{11,3},{4,12},{12,4},... | collective-permute-start | bytes 786440 | tf_op jit(solution)/shard_map/ppermute | solution.py:422
  6.2 11.1 %collective-permute-start.1 = (bf16[512,128]{1,0:T(8,128)(2,1)S(1)}, bf16[512,128]{1,0:T(8,128)(2,1)S(1)}, u32[]{:S(2)}, u32[]{:S(2)}) collective-permute-start(bf16[512,128]{1,0:T(8,128)(2,1)S(1)} %get-tuple-element.38), channel_id=1, source_target_pairs={{0,1},{1,0},{2,3},{3,2},{4,5},{5,4},{6,7},{7,6},{8,9},{9,8},{10,11... | collective-permute-start | bytes 393224 | tf_op jit(solution)/shard_map/ppermute | solution.py:423
  8.8 8.5 %collective-permute-start.2 = (bf16[512,128]{1,0:T(8,128)(2,1)S(1)}, bf16[512,128]{1,0:T(8,128)(2,1)S(1)}, u32[]{:S(2)}, u32[]{:S(2)}) collective-permute-start(bf16[512,128]{1,0:T(8,128)(2,1)S(1)} %get-tuple-element.39), channel_id=1, source_target_pairs={{0,9},{1,8},{2,11},{3,10},{4,13},{5,12},{6,15},{7,14},{8,1},{9,0},... | collective-permute-start | bytes 393224 | tf_op jit(solution)/shard_map/ppermute | solution.py:424
  8.8 8.5 %collective-permute-start.3 = (bf16[512,128]{1,0:T(8,128)(2,1)S(1)}, bf16[512,128]{1,0:T(8,128)(2,1)S(1)}, u32[]{:S(2)}, u32[]{:S(2)}) collective-permute-start(bf16[512,128]{1,0:T(8,128)(2,1)S(1)} %get-tuple-element.40), channel_id=1, source_target_pairs={{1,2},{2,1},{3,4},{4,3},{5,6},{6,5},{9,10},{10,9},{11,12},{12,11},... | collective-permute-start | bytes 393224 | tf_op jit(solution)/shard_map/ppermute | solution.py:425
  9.4 2.3 %collective-permute-start.4 = (bf16[128,128]{1,0:T(8,128)(2,1)S(1)}, bf16[128,128]{1,0:T(8,128)(2,1)S(1)}, u32[]{:S(2)}, u32[]{:S(2)}) collective-permute-start(bf16[128,128]{1,0:T(8,128)(2,1)S(1)} %get-tuple-element.41), channel_id=1, source_target_pairs={{1,10},{2,9},{3,12},{4,11},{5,14},{6,13},{9,2},{10,1},{11,4},{12,3... | collective-permute-start | bytes 98312 | tf_op jit(solution)/shard_map/ppermute | solution.py:426
  23.0 5.9 %collective-permute-start.5 = (bf16[64,24,128]{2,1,0:T(8,128)(2,1)S(1)}, bf16[64,24,128]{2,1,0:T(8,128)(2,1)S(1)}, u32[]{:S(2)}, u32[]{:S(2)}) collective-permute-start(bf16[64,24,128]{2,1,0:T(8,128)(2,1)S(1)} %get-tuple-element.51), channel_id=1, source_target_pairs={{0,16},{16,0},{32,48},{48,32},{64,80},{80,64},{96,112},{112,96},{1... | collective-permute-start | bytes 1179656 | tf_op jit(solution)/shard_map/ppermute | solution.py:454
  29.7 21.4 %all-to-all-start = ((bf16[64,24,128]{2,1,0:T(8,128)(2,1)}), bf16[64,24,128]{2,1,0:T(8,128)(2,1)S(1)}, u32[]{:S(2)}, u32[]{:S(2)}) async-start(bf16[64,24,128]{2,1,0:T(8,128)(2,1)} %shard_map.114), calls=%async_computation | async-start | bytes 786432 | tf_op jit(solution)/shard_map/all_to_all | solution.py:461
  43.2 29.6 %copy-start.3 = (f32[4,16,32,128]{3,2,1,0:T(8,128)S(1)}, f32[4,16,32,128]{3,2,1,0:T(8,128)}, u32[]{:S(2)}) copy-start(f32[4,16,32,128]{3,2,1,0:T(8,128)} %get-tuple-element.55.refs_0_) | copy-start | bytes 3145732
  43.2 7.2 %collective-permute-start.6 = (bf16[16,32,128]{2,1,0:T(8,128)(2,1)S(1)}, bf16[16,32,128]{2,1,0:T(8,128)(2,1)S(1)}, u32[]{:S(2)}, u32[]{:S(2)}) collective-permute-start(bf16[16,32,128]{2,1,0:T(8,128)(2,1)S(1)} %get-tuple-element.54), channel_id=1, source_target_pairs={{0,8},{8,0},{1,9},{9,1},{2,10},{10,2},{3,11},{11,3},{4,12},{12,4},... | collective-permute-start | bytes 393224 | tf_op jit(solution)/shard_map/ppermute | solution.py:469
  51.1 23.1 %copy-start.1 = (f32[128,1728]{0,1:T(8,128)S(1)}, f32[128,1728]{0,1:T(8,128)}, u32[]{:S(2)}) copy-start(f32[128,1728]{0,1:T(8,128)} %param.11) | copy-start | bytes 2654212
  69.7 4.5 %collective-permute-start.7 = (bf16[64,32,128]{2,1,0:T(8,128)(2,1)S(1)}, bf16[64,32,128]{2,1,0:T(8,128)(2,1)S(1)}, u32[]{:S(2)}, u32[]{:S(2)}) collective-permute-start(bf16[64,32,128]{2,1,0:T(8,128)(2,1)S(1)} %all_to_all.10.full_ref), channel_id=1, source_target_pairs={{0,16},{16,0},{32,48},{48,32},{64,80},{80,64},{96,112},{112,96},{1... | collective-permute-start | bytes 1572872 | tf_op jit(solution)/shard_map/ppermute | solution.py:485

commit v9 on v8

--- a/solution.py
+++ b/solution.py
@@ -237,15 +237,9 @@
         near[:, 32 * ow : 32 * ow + 32, :] = value.astype(BF16)
 
     def correlate(z, lhs):
-        total = None
-        for h in range(4):
-            left = jnp.concatenate([lhs(h + 4 * i) for i in range(4)], axis=1)
-            right = jnp.concatenate(
-                [z_out[z, h + 4 * i : h + 4 * i + 3].reshape(192, 128) for i in range(4)], axis=1
-            )
-            r = dot_nt(left, right)
-            total = r if total is None else total + r
-        return total
+        left = jnp.concatenate([lhs(h) for h in range(16)], axis=1)
+        right = jnp.concatenate([z_out[z, h : h + 3].reshape(192, 128) for h in range(16)], axis=1)
+        return dot_nt(left, right)
 
     sums = [None, None, None]
     for z in range(4):

time: 77.4 us -> 77.2 us (level)
  no operation moved by 1% of the time
where the time goes in v9:
time: 77.2 us; the launch traced here: 76.9 us
  starting transfers between devices  25 us (32%)
  Pallas kernels  19 us (25%)
  blocking collectives  17.7 us (23%)
  waiting for transfers between devices  14.4 us (19%)
  between operations  0.82 us (1%)
    pallas_call x9, Pallas kernels, run(): pl.pallas_call(body, out_shape=[pltpu.HBM(shape, dtype) if i in far_out e...  19 us
    all_to_all x1, blocking collectives, local(): lax.all_to_all(send, AXES, 0, 0, axis_index_groups=groups, tiled=True)  17.7 us
    all_to_all x1, starting transfers between devices, local(): lax.all_to_all(parts, AXES, 0, 0, axis_index_groups=groups, tiled=True)  10.3 us
    ppermute x1, waiting for transfers between devices, local(): ship = lax.ppermute(ship, 'depth', swap)  6.23 us
    ppermute x1, waiting for transfers between devices, local(): got_a = lax.ppermute(send_a, 'height', pairs_a)  5.56 us
    ppermute x1, starting transfers between devices, local(): got = lax.ppermute(theirs, 'dp', cores)  4.58 us
    ppermute x1, starting transfers between devices, local(): other = lax.ppermute(full, 'dp', cores)  3.01 us
    ppermute x1, starting transfers between devices, local(): got_a = lax.ppermute(send_a, 'height', pairs_a)  2.62 us
  transfers between devices with their start and end apart: 9, of which 5 were waited for; matrix products, arithmetic and copies ran while one was open for 0% of the time, Pallas kernels for 7%

profile of v9, /device:TPU:1, one launch (start us, length us, event | category | flops | bytes accessed | tf_op | source)
XLA Modules:
  0.0 76.9 jit_solution(8395716453479035275)
XLA Ops:
  0.6 0.0 copy-start
  0.6 0.0 copy-start.2
  0.7 0.0 copy-start.5
  0.7 0.0 copy-start.6
  0.7 3.3 %shard_map.110 = (bf16[2,128,512]{2,1,0:T(8,128)(2,1)S(1)}, bf16[1024,128]{1,0:T(8,128)(2,1)S(1)}, bf16[512,128]{1,0:T(8,128)(2,1)S(1)}, bf16[512,128]{1,0:T(8,1...) custom-call(bf16[128,2,512]{2,1,0:T(2,128)(2,1)} %bitcast.15, ...), custom_call_target="tpu_custom_call" | custom-call | bytes 4000000 | tf_op jit(solution)/shard_map/pallas_call | solution.py:20
  4.0 2.2 %collective-permute-start = (bf16[1024,128]{1,0:T(8,128)(2,1)S(1)}, bf16[1024,128]{1,0:T(8,128)(2,1)S(1)}, u32[]{:S(2)}, u32[]{:S(2)}) collective-permute-start(bf16[1024,128]{1,0:T(8,128)(2,1)S(1)} %get-tuple-element.37), channel_id=1, source_target_pairs={{0,8},{8,0},{1,9},{9,1},{2,10},{10,2},{3,11},{11,3},{4,12},{12,4},... | collective-permute-start | bytes 786440 | tf_op jit(solution)/shard_map/ppermute | solution.py:416
  6.2 2.6 %collective-permute-start.1 = (bf16[512,128]{1,0:T(8,128)(2,1)S(1)}, bf16[512,128]{1,0:T(8,128)(2,1)S(1)}, u32[]{:S(2)}, u32[]{:S(2)}) collective-permute-start(bf16[512,128]{1,0:T(8,128)(2,1)S(1)} %get-tuple-element.38), channel_id=1, source_target_pairs={{0,1},{1,0},{2,3},{3,2},{4,5},{5,4},{6,7},{7,6},{8,9},{9,8},{10,11... | collective-permute-start | bytes 393224 | tf_op jit(solution)/shard_map/ppermute | solution.py:417
  8.8 0.0 collective-permute-start.2
  8.8 0.7 collective-permute-start.3
  9.4 0.7 collective-permute-start.4
  10.2 1.6 %shard_map.111 = (bf16[4,16,64,128]{3,2,1,0:T(8,128)(2,1)S(1)}, bf16[128,512]{1,0:T(8,128)(2,1)S(1)}, bf16[16,384,128]{2,1,0:T(8,128)(2,1)S(1)}, bf16[192,768]{1...) custom-call(bf16[64,4,16,128]{3,2,1,0:T(8,128)(2,1)S(1)} %bitcast.8, ...), custom_call_target="tpu_custom_call" | custom-call | flops 100000000 | bytes 8000000 | tf_op jit(solution)/shard_map/pallas_call | solution.py:20
  11.7 0.0 collective-permute-done.4.refs_5_
  11.7 5.6 %collective-permute-done.1.refs_2_.a_ref = bf16[512,128]{1,0:T(8,128)(2,1)S(1)} collective-permute-done((bf16[512,128]{1,0:T(8,128)(2,1)S(1)}, bf16[512,128]{1,0:T(8,128)(2,1)S(1)}, u32[]{:S(2)}, u32[]{:S(2)}) %collective-permute-start.1) | collective-permute-done | bytes 131104 | tf_op jit(solution)/shard_map/ppermute | solution.py:417
  17.3 0.0 collective-permute-done.2.refs_3_
  17.3 0.0 collective-permute-done.3.refs_4_.b_ref
  17.3 0.0 collective-permute-done.refs_1_.side_ref
  17.3 2.8 %shard_map.112 = (bf16[2,64,768]{2,1,0:T(8,128)(2,1)S(1)}, f32[14,128,128]{2,1,0:T(8,128)S(1)}) custom-call(bf16[2,128,512]{2,1,0:T(8,128)(2,1)S(1)} %get-tuple-element.36.refs_0_, bf16[1024,128]{1,0:T(8,128)(2,1)S(1)} %collective-permute-done.refs_1_.side_ref, bf16[512,128]{1,0:T(8,128)(2,1)S(1)} %collective-permute-done.1.refs_2_.a_ref, ...), custom_call_target="tpu_custom_call" | custom-call | flops 2000000000 | bytes 4000000 | tf_op jit(solution)/shard_map/pallas_call | solution.py:20
  20.2 2.7 %shard_map.113 = (f32[64,24,128]{2,1,0:T(8,128)S(1)}, bf16[64,24,128]{2,1,0:T(8,128)(2,1)S(1)}) custom-call(bf16[2,64,768]{2,1,0:T(8,128)(2,1)S(1)} %get-tuple-element.45.back_ref, bf16[4,16,64,128]{3,2,1,0:T(8,128)(2,1)S(1)} %get-tuple-element.46.pre_ref, bf16[512,128]{1,0:T(8,128)(2,1)S(1)} %collective-permute-done.1.refs_2_.a_ref, ...), custom_call_target="tpu_custom_call" | custom-call | flops 2000000000 | bytes 6000000 | tf_op jit(solution)/shard_map/pallas_call | solution.py:20
  22.9 4.6 %collective-permute-start.5 = (bf16[64,24,128]{2,1,0:T(8,128)(2,1)S(1)}, bf16[64,24,128]{2,1,0:T(8,128)(2,1)S(1)}, u32[]{:S(2)}, u32[]{:S(2)}) collective-permute-start(bf16[64,24,128]{2,1,0:T(8,128)(2,1)S(1)} %get-tuple-element.51), channel_id=1, source_target_pairs={{0,16},{16,0},{32,48},{48,32},{64,80},{80,64},{96,112},{112,96},{1... | collective-permute-start | bytes 1179656 | tf_op jit(solution)/shard_map/ppermute | solution.py:448
  27.4 1.3 %collective-permute-done.5.got_ref = bf16[64,24,128]{2,1,0:T(8,128)(2,1)S(1)} collective-permute-done((bf16[64,24,128]{2,1,0:T(8,128)(2,1)S(1)}, bf16[64,24,128]{2,1,0:T(8,128)(2,1)S(1)}, u32[]{:S(2)}, u32[]{:S(2)}) %collective-permute-start.5) | collective-permute-done | bytes 393248 | tf_op jit(solution)/shard_map/ppermute | solution.py:448
  28.8 0.8 %shard_map.114 = bf16[64,24,128]{2,1,0:T(8,128)(2,1)} custom-call(f32[64,24,128]{2,1,0:T(8,128)S(1)} %get-tuple-element.50.mine_ref, bf16[64,24,128]{2,1,0:T(8,128)(2,1)S(1)} %collective-permute-done.5.got_ref), custom_call_target="tpu_custom_call" | custom-call | bytes 2000000 | tf_op jit(solution)/shard_map/pallas_call | solution.py:20
  29.6 10.3 %all-to-all-start = ((bf16[64,24,128]{2,1,0:T(8,128)(2,1)}), bf16[64,24,128]{2,1,0:T(8,128)(2,1)S(1)}, u32[]{:S(2)}, u32[]{:S(2)}) async-start(bf16[64,24,128]{2,1,0:T(8,128)(2,1)} %shard_map.114), calls=%async_computation | async-start | bytes 786432 | tf_op jit(solution)/shard_map/all_to_all | solution.py:455
  39.9 3.1 %shard_map.115 = (f32[4,16,32,128]{3,2,1,0:T(8,128)}, bf16[16,32,128]{2,1,0:T(8,128)(2,1)S(1)}) custom-call(bf16[2,64,768]{2,1,0:T(8,128)(2,1)S(1)} %get-tuple-element.45.back_ref, bf16[64,4,16,128]{3,2,1,0:T(8,128)(2,1)S(1)} %bitcast.9, bf16[512,128]{1,0:T(8,128)(2,1)S(1)} %collective-permute-done.1.refs_2_.a_ref, ...), custom_call_target="tpu_custom_call" | custom-call | flops 4000000000 | bytes 6000000 | tf_op jit(solution)/shard_map/pallas_call | solution.py:20
  43.1 0.9 %collective-permute-start.6 = (bf16[16,32,128]{2,1,0:T(8,128)(2,1)S(1)}, bf16[16,32,128]{2,1,0:T(8,128)(2,1)S(1)}, u32[]{:S(2)}, u32[]{:S(2)}) collective-permute-start(bf16[16,32,128]{2,1,0:T(8,128)(2,1)S(1)} %get-tuple-element.54), channel_id=1, source_target_pairs={{0,8},{8,0},{1,9},{9,1},{2,10},{10,2},{3,11},{11,3},{4,12},{12,4},... | collective-permute-start | bytes 393224 | tf_op jit(solution)/shard_map/ppermute | solution.py:463
  44.0 6.2 %collective-permute-done.6.refs_1_ = bf16[16,32,128]{2,1,0:T(8,128)(2,1)S(1)} collective-permute-done((bf16[16,32,128]{2,1,0:T(8,128)(2,1)S(1)}, bf16[16,32,128]{2,1,0:T(8,128)(2,1)S(1)}, u32[]{:S(2)}, u32[]{:S(2)}) %collective-permute-start.6) | collective-permute-done | bytes 131104 | tf_op jit(solution)/shard_map/ppermute | solution.py:463
  50.2 0.8 %all-to-all-done.refs_0_.first_ref = bf16[64,24,128]{2,1,0:T(8,128)(2,1)S(1)} async-done(((bf16[64,24,128]{2,1,0:T(8,128)(2,1)}), bf16[64,24,128]{2,1,0:T(8,128)(2,1)S(1)}, u32[]{:S(2)}, u32[]{:S(2)}) %all-to-all-start) | async-done | bytes 393248 | tf_op jit(solution)/shard_map/all_to_all | solution.py:455
  51.0 0.9 %shard_map.117 = (bf16[64,32,128]{2,1,0:T(8,128)(2,1)}, f32[18,128]{1,0:T(8,128)S(1)}) custom-call(bf16[64,24,128]{2,1,0:T(8,128)(2,1)S(1)} %all-to-all-done.refs_0_.first_ref, f32[24,128]{1,0:T(8,128)S(1)} %get-tuple-element.49.m_ref.refs_1_), custom_call_target="tpu_custom_call" | custom-call | bytes 2000000 | tf_op jit(solution)/shard_map/pallas_call | solution.py:20
  51.9 17.7 %all_to_all.10.full_ref = bf16[64,32,128]{2,1,0:T(8,128)(2,1)S(1)} all-to-all(bf16[64,32,128]{2,1,0:T(8,128)(2,1)} %get-tuple-element.58), channel_id=1, replica_groups={{0,1,2,3,4,5,6,7,8,9,10,11,12,13,14,15,32,33,34,35,36,37,38,39,40,41,42..., dimensions={0} | all-to-all | bytes 1048576 | tf_op jit(solution)/shard_map/all_to_all | solution.py:478
  69.6 3.0 %collective-permute-start.7 = (bf16[64,32,128]{2,1,0:T(8,128)(2,1)S(1)}, bf16[64,32,128]{2,1,0:T(8,128)(2,1)S(1)}, u32[]{:S(2)}, u32[]{:S(2)}) collective-permute-start(bf16[64,32,128]{2,1,0:T(8,128)(2,1)S(1)} %all_to_all.10.full_ref), channel_id=1, source_target_pairs={{0,16},{16,0},{32,48},{48,32},{64,80},{80,64},{96,112},{112,96},{1... | collective-permute-start | bytes 1572872 | tf_op jit(solution)/shard_map/ppermute | solution.py:479
  72.6 1.1 %shard_map.116 = bf16[32,4,16,128]{3,2,1,0:T(8,128)(2,1)} custom-call(f32[4,16,32,128]{3,2,1,0:T(8,128)S(1)} %copy-done.3, bf16[16,32,128]{2,1,0:T(8,128)(2,1)S(1)} %collective-permute-done.6.refs_1_), custom_call_target="tpu_custom_call" | custom-call | bytes 2000000 | tf_op jit(solution)/shard_map/pallas_call | solution.py:20
  73.7 0.5 collective-permute-done.7.other_ref
  74.1 2.7 %shard_map.118 = (f32[64,864]{1,0:T(8,128)}, f32[1728,128]{1,0:T(8,128)}, f32[432]{0:T(512)}, f32[1728]{0:T(1024)}) custom-call(bf16[64,32,128]{2,1,0:T(8,128)(2,1)S(1)} %all_to_all.10.full_ref, bf16[64,32,128]{2,1,0:T(8,128)(2,1)S(1)} %collective-permute-done.7.other_ref, bf16[64,24,128]{2,1,0:T(8,128)(2,1)S(1)} %all-to-all-done.refs_0_.first_ref, ...), custom_call_target="tpu_custom_call" | custom-call | bytes 4000000 | tf_op jit(solution)/shard_map/pallas_call | solution.py:20
  (10 shorter events, 0.0 us)
Async XLA Ops:
  0.6 9.5 %copy-start = (bf16[1,64,4,16,128]{4,3,2,1,0:T(8,128)(2,1)S(1)}, bf16[1,64,4,16,128]{4,3,2,1,0:T(8,128)(2,1)}, u32[]{:S(2)}) copy-start(bf16[1,64,4,16,128]{4,3,2,1,0:T(8,128)(2,1)} %param.8) | copy-start | bytes 3145732
  0.6 9.5 %copy-start.2 = (bf16[1,32,4,16,128]{4,3,2,1,0:T(8,128)(2,1)S(1)}, bf16[1,32,4,16,128]{4,3,2,1,0:T(8,128)(2,1)}, u32[]{:S(2)}) copy-start(bf16[1,32,4,16,128]{4,3,2,1,0:T(8,128)(2,1)} %param.7) | copy-start | bytes 1572868
  0.7 9.5 %copy-start.5 = (f32[1728]{0:T(1024)S(1)}, f32[1728]{0:T(1024)}, u32[]{:S(2)}) copy-start(f32[1728]{0:T(1024)} %m3_ref.3) | copy-start | bytes 20740
  0.7 9.5 %copy-start.6 = (f32[432]{0:T(512)S(1)}, f32[432]{0:T(512)}, u32[]{:S(2)}) copy-start(f32[432]{0:T(512)} %m2_ref.3) | copy-start | bytes 5188
  0.7 9.5 %copy-start.4 = (f32[64,864]{1,0:T(8,128)S(1)}, f32[64,864]{1,0:T(8,128)}, u32[]{:S(2)}) copy-start(f32[64,864]{1,0:T(8,128)} %w2_ref.2) | copy-start | bytes 663556
  4.0 13.4 %collective-permute-start = (bf16[1024,128]{1,0:T(8,128)(2,1)S(1)}, bf16[1024,128]{1,0:T(8,128)(2,1)S(1)}, u32[]{:S(2)}, u32[]{:S(2)}) collective-permute-start(bf16[1024,128]{1,0:T(8,128)(2,1)S(1)} %get-tuple-element.37), channel_id=1, source_target_pairs={{0,8},{8,0},{1,9},{9,1},{2,10},{10,2},{3,11},{11,3},{4,12},{12,4},... | collective-permute-start | bytes 786440 | tf_op jit(solution)/shard_map/ppermute | solution.py:416
  6.2 11.1 %collective-permute-start.1 = (bf16[512,128]{1,0:T(8,128)(2,1)S(1)}, bf16[512,128]{1,0:T(8,128)(2,1)S(1)}, u32[]{:S(2)}, u32[]{:S(2)}) collective-permute-start(bf16[512,128]{1,0:T(8,128)(2,1)S(1)} %get-tuple-element.38), channel_id=1, source_target_pairs={{0,1},{1,0},{2,3},{3,2},{4,5},{5,4},{6,7},{7,6},{8,9},{9,8},{10,11... | collective-permute-start | bytes 393224 | tf_op jit(solution)/shard_map/ppermute | solution.py:417
  8.8 8.5 %collective-permute-start.2 = (bf16[512,128]{1,0:T(8,128)(2,1)S(1)}, bf16[512,128]{1,0:T(8,128)(2,1)S(1)}, u32[]{:S(2)}, u32[]{:S(2)}) collective-permute-start(bf16[512,128]{1,0:T(8,128)(2,1)S(1)} %get-tuple-element.39), channel_id=1, source_target_pairs={{0,9},{1,8},{2,11},{3,10},{4,13},{5,12},{6,15},{7,14},{8,1},{9,0},... | collective-permute-start | bytes 393224 | tf_op jit(solution)/shard_map/ppermute | solution.py:418
  8.8 8.5 %collective-permute-start.3 = (bf16[512,128]{1,0:T(8,128)(2,1)S(1)}, bf16[512,128]{1,0:T(8,128)(2,1)S(1)}, u32[]{:S(2)}, u32[]{:S(2)}) collective-permute-start(bf16[512,128]{1,0:T(8,128)(2,1)S(1)} %get-tuple-element.40), channel_id=1, source_target_pairs={{1,2},{2,1},{3,4},{4,3},{5,6},{6,5},{9,10},{10,9},{11,12},{12,11},... | collective-permute-start | bytes 393224 | tf_op jit(solution)/shard_map/ppermute | solution.py:419
  9.4 2.3 %collective-permute-start.4 = (bf16[128,128]{1,0:T(8,128)(2,1)S(1)}, bf16[128,128]{1,0:T(8,128)(2,1)S(1)}, u32[]{:S(2)}, u32[]{:S(2)}) collective-permute-start(bf16[128,128]{1,0:T(8,128)(2,1)S(1)} %get-tuple-element.41), channel_id=1, source_target_pairs={{1,10},{2,9},{3,12},{4,11},{5,14},{6,13},{9,2},{10,1},{11,4},{12,3... | collective-permute-start | bytes 98312 | tf_op jit(solution)/shard_map/ppermute | solution.py:420
  22.9 5.9 %collective-permute-start.5 = (bf16[64,24,128]{2,1,0:T(8,128)(2,1)S(1)}, bf16[64,24,128]{2,1,0:T(8,128)(2,1)S(1)}, u32[]{:S(2)}, u32[]{:S(2)}) collective-permute-start(bf16[64,24,128]{2,1,0:T(8,128)(2,1)S(1)} %get-tuple-element.51), channel_id=1, source_target_pairs={{0,16},{16,0},{32,48},{48,32},{64,80},{80,64},{96,112},{112,96},{1... | collective-permute-start | bytes 1179656 | tf_op jit(solution)/shard_map/ppermute | solution.py:448
  29.6 21.4 %all-to-all-start = ((bf16[64,24,128]{2,1,0:T(8,128)(2,1)}), bf16[64,24,128]{2,1,0:T(8,128)(2,1)S(1)}, u32[]{:S(2)}, u32[]{:S(2)}) async-start(bf16[64,24,128]{2,1,0:T(8,128)(2,1)} %shard_map.114), calls=%async_computation | async-start | bytes 786432 | tf_op jit(solution)/shard_map/all_to_all | solution.py:455
  43.1 29.6 %copy-start.3 = (f32[4,16,32,128]{3,2,1,0:T(8,128)S(1)}, f32[4,16,32,128]{3,2,1,0:T(8,128)}, u32[]{:S(2)}) copy-start(f32[4,16,32,128]{3,2,1,0:T(8,128)} %get-tuple-element.55.refs_0_) | copy-start | bytes 3145732
  43.1 7.2 %collective-permute-start.6 = (bf16[16,32,128]{2,1,0:T(8,128)(2,1)S(1)}, bf16[16,32,128]{2,1,0:T(8,128)(2,1)S(1)}, u32[]{:S(2)}, u32[]{:S(2)}) collective-permute-start(bf16[16,32,128]{2,1,0:T(8,128)(2,1)S(1)} %get-tuple-element.54), channel_id=1, source_target_pairs={{0,8},{8,0},{1,9},{9,1},{2,10},{10,2},{3,11},{11,3},{4,12},{12,4},... | collective-permute-start | bytes 393224 | tf_op jit(solution)/shard_map/ppermute | solution.py:463
  51.0 23.1 %copy-start.1 = (f32[128,1728]{0,1:T(8,128)S(1)}, f32[128,1728]{0,1:T(8,128)}, u32[]{:S(2)}) copy-start(f32[128,1728]{0,1:T(8,128)} %param.11) | copy-start | bytes 2654212
  69.6 4.5 %collective-permute-start.7 = (bf16[64,32,128]{2,1,0:T(8,128)(2,1)S(1)}, bf16[64,32,128]{2,1,0:T(8,128)(2,1)S(1)}, u32[]{:S(2)}, u32[]{:S(2)}) collective-permute-start(bf16[64,32,128]{2,1,0:T(8,128)(2,1)S(1)} %all_to_all.10.full_ref), channel_id=1, source_target_pairs={{0,16},{16,0},{32,48},{48,32},{64,80},{80,64},{96,112},{112,96},{1... | collective-permute-start | bytes 1572872 | tf_op jit(solution)/shard_map/ppermute | solution.py:479
